TPU v7x, 256 devices: a whole 4x4x8 slice. The times are simulated.
256 devices in a mesh: section: 64 (over x_lo, y, z), team: 4 (over x_hi, core).
Axes of the slice: x: 4 (x_hi: 2, x_lo: 2; x = x_hi * 2 + x_lo), y: 4, z: 8, core: 2. Of those that a mesh axis runs over, the one named last changes fastest.
Arguments:
- features: bfloat16 [65536, 128], P(('section', 'team')), may hold values from -6 to 6
- weight: bfloat16 [128, 256], replicated, may hold values from -0.5 to 0.5
- tiles: bfloat16 [64, 4, 256, 128, 128], P('section', 'team'), may hold values from -0.4375 to 0.4375
- tile_rows: int32 [64, 4, 256], P('section', 'team'), may hold values from 0 to 7, as said below
- tile_cols: int32 [64, 4, 256], P('section', 'team'), may hold values from 0 to 127, as said below
- tile_count: int32 [64, 4], P('section', 'team'), may hold values from 1 to 256, as said below
- cotangent: bfloat16 [65536, 256], P(('section', 'team')), may hold values from -6 to 6
Outputs:
- output: bfloat16 [65536, 256], P(('section', 'team'))
- grad_features: bfloat16 [65536, 128], P(('section', 'team'))
- grad_weight: float32 [128, 256], replicated
Inputs may be any that keep to these rules, and one draw needn't show every extreme that they name: `tile_rows`: row tile of a slot, from 0 to 7. `tile_cols`: column tile of a slot, from 0 to 127; some column tiles are named far more often than others. The live slots of a device are its first tile_count slots; some device has all 256 live.
All inputs are finite; a program needn't handle non-finite values.
Results may differ from a plain program's by a relative error of at most 0.02.
Values may be sent and summed in bfloat16 or wider, within the bound.
No kernel may reach another device: no remote copies, remote signals or barrier semaphores. Data moves between devices by JAX's collectives and lax.ppermute only.
A program may use at most 128 MiB of HBM per device.

v0:
```python
import math

import jax
import jax.numpy as jnp
from jax import lax
from jax.sharding import PartitionSpec as P


def reduce_weight(weight_part, scale):
    return lax.psum(weight_part, ("section", "team")) * scale


def per_device(features, weight, tiles, tile_rows, tile_cols, tile_count, cotangent):
    node_dev, fin = features.shape
    tile = tiles.shape[-1]
    slots = tiles.shape[2]
    sections = lax.axis_size("section")
    teams = lax.axis_size("team")
    per_dev = node_dev // tile
    row_tiles = per_dev * teams
    col_tiles = per_dev * sections
    scale = 1.0 / math.sqrt(node_dev * sections * teams)
    slab = tiles.reshape(slots, tile, tile)
    rows_index = tile_rows.reshape(slots)
    cols_index = tile_cols.reshape(slots)
    live_count = tile_count.reshape(())
    slot_ids = jnp.arange(slots, dtype=jnp.int32)
    row_ids = jnp.arange(row_tiles, dtype=jnp.int32)
    gathered = lax.all_gather(features, "section", axis=0, tiled=True)
    blocks = gathered.reshape(col_tiles, tile, fin)
    picked = blocks[cols_index]
    prod = jnp.einsum("sij,sjf->sif", slab, picked, preferred_element_type=jnp.float32)
    select = ((rows_index[None, :] == row_ids[:, None]) & (slot_ids < live_count)[None, :]).astype(
        jnp.float32
    )
    partial_value = jnp.einsum("rs,sif->rif", select, prod)
    summed = lax.psum_scatter(
        partial_value.reshape(row_tiles * tile, fin), "team", scatter_dimension=0, tiled=True
    )
    aggregated = summed.astype(jnp.bfloat16)
    pre = jnp.dot(aggregated, weight, preferred_element_type=jnp.float32)
    sig = jax.nn.sigmoid(pre)
    output = (pre * sig).astype(jnp.bfloat16)
    grad_pre = (cotangent.astype(jnp.float32) * sig * (1.0 + pre * (1.0 - sig))).astype(
        jnp.bfloat16
    )
    weight_part = lax.dot_general(
        aggregated, grad_pre, (((0,), (0,)), ((), ())), preferred_element_type=jnp.float32
    )
    back = lax.dot_general(
        grad_pre, weight, (((1,), (1,)), ((), ())), preferred_element_type=jnp.float32
    ).astype(jnp.bfloat16)
    section_back = lax.all_gather(back, "team", axis=0, tiled=True).reshape(row_tiles, tile, fin)
    picked_back = section_back[rows_index]
    prod_back = jnp.einsum("sij,sif->sjf", slab, picked_back, preferred_element_type=jnp.float32)
    prod_back = prod_back * (slot_ids < live_count).astype(jnp.float32)[:, None, None]
    column_terms = jax.ops.segment_sum(prod_back, cols_index, num_segments=col_tiles)
    flat_terms = column_terms.reshape(col_tiles * tile, fin)
    grad_features = lax.psum_scatter(flat_terms, "section", scatter_dimension=0, tiled=True).astype(
        jnp.bfloat16
    )
    grad_weight = reduce_weight(weight_part, scale)
    return (output, grad_features, grad_weight)


def solution(mesh):
    in_specs = (
        P(("section", "team"), None),
        P(),
        P("section", "team", None, None, None),
        P("section", "team", None),
        P("section", "team", None),
        P("section", "team"),
        P(("section", "team"), None),
    )
    out_specs = (P(("section", "team"), None), P(("section", "team"), None), P())
    return jax.shard_map(
        per_device, mesh=mesh, in_specs=in_specs, out_specs=out_specs, check_vma=False
    )
```

profile of v0, /device:TPU:2, one launch (start us, length us, event | category | flops | bytes accessed | tf_op | source)
XLA Modules:
  0.0 974.9 jit_solution(8687335192589745691)
XLA Ops:
  7.2 0.0 copy-start
  7.2 0.0 all-gather.2.cloned.1.call-start
  7.2 0.7 all-gather.2.cloned.1.call-update
  7.9 0.0 reduce-scatter.3.cloned.1.call-start
  8.6 0.7 compare_select_fusion.1
  9.3 306.8 %all-gather.2.cloned.1.call-done = bf16[16384,128]{1,0:T(8,128)(2,1)} async-done(((bf16[256,128]{1,0:T(8,128)(2,1)}), bf16[16384,128]{1,0:T(8,128)(2,1)}) %all-gather.2.cloned.1.call-update) | async-done | bytes 4194320 | tf_op jit(solution)/shard_map/all_gather | solution.py:29
  316.1 10.8 %gather_fusion = bf16[256,128,128]{2,1,0:T(8,128)(2,1)} fusion(bf16[128,128,128]{2,1,0:T(8,128)(2,1)} %bitcast.36, s32[1024]{0:T(1024)S(1)} %pad_clamp_fusion.1), kind=kCustom, calls=%fused_computation | custom fusion | bytes 16778240 | tf_op jit(solution)/shard_map/gather | solution.py:31
  326.9 11.6 %fusion.3 = bf16[256,128,128]{2,1,0:T(8,128)(2,1)} fusion(bf16[256,128,128]{2,1,0:T(8,128)(2,1)} %gather_fusion, bf16[1,1,256,128,128]{4,3,2,1,0:T(8,128)(2,1)} %param.9), kind=kOutput, calls=%fused_computation.7 | convolution fusion | flops 1073741824 | bytes 25165824 | tf_op jit(solution)/shard_map/sij,sjf->sif/dot_general | solution.py:32
  338.5 0.0 copy-start.2
  338.5 11.9 %copy.14 = bf16[256,128,128]{1,0,2:T(8,128)(2,1)} copy(bf16[256,128,128]{2,1,0:T(8,128)(2,1)} %fusion.3) | data formatting | bytes 16777216 | tf_op jit(solution)/shard_map/sij,sjf->sif/dot_general | solution.py:32
  350.3 0.0 copy-start.4
  350.3 0.0 copy-done.2
  350.3 4.6 fusion
  354.9 0.9 copy.11
  355.8 0.0 reduce-scatter.3.cloned.1.call-update
  355.9 0.0 all-reduce.2.cloned.1.call-start
  356.0 31.1 %reduce-scatter.3.cloned.1.call-done = f32[256,128]{1,0:T(8,128)} async-done(((f32[1024,128]{1,0:T(8,128)}), f32[256,128]{1,0:T(8,128)}) %reduce-scatter.3.cloned.1.call-update) | async-done | bytes 131088 | tf_op jit(solution)/shard_map/reduce_scatter | solution.py:37
  387.0 0.0 copy-done
  387.0 0.0 copy-done.4
  387.0 1.8 multiply_convert_fusion
  388.8 0.2 convolution_convert_fusion
  389.0 1.8 fusion.5
  390.8 0.0 all-reduce.2.cloned.1.call-update
  390.8 0.0 reduce-scatter.5.cloned.1.call-start
  390.9 7.5 all_gather.7
  398.3 8.6 gather_fusion.1
  406.9 15.4 %multiply_bitcast_fusion = f32[256,128,128]{1,2,0:T(8,128)} fusion(bf16[256,128,128]{2,1,0:T(8,128)(2,1)} %gather_fusion.1, bf16[1,1,256,128,128]{4,3,2,1,0:T(8,128)(2,1)} %param.9, f32[256]{0:T(256)S(1)} %fusion.14), kind=kOutput, calls=%fused_computation.5 | convolution fusion | flops 1077936128 | bytes 33555456 | tf_op jit(solution)/shard_map/sij,sif->sjf/dot_general | solution.py:55
  422.4 17.5 %copy.13 = f32[256,128,128]{2,1,0:T(8,128)} copy(f32[256,128,128]{1,2,0:T(8,128)} %multiply_bitcast_fusion) | data formatting | bytes 33554432 | tf_op jit(solution)/shard_map/mul | solution.py:56
  439.9 0.0 copy-start.3
  439.9 4.3 broadcast_in_dim.2
  444.1 0.0 copy-done.3
  444.1 0.0 copy-start.1
  444.1 52.0 %scatter_fusion = f32[128,128,128]{2,1,0:T(8,128)} fusion(f32[128,128,128]{2,1,0:T(8,128)} %broadcast_in_dim.2, s32[256]{0:T(256)S(1)} %bitcast.39, f32[256,128,128]{2,1,0:T(8,128)} %copy.13), kind=kCustom, calls=%fused_computation.2 | custom fusion | flops 4194304 | bytes 50332672 | tf_op jit(solution)/shard_map/scatter-add | solution.py:57
  496.1 0.0 reduce-scatter.5.cloned.1.call-update
  496.1 140.0 %all-reduce.2.cloned.1.call-done = f32[128,256]{1,0:T(8,128)} async-done(((f32[128,256]{1,0:T(8,128)}), f32[128,256]{1,0:T(8,128)}) %all-reduce.2.cloned.1.call-update) | async-done | bytes 131088 | tf_op jit(solution)/shard_map/psum | solution.py:10
  636.1 1.6 broadcast_multiply_fusion
  637.7 329.1 %reduce-scatter.5.cloned.1.call-done = f32[256,128]{1,0:T(8,128)} async-done(((f32[16384,128]{1,0:T(8,128)}), f32[256,128]{1,0:T(8,128)}) %reduce-scatter.5.cloned.1.call-update) | async-done | bytes 131088 | tf_op jit(solution)/shard_map/reduce_scatter | solution.py:59
  966.8 1.5 convert_element_type.32
  968.4 0.0 copy-done.1
  (5 shorter events, 0.0 us)
Async XLA Ops:
  7.2 379.9 %copy-start = (bf16[128,256]{1,0:T(8,128)(2,1)S(1)}, bf16[128,256]{1,0:T(8,128)(2,1)}, u32[]{:S(2)}) copy-start(bf16[128,256]{1,0:T(8,128)(2,1)} %param.8) | copy-start | bytes 196612
  7.2 308.9 %all-gather.2.cloned.1.call-start = ((), (), s32[]{:S(2)}) async-start(), calls=%async_computation.2 | async-start | bytes 4259840 | tf_op jit(solution)/shard_map/all_gather | solution.py:29
  7.9 379.1 %reduce-scatter.3.cloned.1.call-start = ((), (), s32[]{:S(2)}) async-start(), calls=%async_computation.3 | async-start | bytes 655360 | tf_op jit(solution)/shard_map/reduce_scatter | solution.py:37
  338.5 11.9 %copy-start.2 = (s32[1,1,256]{2,1,0:T(1,128)S(1)}, s32[1,1,256]{2,1,0:T(1,128)}, u32[]{:S(2)}) copy-start(s32[1,1,256]{2,1,0:T(1,128)} %param.10) | copy-start | bytes 3076
  350.3 36.7 %copy-start.4 = (bf16[256,256]{1,0:T(8,128)(2,1)S(1)}, bf16[256,256]{1,0:T(8,128)(2,1)}, u32[]{:S(2)}) copy-start(bf16[256,256]{1,0:T(8,128)(2,1)} %param.13) | copy-start | bytes 393220
  355.9 280.3 %all-reduce.2.cloned.1.call-start = ((), (), s32[]{:S(2)}) async-start(), calls=%async_computation.5 | async-start | bytes 262144 | tf_op jit(solution)/shard_map/psum | solution.py:10
  390.8 576.0 %reduce-scatter.5.cloned.1.call-start = ((), (), s32[]{:S(2)}) async-start(), calls=%async_computation.4 | async-start | bytes 8519680 | tf_op jit(solution)/shard_map/reduce_scatter | solution.py:59
  439.9 4.3 copy-start.3
  444.1 524.3 %copy-start.1 = (bf16[128,256]{1,0:T(8,128)(2,1)S(1)}, bf16[128,256]{1,0:T(8,128)(2,1)}, u32[]{:S(2)}) copy-start(bf16[128,256]{1,0:T(8,128)(2,1)} %param.8) | copy-start | bytes 196612
Sparse Core Ops, SparseCore 0:
  9.8 306.2 all-gather.1
  356.0 30.9 reduce-scatter.2
  394.0 242.0 all-reduce.1
  638.7 328.1 reduce-scatter.4
where the time goes:
time: 976 us; the launch traced here: 975 us
  waiting for transfers between devices  808 us (83%)
  other arithmetic  55.8 us (6%)
  local copies, waits for them, and re-layouts  53.9 us (6%)
  matrix products  35.4 us (4%)
  between operations  14.5 us (1%)
    reduce_scatter x1, waiting for transfers between devices, per_device(): lax.psum_scatter(flat_terms, 'section', scatter_dimension=0, tiled=True)  329 us
    all_gather x1, waiting for transfers between devices, per_device(): gathered = lax.all_gather(features, 'section', axis=0, tiled=True)  307 us
    psum x1, waiting for transfers between devices, reduce_weight(): return lax.psum(weight_part, ('section', 'team')) * scale  140 us
    scatter-add x1, other arithmetic, per_device(): jax.ops.segment_sum(prod_back, cols_index, num_segments=col_tiles)  52 us
    reduce_scatter x1, waiting for transfers between devices, per_device(): lax.psum_scatter(partial_value.reshape(row_tiles * tile, fin), 'team', sc...  31.1 us
  transfers between devices with their start and end apart: 4, of which 4 were waited for; matrix products, arithmetic and copies ran while one was open for 10% of the time, Pallas kernels for 0%

commit v1 on v0

v1 whole, which is shorter than its diff:
```python
import math

import jax
import jax.numpy as jnp
from jax import lax
from jax.experimental import pallas as pl
from jax.experimental.pallas import tpu as pltpu
from jax.sharding import PartitionSpec as P

NX, NY, NZ = 2, 4, 8
UNROLL = 16
NEAR = (0, 1, 2, 6, 7)
FAR = (3, 4, 5)
F32 = jnp.float32
BF16 = jnp.bfloat16
VMEM_LIMIT = 56 * 2**20


def section_index(x, y, z):
    return ((x % NX) * NY + y % NY) * NZ + z % NZ


def send(value, dx=0, dy=0, dz=0):
    pairs = [
        (section_index(x, y, z), section_index(x + dx, y + dy, z + dz))
        for x in range(NX)
        for y in range(NY)
        for z in range(NZ)
    ]
    return lax.ppermute(value, "section", pairs)


def send_team(value, mask):
    return lax.ppermute(value, "team", [(t, t ^ mask) for t in range(4)])


def fence(*arrays):
    return lax.optimization_barrier(arrays)


def add(*terms):
    total = terms[0].astype(F32)
    for term in terms[1:]:
        total = total + term.astype(F32)
    return total


def join(*arrays):
    return jnp.concatenate(arrays)


def sort_kernel(row_tiles, rows, cols, info, out):
    slots = rows.shape[0]
    region = slots + UNROLL
    length = 2 * region + UNROLL
    blocks = NY * NX * 2
    count, me = info[0], info[1]

    def put(p, slot, row, col):
        out[p] = slot
        out[length + p] = row
        out[2 * length + p] = col

    def body(step, carry):
        near_n, far_n = carry
        for j in range(8):
            i = step * 8 + j
            col = cols[i]
            owner = col >> 1
            dx = (owner >> 5) ^ (me >> 5)
            dy = ((owner >> 3) - (me >> 3)) & (NY - 1)
            dz = (owner - me) & (NZ - 1)
            far = ((dz >= FAR[0]) & (dz <= FAR[-1])).astype(jnp.int32)
            live = (i < count).astype(jnp.int32)
            plane = jnp.where(dz < FAR[0], dz, dz - FAR[0])
            place = plane * blocks + dy * (NX * 2) + dx * 2 + (col & 1)
            spot = jnp.where(far == 1, region + far_n, near_n)
            put(jnp.where(live == 1, spot, 2 * region), i, rows[i], place)
            near_n = near_n + live * (1 - far)
            far_n = far_n + live * far
        return near_n, far_n

    zero = jnp.int32(0)
    near_n, far_n = lax.fori_loop(0, slots // 8, body, (zero, zero))
    for j in range(UNROLL):
        put(near_n + j, 0, row_tiles, len(NEAR) * blocks)
        put(region + far_n + j, 0, row_tiles, len(FAR) * blocks)
    out[3 * length] = (near_n + UNROLL - 1) // UNROLL
    out[3 * length + 1] = (far_n + UNROLL - 1) // UNROLL


def sort_slots(rows, cols, count, me, row_tiles):
    smem = pl.BlockSpec(memory_space=pltpu.SMEM)
    length = 2 * (rows.shape[0] + UNROLL) + UNROLL

    def kernel(*refs):
        sort_kernel(row_tiles, *refs)

    return pl.pallas_call(
        kernel,
        out_shape=jax.ShapeDtypeStruct((3 * length + 2,), jnp.int32),
        in_specs=[smem] * 3,
        out_specs=smem,
        name="sort_slots",
    )(rows, cols, jnp.stack([count, me.astype(jnp.int32)]))


class Slots:
    def __init__(self, ref, group):
        self.ref = ref
        self.length = (ref.shape[0] - 2) // 3
        self.start = group * ((self.length - UNROLL) // 2)
        self.chunks = ref[3 * self.length + group]

    def get(self, field, i):
        return self.ref[field * self.length + self.start + i]

    def slot(self, i):
        return self.get(0, i)

    def row(self, i):
        return self.get(1, i)

    def col(self, i):
        return self.get(2, i)

    def fetch(self, tiles, buf, sem):
        def body(c, carry):
            for j in range(UNROLL):
                i = c * UNROLL + j
                pltpu.make_async_copy(tiles.at[self.slot(i)], buf.at[i], sem.at[c]).start()
            return carry

        lax.fori_loop(0, self.chunks, body, 0)

    def each(self, tiles, buf, sem, fn):
        def body(c, carry):
            part = pl.ds(c * UNROLL, UNROLL)
            pltpu.make_async_copy(tiles.at[pl.ds(0, UNROLL)], buf.at[part], sem.at[c]).wait()
            for j in range(UNROLL):
                fn(c * UNROLL + j)
            return carry

        lax.fori_loop(0, self.chunks, body, 0)


def forward_kernel(group, spans, slots_ref, tiles, *refs):
    n = len(spans)
    pieces = refs[:n]
    before = refs[n] if group else None
    out, feat, buf, acc, tsem, fsem = refs[n + group :]
    slots = Slots(slots_ref, group)
    copies = []
    for i, (at, size) in enumerate(spans):
        copies.append(pltpu.make_async_copy(pieces[i], feat.at[pl.ds(at, size)], fsem.at[i]))
        copies[-1].start()
    slots.fetch(tiles, buf, tsem)
    acc[...] = before[...] if group else jnp.zeros_like(acc)
    feat[feat.shape[0] - 1] = jnp.zeros(feat.shape[1:], feat.dtype)
    for copy in copies:
        copy.wait()

    def one(i):
        r = slots.row(i)
        acc[r] = acc[r] + jnp.dot(buf[i], feat[slots.col(i)], preferred_element_type=F32)

    slots.each(tiles, buf, tsem, one)
    out[...] = acc[: out.shape[0]].astype(out.dtype)


def forward_call(group, slot_info, tiles, pieces, spans, before, row_tiles):
    slots, tile, _ = tiles.shape
    fin = pieces[0].shape[-1]
    blocks = sum(size for _, size in spans)
    smem = pl.BlockSpec(memory_space=pltpu.SMEM)
    vmem = pl.BlockSpec(memory_space=pltpu.VMEM)
    hbm = pl.BlockSpec(memory_space=pl.ANY)

    def kernel(*refs):
        forward_kernel(group, spans, *refs)

    shape = (row_tiles, tile, fin) if group else (row_tiles + 1, tile, fin)
    return pl.pallas_call(
        kernel,
        out_shape=jax.ShapeDtypeStruct(shape, BF16 if group else F32),
        in_specs=[smem] + [hbm] * (1 + len(pieces)) + [vmem] * group,
        out_specs=vmem,
        scratch_shapes=[
            pltpu.VMEM((blocks + 1, tile, fin), BF16),
            pltpu.VMEM((slots, tile, tile), BF16),
            pltpu.VMEM((row_tiles + 1, tile, fin), F32),
            pltpu.SemaphoreType.DMA((slots // UNROLL,)),
            pltpu.SemaphoreType.DMA((len(pieces),)),
        ],
        compiler_params=pltpu.CompilerParams(vmem_limit_bytes=VMEM_LIMIT),
        cost_estimate=pl.CostEstimate(
            flops=blocks * 2 * 2 * tile**3, bytes_accessed=blocks * 4 * tile**2, transcendentals=0
        ),
        name="forward_far" if group else "forward_near",
    )(slot_info, tiles, *pieces, *([before] if group else []))


def backward_tiles(slots, layout, tiles, backs, outs, rider, none, buf, acc, stage, tsem, osem):
    def one(i):
        c = slots.col(i)
        acc[c] = acc[c] + jnp.dot(backs[slots.row(i)], buf[i], preferred_element_type=F32)

    slots.each(tiles, buf, tsem, one)
    copies = []
    size = acc.shape[0] // len(layout)
    for i, kind in enumerate(layout):
        part = pl.ds(i * size, size)
        stage[part] = acc[part].astype(BF16)
        copies.append(
            pltpu.make_async_copy(stage.at[part], outs[i].at[pl.ds(0, size)], osem.at[i, 0])
        )
        copies[-1].start()
        if kind:
            extra = rider if kind == "rider" else none
            copies.append(
                pltpu.make_async_copy(extra, outs[i].at[pl.ds(size, 1)], osem.at[i, 1])
            )
            copies[-1].start()
    for copy in copies:
        copy.wait()


def piece_shapes(layout, size, fin, tile):
    return [
        jax.ShapeDtypeStruct((size + 1 if kind else size, fin, tile), BF16) for kind in layout
    ]


def backward_far_kernel(
    layout, slots_ref, member_ref, tiles, sum_a, sum_b, c0, c1, c2, c3, weight,
    out, rider, backs, *refs,
):
    n = len(layout)
    outs = refs[:n]
    buf, acc, stage, agg, gpre, wfull, none, tsem, osem = refs[n:]
    member = member_ref[0]
    slots = Slots(slots_ref, 1)
    slots.fetch(tiles, buf, tsem)
    _, tile, _ = sum_a.shape
    node_dev = out.shape[0]
    per_dev = node_dev // tile
    total = sum_a[...].astype(F32) + sum_b[...].astype(F32)
    agg[...] = total.astype(BF16).reshape(agg.shape)
    acc[...] = jnp.zeros_like(acc)
    for d, cot in enumerate((c0, c1, c2, c3)):
        who = member ^ d
        at = pl.multiple_of(who * node_dev, node_dev)
        mine = agg[pl.ds(at, node_dev), :]
        pre = jnp.dot(mine, weight[...], preferred_element_type=F32)
        sig = jax.nn.sigmoid(pre)
        if d == 0:
            out[...] = (pre * sig).astype(BF16)
        grad = (cot[...].astype(F32) * sig * (1.0 + pre * (1.0 - sig))).astype(BF16)
        gpre[pl.ds(at, node_dev), :] = grad
        back = lax.dot_general(
            weight[...], grad, (((1,), (1,)), ((), ())), preferred_element_type=F32
        ).astype(BF16)
        for j in range(per_dev):
            backs[who * per_dev + j] = back[:, j * tile : (j + 1) * tile]
    backs[backs.shape[0] - 1] = jnp.zeros(backs.shape[1:], BF16)
    none[...] = jnp.zeros_like(none)
    wfull[...] = lax.dot_general(
        agg[...], gpre[...], (((0,), (0,)), ((), ())), preferred_element_type=F32
    )
    fin, fout = wfull.shape
    share = fin // 2
    part = wfull[pl.ds(pl.multiple_of(member % 2 * share, share), share), :].astype(BF16)
    rider[0, pl.ds(0, share), :] = part[:, : fout // 2]
    rider[0, pl.ds(share, share), :] = part[:, fout // 2 :]
    backward_tiles(
        slots, layout, tiles, backs, outs, rider, none, buf, acc, stage, tsem, osem
    )


def backward_far_call(slot_info, member, tiles, sum_a, sum_b, cots, weight, size):
    slots, tile, _ = tiles.shape
    row_tiles, _, fin = sum_a.shape
    node_dev, fout = cots[0].shape
    nodes = row_tiles * tile
    layout = (None, "rider", None, "rider", None, "none")
    blocks = size * len(layout)
    smem = pl.BlockSpec(memory_space=pltpu.SMEM)
    vmem = pl.BlockSpec(memory_space=pltpu.VMEM)
    hbm = pl.BlockSpec(memory_space=pl.ANY)

    def kernel(*refs):
        backward_far_kernel(layout, *refs)

    return pl.pallas_call(
        kernel,
        out_shape=[
            jax.ShapeDtypeStruct((node_dev, fout), BF16),
            jax.ShapeDtypeStruct((1, fin, tile), BF16),
            jax.ShapeDtypeStruct((row_tiles + 1, fin, tile), BF16),
            *piece_shapes(layout, size, fin, tile),
        ],
        in_specs=[smem] * 2 + [hbm] + [vmem] * 7,
        out_specs=[vmem] * 3 + [hbm] * len(layout),
        scratch_shapes=[
            pltpu.VMEM((slots, tile, tile), BF16),
            pltpu.VMEM((blocks + 1, fin, tile), F32),
            pltpu.VMEM((blocks, fin, tile), BF16),
            pltpu.VMEM((nodes, fin), BF16),
            pltpu.VMEM((nodes, fout), BF16),
            pltpu.VMEM((fin, fout), F32),
            pltpu.VMEM((1, fin, tile), BF16),
            pltpu.SemaphoreType.DMA((slots // UNROLL,)),
            pltpu.SemaphoreType.DMA((len(layout), 2)),
        ],
        compiler_params=pltpu.CompilerParams(vmem_limit_bytes=VMEM_LIMIT),
        cost_estimate=pl.CostEstimate(
            flops=blocks * 2 * 2 * tile**3, bytes_accessed=blocks * 6 * tile**2, transcendentals=0
        ),
        name="dense_and_backward_far",
    )(slot_info, member, tiles, sum_a, sum_b, *cots, weight)


def backward_near_kernel(layout, slots_ref, tiles, backs, *refs):
    n = len(layout)
    outs = refs[:n]
    buf, acc, stage, none, tsem, osem = refs[n:]
    slots = Slots(slots_ref, 0)
    slots.fetch(tiles, buf, tsem)
    acc[...] = jnp.zeros_like(acc)
    none[...] = jnp.zeros_like(none)
    backward_tiles(slots, layout, tiles, backs, outs, None, none, buf, acc, stage, tsem, osem)


def backward_near_call(slot_info, tiles, backs, size):
    slots, tile, _ = tiles.shape
    fin = backs.shape[1]
    layout = (None, None) + (None, "none") * 4
    blocks = size * len(layout)
    smem = pl.BlockSpec(memory_space=pltpu.SMEM)
    vmem = pl.BlockSpec(memory_space=pltpu.VMEM)
    hbm = pl.BlockSpec(memory_space=pl.ANY)

    def kernel(*refs):
        backward_near_kernel(layout, *refs)

    return pl.pallas_call(
        kernel,
        out_shape=piece_shapes(layout, size, fin, tile),
        in_specs=[smem, hbm, vmem],
        out_specs=[hbm] * len(layout),
        scratch_shapes=[
            pltpu.VMEM((slots, tile, tile), BF16),
            pltpu.VMEM((blocks + 1, fin, tile), F32),
            pltpu.VMEM((blocks, fin, tile), BF16),
            pltpu.VMEM((1, fin, tile), BF16),
            pltpu.SemaphoreType.DMA((slots // UNROLL,)),
            pltpu.SemaphoreType.DMA((len(layout), 2)),
        ],
        compiler_params=pltpu.CompilerParams(vmem_limit_bytes=VMEM_LIMIT),
        cost_estimate=pl.CostEstimate(
            flops=blocks * 2 * 2 * tile**3, bytes_accessed=blocks * 6 * tile**2, transcendentals=0
        ),
        name="backward_near",
    )(slot_info, tiles, backs)


def gather_features(features, cotangent, tile):
    fin = features.shape[1]
    mine = features.reshape(-1, tile, fin)
    own = join(mine, send(mine, dx=1))
    cot1 = send_team(cotangent, 1)
    y1 = send(own, dy=-1)
    y3 = send(own, dy=1)
    y2 = send(own, dy=-2)
    up0, up1 = [join(own, y1)], [join(y2, y3)]
    down0, down1 = [up0[0]], [up1[0]]
    for step in range(4):
        up0.append(send(up0[-1], dz=-1))
        down1.append(send(down1[-1], dz=1))
        if step < 3:
            down0.append(send(down0[-1], dz=1))
            up1.append(send(up1[-1], dz=-1))
    cot2 = send_team(cotangent, 2)
    cot3 = send_team(cot1, 2)
    near = [up0[0], up1[0], up0[1], up1[1], up0[2], up1[2]]
    near += [down0[2], down1[2], down0[1], down1[1]]
    far = [up0[3], up1[3], up0[4], down1[4], down0[3], down1[3]]
    return near, far, (cotangent, cot1, cot2, cot3)


def spans_of(pieces):
    spans, at = [], 0
    for piece in pieces:
        spans.append((at, piece.shape[0]))
        at += piece.shape[0]
    return spans


def ring_sum(terms, dz):
    arrived = [send(terms[0], dz=dz)]
    for term in terms[1:]:
        arrived.append(send(add(term, arrived[-1]).astype(BF16), dz=dz))
    return arrived


def scatter_sums(near, far, rider):
    g0, g1, g2, g6, g7 = [near[2 * i : 2 * i + 2] for i in range(5)]
    g3, g4, g5 = [far[2 * i : 2 * i + 2] for i in range(3)]
    up0 = ring_sum((g4[0], g3[0], g2[0], g1[0]), 1)
    down1 = ring_sum((g4[1], g5[1], g6[1], g7[1]), -1)
    up1 = ring_sum((g3[1], g2[1], g1[1]), 1)
    down0 = ring_sum((g5[0], g6[0], g7[0]), -1)
    size = g0[0].shape[0]
    plane0 = add(g0[0], up0[-1], down0[-1])
    plane1 = add(g0[1], up1[-1][:size], down1[-1][:size]).astype(BF16)
    u1, u2, u3 = [part[size:] for part in up1]
    d1, d2, d3, d4 = [part[size:] for part in down1]
    rider = ((add(rider, d4) + add(u2, d2)) + (add(u1, d3) + add(u3, d1))).astype(BF16)
    half = size // 2
    got1 = send(join(plane0[half:].astype(BF16), rider), dy=1)
    got2 = send(join(plane1[:half], rider), dy=2)
    got3 = send(join(plane1[half:], rider), dy=-1)
    line = add(plane0[:half], got1[:half], got2[:half], got3[:half])
    rider = (add(rider, got2[half:]) + add(got1[half:], got3[half:])).astype(BF16)
    size = half
    half = size // 2
    got = send(join(line[half:].astype(BF16), rider), dx=1)
    total = add(line[:half], got[:half])
    weight = add(rider, got[half:])[0]
    share = weight.shape[0] // 2
    weight = jnp.concatenate([weight[:share], weight[share:]], axis=1)
    other = send_team(weight, 1)
    low = lax.axis_index("team") % 2 == 0
    return total, jnp.where(low, join(weight, other), join(other, weight))


def per_device(features, weight, tiles, tile_rows, tile_cols, tile_count, cotangent):
    node_dev, fin = features.shape
    tile = tiles.shape[-1]
    slots = tiles.shape[2]
    sections = lax.axis_size("section")
    teams = lax.axis_size("team")
    row_tiles = node_dev // tile * teams
    scale = 1.0 / math.sqrt(node_dev * sections * teams)
    slab = tiles.reshape(slots, tile, tile)
    slot_info = sort_slots(
        tile_rows.reshape(slots),
        tile_cols.reshape(slots),
        tile_count.reshape(()),
        lax.axis_index("section"),
        row_tiles,
    )
    member = lax.axis_index("team").astype(jnp.int32).reshape(1)

    near, far, cots = gather_features(features, cotangent, tile)
    partial_sum = forward_call(0, slot_info, slab, near, spans_of(near), None, row_tiles)
    partial_sum, *cots = fence(partial_sum, *cots)
    partial_sum = forward_call(1, slot_info, slab, far, spans_of(far), partial_sum, row_tiles)
    pair = add(partial_sum, send_team(partial_sum, 1)).astype(BF16)
    size = near[0].shape[0]
    output, rider, backs, *far_terms = backward_far_call(
        slot_info, member, slab, pair, send_team(pair, 2), cots, weight, size
    )
    near_terms = backward_near_call(slot_info, slab, backs, size)
    total, weight_sum = scatter_sums(near_terms, far_terms, rider)
    grad_features = total.transpose(0, 2, 1).reshape(node_dev, fin).astype(BF16)
    return output, grad_features, weight_sum * scale


def solution(mesh):
    in_specs = (
        P(("section", "team"), None),
        P(),
        P("section", "team", None, None, None),
        P("section", "team", None),
        P("section", "team", None),
        P("section", "team"),
        P(("section", "team"), None),
    )
    out_specs = (P(("section", "team"), None), P(("section", "team"), None), P())
    return jax.shard_map(
        per_device, mesh=mesh, in_specs=in_specs, out_specs=out_specs, check_vma=False
    )
```

time: 976 us -> 168 us (0.17)
  the two profiles are of different devices: /device:TPU:2 before, /device:TPU:1 now
where the time goes in v1:
time: 168 us; the launch traced here: 167 us
  starting transfers between devices  85.4 us (51%)
  waiting for transfers between devices  42.6 us (25%)
  Pallas kernels  22.1 us (13%)
  other arithmetic  12.9 us (8%)
  local copies, waits for them, and re-layouts  1.94 us (1%)
  between operations  1.87 us (1%)
    ppermute x36, starting transfers between devices, send(): return lax.ppermute(value, 'section', pairs)  64.9 us
    ppermute x36, waiting for transfers between devices, send(): return lax.ppermute(value, 'section', pairs)  32.3 us
    ppermute x6, starting transfers between devices, send_team(): return lax.ppermute(value, 'team', [(t, t ^ mask) for t in range(4)])  20.5 us
    ppermute x6, waiting for transfers between devices, send_team(): return lax.ppermute(value, 'team', [(t, t ^ mask) for t in range(4)])  10.3 us
    convert_element_type x10, other arithmetic, ring_sum(): arrived.append(send(add(term, arrived[-1]).astype(BF16), dz=dz))  8.42 us
    pallas_call x2, Pallas kernels, forward_call(): pl.pallas_call(kernel, out_shape=jax.ShapeDtypeStruct(shape, BF16 if grou...  8.02 us
    pallas_call x1, Pallas kernels, backward_far_call(): pl.pallas_call(kernel, out_shape=[jax.ShapeDtypeStruct((node_dev, fout),...  4.9 us
    pallas_call x1, Pallas kernels, sort_slots(): pl.pallas_call(kernel, out_shape=jax.ShapeDtypeStruct((3 * length + 2,),...  4.63 us
  transfers between devices with their start and end apart: 42, of which 20 were waited for; matrix products, arithmetic and copies ran while one was open for 6% of the time, Pallas kernels for 8%

profile of v1, /device:TPU:1, one launch (start us, length us, event | category | flops | bytes accessed | tf_op | source)
XLA Modules:
  0.0 166.8 jit_solution(17822115055467192779)
XLA Ops:
  0.6 2.1 %collective-permute-start = (bf16[2,128,128]{2,1,0:T(8,128)(2,1)}, bf16[2,128,128]{2,1,0:T(8,128)(2,1)S(1)}, u32[]{:S(2)}, u32[]{:S(2)}) collective-permute-start(bf16[2,128,128]{2,1,0:T(8,128)(2,1)} %bitcast.19), channel_id=1, source_target_pairs={{0,128},{4,132},{8,136},{12,140},{16,144},{20,148},{24,152},{28,15... | collective-permute-start | bytes 196616 | tf_op jit(solution)/shard_map/ppermute | solution.py:30
  2.8 1.9 %collective-permute-done = bf16[2,128,128]{2,1,0:T(8,128)(2,1)S(1)} collective-permute-done((bf16[2,128,128]{2,1,0:T(8,128)(2,1)}, bf16[2,128,128]{2,1,0:T(8,128)(2,1)S(1)}, u32[]{:S(2)}, u32[]{:S(2)}) %collective-permute-start) | collective-permute-done | bytes 65568 | tf_op jit(solution)/shard_map/ppermute | solution.py:30
  5.5 3.1 %collective-permute-start.1 = (bf16[4,128,128]{2,1,0:T(8,128)(2,1)S(1)}, bf16[4,128,128]{2,1,0:T(8,128)(2,1)S(1)}, u32[]{:S(2)}, u32[]{:S(2)}) collective-permute-start(bf16[4,128,128]{2,1,0:T(8,128)(2,1)S(1)} %pad_maximum_fusion.4), channel_id=1, source_target_pairs={{0,96},{4,100},{8,104},{12,108},{16,112},{20,116},{24,120},{28,124... | collective-permute-start | bytes 393224 | tf_op jit(solution)/shard_map/ppermute | solution.py:30
  9.6 2.6 %collective-permute-done.1 = bf16[4,128,128]{2,1,0:T(8,128)(2,1)S(1)} collective-permute-done((bf16[4,128,128]{2,1,0:T(8,128)(2,1)S(1)}, bf16[4,128,128]{2,1,0:T(8,128)(2,1)S(1)}, u32[]{:S(2)}, u32[]{:S(2)}) %collective-permute-start.1) | collective-permute-done | bytes 131104 | tf_op jit(solution)/shard_map/ppermute | solution.py:30
  13.0 4.4 %collective-permute-start.2 = (bf16[8,128,128]{2,1,0:T(8,128)(2,1)S(1)}, bf16[8,128,128]{2,1,0:T(8,128)(2,1)S(1)}, u32[]{:S(2)}, u32[]{:S(2)}) collective-permute-start(bf16[8,128,128]{2,1,0:T(8,128)(2,1)S(1)} %pad_maximum_fusion.refs_2_), channel_id=1, source_target_pairs={{0,28},{4,0},{8,4},{12,8},{16,12},{20,16},{24,20},{28,24},{32,60},... | collective-permute-start | bytes 786440 | tf_op jit(solution)/shard_map/ppermute | solution.py:30
  17.6 3.9 %collective-permute-start.7 = (bf16[8,128,128]{2,1,0:T(8,128)(2,1)S(1)}, bf16[8,128,128]{2,1,0:T(8,128)(2,1)S(1)}, u32[]{:S(2)}, u32[]{:S(2)}) collective-permute-start(bf16[8,128,128]{2,1,0:T(8,128)(2,1)S(1)} %constant_dynamic-update-slice_fusion.refs_3_), channel_id=1, source_target_pairs={{0,28},{4,0},{8,4},{12,8},{16,12},{20,16},{24,20},{28,24},{32,60},... | collective-permute-start | bytes 786440 | tf_op jit(solution)/shard_map/ppermute | solution.py:30
  21.5 2.7 %collective-permute-start.3 = (bf16[8,128,128]{2,1,0:T(8,128)(2,1)S(1)}, bf16[8,128,128]{2,1,0:T(8,128)(2,1)S(1)}, u32[]{:S(2)}, u32[]{:S(2)}) collective-permute-start(bf16[8,128,128]{2,1,0:T(8,128)(2,1)S(1)} %collective-permute-done.2.refs_4_), channel_id=1, source_target_pairs={{0,28},{4,0},{8,4},{12,8},{16,12},{20,16},{24,20},{28,24},{32,60},... | collective-permute-start | bytes 786440 | tf_op jit(solution)/shard_map/ppermute | solution.py:30
  25.2 1.8 %collective-permute-done.7.refs_5_ = bf16[8,128,128]{2,1,0:T(8,128)(2,1)S(1)} collective-permute-done((bf16[8,128,128]{2,1,0:T(8,128)(2,1)S(1)}, bf16[8,128,128]{2,1,0:T(8,128)(2,1)S(1)}, u32[]{:S(2)}, u32[]{:S(2)}) %collective-permute-start.7) | collective-permute-done | bytes 262176 | tf_op jit(solution)/shard_map/ppermute | solution.py:30
  27.0 3.4 %collective-permute-start.8 = (bf16[8,128,128]{2,1,0:T(8,128)(2,1)S(1)}, bf16[8,128,128]{2,1,0:T(8,128)(2,1)S(1)}, u32[]{:S(2)}, u32[]{:S(2)}) collective-permute-start(bf16[8,128,128]{2,1,0:T(8,128)(2,1)S(1)} %collective-permute-done.7.refs_5_), channel_id=1, source_target_pairs={{0,28},{4,0},{8,4},{12,8},{16,12},{20,16},{24,20},{28,24},{32,60},... | collective-permute-start | bytes 786440 | tf_op jit(solution)/shard_map/ppermute | solution.py:30
  30.4 2.2 %collective-permute-done.3.refs_6_ = bf16[8,128,128]{2,1,0:T(8,128)(2,1)S(1)} collective-permute-done((bf16[8,128,128]{2,1,0:T(8,128)(2,1)S(1)}, bf16[8,128,128]{2,1,0:T(8,128)(2,1)S(1)}, u32[]{:S(2)}, u32[]{:S(2)}) %collective-permute-start.3) | collective-permute-done | bytes 262176 | tf_op jit(solution)/shard_map/ppermute | solution.py:30
  32.6 3.4 %collective-permute-start.4 = (bf16[8,128,128]{2,1,0:T(8,128)(2,1)S(1)}, bf16[8,128,128]{2,1,0:T(8,128)(2,1)S(1)}, u32[]{:S(2)}, u32[]{:S(2)}) collective-permute-start(bf16[8,128,128]{2,1,0:T(8,128)(2,1)S(1)} %collective-permute-done.3.refs_6_), channel_id=1, source_target_pairs={{0,28},{4,0},{8,4},{12,8},{16,12},{20,16},{24,20},{28,24},{32,60},... | collective-permute-start | bytes 786440 | tf_op jit(solution)/shard_map/ppermute | solution.py:30
  36.0 7.8 %collective-permute-start.18 = (bf16[256,256]{1,0:T(8,128)(2,1)}, bf16[256,256]{1,0:T(8,128)(2,1)S(1)}, u32[]{:S(2)}, u32[]{:S(2)}) collective-permute-start(bf16[256,256]{1,0:T(8,128)(2,1)} %refs_5_), channel_id=1, source_target_pairs={{0,1},{1,0},{2,3},{3,2},{4,5},{5,4},{6,7},{7,6},{8,9},{9,8},{10,11... | collective-permute-start | bytes 393224 | tf_op jit(solution)/shard_map/ppermute | solution.py:34
  43.9 1.2 collective-permute-done.18.refs_6_
  45.1 2.7 %collective-permute-start.19 = (bf16[256,256]{1,0:T(8,128)(2,1)}, bf16[256,256]{1,0:T(8,128)(2,1)}, u32[]{:S(2)}, u32[]{:S(2)}) collective-permute-start(bf16[256,256]{1,0:T(8,128)(2,1)} %refs_5_), channel_id=1, source_target_pairs={{0,2},{1,3},{2,0},{3,1},{4,6},{5,7},{6,4},{7,5},{8,10},{9,11},{10,... | collective-permute-start | bytes 393224 | tf_op jit(solution)/shard_map/ppermute | solution.py:34
  47.8 3.0 %collective-permute-start.9 = (bf16[8,128,128]{2,1,0:T(8,128)(2,1)S(1)}, bf16[8,128,128]{2,1,0:T(8,128)(2,1)S(1)}, u32[]{:S(2)}, u32[]{:S(2)}) collective-permute-start(bf16[8,128,128]{2,1,0:T(8,128)(2,1)S(1)} %collective-permute-done.8.refs_7_), channel_id=1, source_target_pairs={{0,28},{4,0},{8,4},{12,8},{16,12},{20,16},{24,20},{28,24},{32,60},... | collective-permute-start | bytes 786440 | tf_op jit(solution)/shard_map/ppermute | solution.py:30
  50.8 2.7 %collective-permute-start.10 = (bf16[8,128,128]{2,1,0:T(8,128)(2,1)S(1)}, bf16[8,128,128]{2,1,0:T(8,128)(2,1)}, u32[]{:S(2)}, u32[]{:S(2)}) collective-permute-start(bf16[8,128,128]{2,1,0:T(8,128)(2,1)S(1)} %collective-permute-done.4.refs_2_), channel_id=1, source_target_pairs={{0,28},{4,0},{8,4},{12,8},{16,12},{20,16},{24,20},{28,24},{32,60},... | collective-permute-start | bytes 786440 | tf_op jit(solution)/shard_map/ppermute | solution.py:30
  55.1 4.6 %sort_slots.1.refs_0_ = s32[1682]{0:T(1024)} custom-call(s32[256]{0:T(256)} %bitcast.23, s32[256]{0:T(256)} %bitcast.24, s32[2]{0:T(128)} %pad_add_fusion.refs_2_), custom_call_target="tpu_custom_call" | custom-call | tf_op jit(solution)/shard_map/sort_slots/pallas_call | solution.py:99
  59.9 4.3 %forward_near.1.refs_8_ = f32[9,128,128]{2,1,0:T(8,128)} custom-call(s32[1682]{0:T(1024)} %sort_slots.1.refs_0_, bf16[256,128,128]{2,1,0:T(8,128)(2,1)} %bitcast.15, bf16[8,128,128]{2,1,0:T(8,128)(2,1)} %copy-done.1, bf16[8,128,128]{2,1,0:T(8,128)(2,1)} %copy-done.2, bf16[8,128,128]{2,1,0:T(8,128)(2,1)} %copy-done.4, bf16[8,128,128]{2,1,0:T(8,128)(2,1)} %copy-done.7, ...), custom_call_target="tpu_custom_call" | custom-call | flops 671088640 | bytes 5242880 | tf_op jit(solution)/shard_map/forward_near/pallas_call | solution.py:183
  64.9 3.7 %forward_far.1 = bf16[8,128,128]{2,1,0:T(8,128)(2,1)} custom-call(s32[1682]{0:T(1024)} %sort_slots.1.refs_0_, bf16[256,128,128]{2,1,0:T(8,128)(2,1)} %bitcast.16, bf16[8,128,128]{2,1,0:T(8,128)(2,1)} %copy-done.11, bf16[8,128,128]{2,1,0:T(8,128)(2,1)} %copy-done.15, bf16[8,128,128]{2,1,0:T(8,128)(2,1)} %collective-permute-done.10.refs_4_, ...), custom_call_target="tpu_custom_call" | custom-call | flops 402653184 | bytes 3145728 | tf_op jit(solution)/shard_map/forward_far/pallas_call | solution.py:183
  68.7 3.3 %collective-permute-start.21 = (bf16[8,128,128]{2,1,0:T(8,128)(2,1)}, bf16[8,128,128]{2,1,0:T(8,128)(2,1)S(1)}, u32[]{:S(2)}, u32[]{:S(2)}) collective-permute-start(bf16[8,128,128]{2,1,0:T(8,128)(2,1)} %forward_far.1), channel_id=1, source_target_pairs={{0,1},{1,0},{2,3},{3,2},{4,5},{5,4},{6,7},{7,6},{8,9},{9,8},{10,11... | collective-permute-start | bytes 786440 | tf_op jit(solution)/shard_map/ppermute | solution.py:34
  72.0 1.4 collective-permute-done.21
  74.4 1.5 collective-permute-start.22
  75.9 7.6 %collective-permute-done.22.refs_4_ = bf16[8,128,128]{2,1,0:T(8,128)(2,1)S(1)} collective-permute-done((bf16[8,128,128]{2,1,0:T(8,128)(2,1)S(1)}, bf16[8,128,128]{2,1,0:T(8,128)(2,1)S(1)}, u32[]{:S(2)}, u32[]{:S(2)}) %collective-permute-start.22) | collective-permute-done | bytes 262176 | tf_op jit(solution)/shard_map/ppermute | solution.py:34
  84.2 4.9 %dense_and_backward_far.1 = (bf16[256,256]{1,0:T(8,128)(2,1)}, bf16[1,128,128]{2,1,0:T(8,128)(2,1)}, bf16[9,128,128]{2,1,0:T(8,128)(2,1)}, bf16[8,128,128]{2,1,0...) custom-call(s32[1682]{0:T(1024)} %sort_slots.1.refs_0_, ...), custom_call_target="tpu_custom_call" | custom-call | flops 402653184 | bytes 4718592 | tf_op jit(solution)/shard_map/dense_and_backward_far/pallas_call | solution.py:294
  89.1 6.1 %collective-permute-start.27 = (bf16[8,128,128]{2,1,0:T(8,128)(2,1)}, bf16[8,128,128]{2,1,0:T(8,128)(2,1)S(1)}, u32[]{:S(2)}, u32[]{:S(2)}) collective-permute-start(bf16[8,128,128]{2,1,0:T(8,128)(2,1)} %get-tuple-element.41), channel_id=1, source_target_pairs={{0,28},{4,0},{8,4},{12,8},{16,12},{20,16},{24,20},{28,24},{32,60},... | collective-permute-start | bytes 786440 | tf_op jit(solution)/shard_map/ppermute | solution.py:30
  95.3 4.6 %backward_near.1 = (bf16[8,128,128]{2,1,0:T(8,128)(2,1)}, bf16[8,128,128]{2,1,0:T(8,128)(2,1)}, bf16[8,128,128]{2,1,0:T(8,128)(2,1)}, bf16[9,128,128]{2,1,0:T(8,...) custom-call(s32[1682]{0:T(1024)} %sort_slots.1.refs_0_, ...), custom_call_target="tpu_custom_call" | custom-call | flops 671088640 | bytes 7864320 | tf_op jit(solution)/shard_map/backward_near/pallas_call | solution.py:346
  99.9 3.3 %collective-permute-start.30 = (bf16[9,128,128]{2,1,0:T(8,128)(2,1)S(1)}, bf16[9,128,128]{2,1,0:T(8,128)(2,1)S(1)}, u32[]{:S(2)}, u32[]{:S(2)}) collective-permute-start(bf16[9,128,128]{2,1,0:T(8,128)(2,1)S(1)} %copy-done.21), channel_id=1, source_target_pairs={{0,28},{4,0},{8,4},{12,8},{16,12},{20,16},{24,20},{28,24},{32,60},... | collective-permute-start | bytes 884744 | tf_op jit(solution)/shard_map/ppermute | solution.py:30
  104.2 2.7 %collective-permute-start.28 = (bf16[8,128,128]{2,1,0:T(8,128)(2,1)S(1)}, bf16[8,128,128]{2,1,0:T(8,128)(2,1)S(1)}, u32[]{:S(2)}, u32[]{:S(2)}) collective-permute-start(bf16[8,128,128]{2,1,0:T(8,128)(2,1)S(1)} %add_convert_fusion.7), channel_id=1, source_target_pairs={{0,28},{4,0},{8,4},{12,8},{16,12},{20,16},{24,20},{28,24},{32,60},... | collective-permute-start | bytes 786440 | tf_op jit(solution)/shard_map/ppermute | solution.py:30
  107.4 2.6 %collective-permute-done.34 = bf16[9,128,128]{2,1,0:T(8,128)(2,1)S(1)} collective-permute-done((bf16[9,128,128]{2,1,0:T(8,128)(2,1)S(1)}, bf16[9,128,128]{2,1,0:T(8,128)(2,1)S(1)}, u32[]{:S(2)}, u32[]{:S(2)}) %collective-permute-start.34) | collective-permute-done | bytes 294944 | tf_op jit(solution)/shard_map/ppermute | solution.py:30
  110.0 1.0 add_convert_fusion.1
  111.2 2.7 %collective-permute-start.31 = (bf16[9,128,128]{2,1,0:T(8,128)(2,1)S(1)}, bf16[9,128,128]{2,1,0:T(8,128)(2,1)S(1)}, u32[]{:S(2)}, u32[]{:S(2)}) collective-permute-start(bf16[9,128,128]{2,1,0:T(8,128)(2,1)S(1)} %add_convert_fusion.4), channel_id=1, source_target_pairs={{0,28},{4,0},{8,4},{12,8},{16,12},{20,16},{24,20},{28,24},{32,60},... | collective-permute-start | bytes 884744 | tf_op jit(solution)/shard_map/ppermute | solution.py:30
  115.0 1.3 collective-permute-start.29
  117.6 1.8 %collective-permute-done.31 = bf16[9,128,128]{2,1,0:T(8,128)(2,1)S(1)} collective-permute-done((bf16[9,128,128]{2,1,0:T(8,128)(2,1)S(1)}, bf16[9,128,128]{2,1,0:T(8,128)(2,1)S(1)}, u32[]{:S(2)}, u32[]{:S(2)}) %collective-permute-start.31) | collective-permute-done | bytes 294944 | tf_op jit(solution)/shard_map/ppermute | solution.py:30
  119.4 1.0 add_convert_fusion.3
  120.5 3.2 %collective-permute-start.32 = (bf16[9,128,128]{2,1,0:T(8,128)(2,1)S(1)}, bf16[9,128,128]{2,1,0:T(8,128)(2,1)S(1)}, u32[]{:S(2)}, u32[]{:S(2)}) collective-permute-start(bf16[9,128,128]{2,1,0:T(8,128)(2,1)S(1)} %add_convert_fusion.3), channel_id=1, source_target_pairs={{0,28},{4,0},{8,4},{12,8},{16,12},{20,16},{24,20},{28,24},{32,60},... | collective-permute-start | bytes 884744 | tf_op jit(solution)/shard_map/ppermute | solution.py:30
  123.7 1.0 add_convert_fusion
  124.8 2.4 %collective-permute-done.25 = bf16[8,128,128]{2,1,0:T(8,128)(2,1)S(1)} collective-permute-done((bf16[8,128,128]{2,1,0:T(8,128)(2,1)S(1)}, bf16[8,128,128]{2,1,0:T(8,128)(2,1)S(1)}, u32[]{:S(2)}, u32[]{:S(2)}) %collective-permute-start.25) | collective-permute-done | bytes 262176 | tf_op jit(solution)/shard_map/ppermute | solution.py:30
  128.4 1.8 %collective-permute-done.32 = bf16[9,128,128]{2,1,0:T(8,128)(2,1)S(1)} collective-permute-done((bf16[9,128,128]{2,1,0:T(8,128)(2,1)S(1)}, bf16[9,128,128]{2,1,0:T(8,128)(2,1)S(1)}, u32[]{:S(2)}, u32[]{:S(2)}) %collective-permute-start.32) | collective-permute-done | bytes 294944 | tf_op jit(solution)/shard_map/ppermute | solution.py:30
  131.3 3.5 %collective-permute-start.33 = (bf16[9,128,128]{2,1,0:T(8,128)(2,1)S(1)}, bf16[9,128,128]{2,1,0:T(8,128)(2,1)S(1)}, u32[]{:S(2)}, u32[]{:S(2)}) collective-permute-start(bf16[9,128,128]{2,1,0:T(8,128)(2,1)S(1)} %add_convert_fusion.2), channel_id=1, source_target_pairs={{0,28},{4,0},{8,4},{12,8},{16,12},{20,16},{24,20},{28,24},{32,60},... | collective-permute-start | bytes 884744 | tf_op jit(solution)/shard_map/ppermute | solution.py:30
  134.8 2.9 %collective-permute-done.26 = bf16[8,128,128]{2,1,0:T(8,128)(2,1)S(1)} collective-permute-done((bf16[8,128,128]{2,1,0:T(8,128)(2,1)S(1)}, bf16[8,128,128]{2,1,0:T(8,128)(2,1)S(1)}, u32[]{:S(2)}, u32[]{:S(2)}) %collective-permute-start.26) | collective-permute-done | bytes 262176 | tf_op jit(solution)/shard_map/ppermute | solution.py:30
  137.8 2.6 %collective-permute-done.33 = bf16[9,128,128]{2,1,0:T(8,128)(2,1)S(1)} collective-permute-done((bf16[9,128,128]{2,1,0:T(8,128)(2,1)S(1)}, bf16[9,128,128]{2,1,0:T(8,128)(2,1)S(1)}, u32[]{:S(2)}, u32[]{:S(2)}) %collective-permute-start.33) | collective-permute-done | bytes 294944 | tf_op jit(solution)/shard_map/ppermute | solution.py:30
  141.2 1.2 collective-permute-start.38
  142.4 2.8 %collective-permute-done.39 = bf16[5,128,128]{2,1,0:T(8,128)(2,1)S(1)} collective-permute-done((bf16[5,128,128]{2,1,0:T(8,128)(2,1)S(1)}, bf16[5,128,128]{2,1,0:T(8,128)(2,1)S(1)}, u32[]{:S(2)}, u32[]{:S(2)}) %collective-permute-start.39) | collective-permute-done | bytes 163872 | tf_op jit(solution)/shard_map/ppermute | solution.py:30
  145.2 1.7 %collective-permute-done.38 = bf16[5,128,128]{2,1,0:T(8,128)(2,1)S(1)} collective-permute-done((bf16[5,128,128]{2,1,0:T(8,128)(2,1)S(1)}, bf16[5,128,128]{2,1,0:T(8,128)(2,1)S(1)}, u32[]{:S(2)}, u32[]{:S(2)}) %collective-permute-start.38) | collective-permute-done | bytes 163872 | tf_op jit(solution)/shard_map/ppermute | solution.py:30
  147.0 1.7 collective-permute-done.37
  148.8 9.7 %collective-permute-start.40 = (bf16[3,128,128]{2,1,0:T(8,128)(2,1)S(1)}, bf16[3,128,128]{2,1,0:T(8,128)(2,1)S(1)}, u32[]{:S(2)}, u32[]{:S(2)}) collective-permute-start(bf16[3,128,128]{2,1,0:T(8,128)(2,1)S(1)} %pad_maximum_fusion.5), channel_id=1, source_target_pairs={{0,128},{4,132},{8,136},{12,140},{16,144},{20,148},{24,152},{28,15... | collective-permute-start | bytes 294920 | tf_op jit(solution)/shard_map/ppermute | solution.py:30
  158.5 2.0 %collective-permute-done.40 = bf16[3,128,128]{2,1,0:T(8,128)(2,1)S(1)} collective-permute-done((bf16[3,128,128]{2,1,0:T(8,128)(2,1)S(1)}, bf16[3,128,128]{2,1,0:T(8,128)(2,1)S(1)}, u32[]{:S(2)}, u32[]{:S(2)}) %collective-permute-start.40) | collective-permute-done | bytes 98336 | tf_op jit(solution)/shard_map/ppermute | solution.py:30
  160.5 4.8 %collective-permute-start.41 = (f32[64,256]{1,0:T(8,128)S(1)}, f32[64,256]{1,0:T(8,128)S(1)}, u32[]{:S(2)}, u32[]{:S(2)}) collective-permute-start(f32[64,256]{1,0:T(8,128)S(1)} %pad_maximum_fusion.6), channel_id=1, source_target_pairs={{0,1},{1,0},{2,3},{3,2},{4,5},{5,4},{6,7},{7,6},{8,9},{9,8},{10,11... | collective-permute-start | bytes 196616 | tf_op jit(solution)/shard_map/ppermute | solution.py:34
  (119 shorter events, 16.1 us)
Async XLA Ops:
  0.6 4.0 %collective-permute-start = (bf16[2,128,128]{2,1,0:T(8,128)(2,1)}, bf16[2,128,128]{2,1,0:T(8,128)(2,1)S(1)}, u32[]{:S(2)}, u32[]{:S(2)}) collective-permute-start(bf16[2,128,128]{2,1,0:T(8,128)(2,1)} %bitcast.19), channel_id=1, source_target_pairs={{0,128},{4,132},{8,136},{12,140},{16,144},{20,148},{24,152},{28,15... | collective-permute-start | bytes 196616 | tf_op jit(solution)/shard_map/ppermute | solution.py:30
  5.5 6.7 %collective-permute-start.1 = (bf16[4,128,128]{2,1,0:T(8,128)(2,1)S(1)}, bf16[4,128,128]{2,1,0:T(8,128)(2,1)S(1)}, u32[]{:S(2)}, u32[]{:S(2)}) collective-permute-start(bf16[4,128,128]{2,1,0:T(8,128)(2,1)S(1)} %pad_maximum_fusion.4), channel_id=1, source_target_pairs={{0,96},{4,100},{8,104},{12,108},{16,112},{20,116},{24,120},{28,124... | collective-permute-start | bytes 393224 | tf_op jit(solution)/shard_map/ppermute | solution.py:30
  8.5 8.9 %collective-permute-start.5 = (bf16[4,128,128]{2,1,0:T(8,128)(2,1)S(1)}, bf16[4,128,128]{2,1,0:T(8,128)(2,1)S(1)}, u32[]{:S(2)}, u32[]{:S(2)}) collective-permute-start(bf16[4,128,128]{2,1,0:T(8,128)(2,1)S(1)} %pad_maximum_fusion.4), channel_id=1, source_target_pairs={{0,64},{4,68},{8,72},{12,76},{16,80},{20,84},{24,88},{28,92},{32,9... | collective-permute-start | bytes 393224 | tf_op jit(solution)/shard_map/ppermute | solution.py:30
  8.9 8.6 %collective-permute-start.6 = (bf16[4,128,128]{2,1,0:T(8,128)(2,1)S(1)}, bf16[4,128,128]{2,1,0:T(8,128)(2,1)S(1)}, u32[]{:S(2)}, u32[]{:S(2)}) collective-permute-start(bf16[4,128,128]{2,1,0:T(8,128)(2,1)S(1)} %pad_maximum_fusion.4), channel_id=1, source_target_pairs={{0,32},{4,36},{8,40},{12,44},{16,48},{20,52},{24,56},{28,60},{32,6... | collective-permute-start | bytes 393224 | tf_op jit(solution)/shard_map/ppermute | solution.py:30
  13.0 46.7 %copy-start.1 = (bf16[8,128,128]{2,1,0:T(8,128)(2,1)}, bf16[8,128,128]{2,1,0:T(8,128)(2,1)S(1)}, u32[]{:S(2)}) copy-start(bf16[8,128,128]{2,1,0:T(8,128)(2,1)S(1)} %pad_maximum_fusion.refs_2_) | copy-start | bytes 786436
  13.0 8.5 %collective-permute-start.2 = (bf16[8,128,128]{2,1,0:T(8,128)(2,1)S(1)}, bf16[8,128,128]{2,1,0:T(8,128)(2,1)S(1)}, u32[]{:S(2)}, u32[]{:S(2)}) collective-permute-start(bf16[8,128,128]{2,1,0:T(8,128)(2,1)S(1)} %pad_maximum_fusion.refs_2_), channel_id=1, source_target_pairs={{0,28},{4,0},{8,4},{12,8},{16,12},{20,16},{24,20},{28,24},{32,60},... | collective-permute-start | bytes 786440 | tf_op jit(solution)/shard_map/ppermute | solution.py:30
  17.5 42.3 %copy-start.2 = (bf16[8,128,128]{2,1,0:T(8,128)(2,1)}, bf16[8,128,128]{2,1,0:T(8,128)(2,1)S(1)}, u32[]{:S(2)}) copy-start(bf16[8,128,128]{2,1,0:T(8,128)(2,1)S(1)} %constant_dynamic-update-slice_fusion.refs_3_) | copy-start | bytes 786436
  17.5 7.6 %collective-permute-start.11 = (bf16[8,128,128]{2,1,0:T(8,128)(2,1)S(1)}, bf16[8,128,128]{2,1,0:T(8,128)(2,1)S(1)}, u32[]{:S(2)}, u32[]{:S(2)}) collective-permute-start(bf16[8,128,128]{2,1,0:T(8,128)(2,1)S(1)} %constant_dynamic-update-slice_fusion.refs_3_), channel_id=1, source_target_pairs={{0,4},{4,8},{8,12},{12,16},{16,20},{20,24},{24,28},{28,0},{32,36},... | collective-permute-start | bytes 786440 | tf_op jit(solution)/shard_map/ppermute | solution.py:30
  17.6 9.4 %collective-permute-start.7 = (bf16[8,128,128]{2,1,0:T(8,128)(2,1)S(1)}, bf16[8,128,128]{2,1,0:T(8,128)(2,1)S(1)}, u32[]{:S(2)}, u32[]{:S(2)}) collective-permute-start(bf16[8,128,128]{2,1,0:T(8,128)(2,1)S(1)} %constant_dynamic-update-slice_fusion.refs_3_), channel_id=1, source_target_pairs={{0,28},{4,0},{8,4},{12,8},{16,12},{20,16},{24,20},{28,24},{32,60},... | collective-permute-start | bytes 786440 | tf_op jit(solution)/shard_map/ppermute | solution.py:30
  21.5 8.9 %collective-permute-start.15 = (bf16[8,128,128]{2,1,0:T(8,128)(2,1)S(1)}, bf16[8,128,128]{2,1,0:T(8,128)(2,1)S(1)}, u32[]{:S(2)}, u32[]{:S(2)}) collective-permute-start(bf16[8,128,128]{2,1,0:T(8,128)(2,1)S(1)} %pad_maximum_fusion.refs_2_), channel_id=1, source_target_pairs={{0,4},{4,8},{8,12},{12,16},{16,20},{20,24},{24,28},{28,0},{32,36},... | collective-permute-start | bytes 786440 | tf_op jit(solution)/shard_map/ppermute | solution.py:30
  21.5 38.3 %copy-start.4 = (bf16[8,128,128]{2,1,0:T(8,128)(2,1)}, bf16[8,128,128]{2,1,0:T(8,128)(2,1)S(1)}, u32[]{:S(2)}) copy-start(bf16[8,128,128]{2,1,0:T(8,128)(2,1)S(1)} %collective-permute-done.2.refs_4_) | copy-start | bytes 786436
  21.5 11.1 %collective-permute-start.3 = (bf16[8,128,128]{2,1,0:T(8,128)(2,1)S(1)}, bf16[8,128,128]{2,1,0:T(8,128)(2,1)S(1)}, u32[]{:S(2)}, u32[]{:S(2)}) collective-permute-start(bf16[8,128,128]{2,1,0:T(8,128)(2,1)S(1)} %collective-permute-done.2.refs_4_), channel_id=1, source_target_pairs={{0,28},{4,0},{8,4},{12,8},{16,12},{20,16},{24,20},{28,24},{32,60},... | collective-permute-start | bytes 786440 | tf_op jit(solution)/shard_map/ppermute | solution.py:30
  25.2 10.8 %collective-permute-start.12 = (bf16[8,128,128]{2,1,0:T(8,128)(2,1)S(1)}, bf16[8,128,128]{2,1,0:T(8,128)(2,1)S(1)}, u32[]{:S(2)}, u32[]{:S(2)}) collective-permute-start(bf16[8,128,128]{2,1,0:T(8,128)(2,1)S(1)} %collective-permute-done.11.refs_11_), channel_id=1, source_target_pairs={{0,4},{4,8},{8,12},{12,16},{16,20},{20,24},{24,28},{28,0},{32,36},... | collective-permute-start | bytes 786440 | tf_op jit(solution)/shard_map/ppermute | solution.py:30
  27.0 20.8 %collective-permute-start.8 = (bf16[8,128,128]{2,1,0:T(8,128)(2,1)S(1)}, bf16[8,128,128]{2,1,0:T(8,128)(2,1)S(1)}, u32[]{:S(2)}, u32[]{:S(2)}) collective-permute-start(bf16[8,128,128]{2,1,0:T(8,128)(2,1)S(1)} %collective-permute-done.7.refs_5_), channel_id=1, source_target_pairs={{0,28},{4,0},{8,4},{12,8},{16,12},{20,16},{24,20},{28,24},{32,60},... | collective-permute-start | bytes 786440 | tf_op jit(solution)/shard_map/ppermute | solution.py:30
  30.4 20.4 %collective-permute-start.16 = (bf16[8,128,128]{2,1,0:T(8,128)(2,1)S(1)}, bf16[8,128,128]{2,1,0:T(8,128)(2,1)S(1)}, u32[]{:S(2)}, u32[]{:S(2)}) collective-permute-start(bf16[8,128,128]{2,1,0:T(8,128)(2,1)S(1)} %collective-permute-done.15.refs_10_), channel_id=1, source_target_pairs={{0,4},{4,8},{8,12},{12,16},{16,20},{20,24},{24,28},{28,0},{32,36},... | collective-permute-start | bytes 786440 | tf_op jit(solution)/shard_map/ppermute | solution.py:30
  32.6 18.2 %collective-permute-start.4 = (bf16[8,128,128]{2,1,0:T(8,128)(2,1)S(1)}, bf16[8,128,128]{2,1,0:T(8,128)(2,1)S(1)}, u32[]{:S(2)}, u32[]{:S(2)}) collective-permute-start(bf16[8,128,128]{2,1,0:T(8,128)(2,1)S(1)} %collective-permute-done.3.refs_6_), channel_id=1, source_target_pairs={{0,28},{4,0},{8,4},{12,8},{16,12},{20,16},{24,20},{28,24},{32,60},... | collective-permute-start | bytes 786440 | tf_op jit(solution)/shard_map/ppermute | solution.py:30
  36.0 17.4 %collective-permute-start.13 = (bf16[8,128,128]{2,1,0:T(8,128)(2,1)S(1)}, bf16[8,128,128]{2,1,0:T(8,128)(2,1)S(1)}, u32[]{:S(2)}, u32[]{:S(2)}) collective-permute-start(bf16[8,128,128]{2,1,0:T(8,128)(2,1)S(1)} %collective-permute-done.12.refs_9_), channel_id=1, source_target_pairs={{0,4},{4,8},{8,12},{12,16},{16,20},{20,24},{24,28},{28,0},{32,36},... | collective-permute-start | bytes 786440 | tf_op jit(solution)/shard_map/ppermute | solution.py:30
  36.0 9.0 %collective-permute-start.18 = (bf16[256,256]{1,0:T(8,128)(2,1)}, bf16[256,256]{1,0:T(8,128)(2,1)S(1)}, u32[]{:S(2)}, u32[]{:S(2)}) collective-permute-start(bf16[256,256]{1,0:T(8,128)(2,1)} %refs_5_), channel_id=1, source_target_pairs={{0,1},{1,0},{2,3},{3,2},{4,5},{5,4},{6,7},{7,6},{8,9},{9,8},{10,11... | collective-permute-start | bytes 393224 | tf_op jit(solution)/shard_map/ppermute | solution.py:34
  45.1 38.4 %copy-start.19 = (bf16[256,256]{1,0:T(8,128)(2,1)}, bf16[256,256]{1,0:T(8,128)(2,1)S(1)}, u32[]{:S(2)}) copy-start(bf16[256,256]{1,0:T(8,128)(2,1)S(1)} %collective-permute-done.18.refs_6_) | copy-start | bytes 393220
  45.1 9.1 %collective-permute-start.19 = (bf16[256,256]{1,0:T(8,128)(2,1)}, bf16[256,256]{1,0:T(8,128)(2,1)}, u32[]{:S(2)}, u32[]{:S(2)}) collective-permute-start(bf16[256,256]{1,0:T(8,128)(2,1)} %refs_5_), channel_id=1, source_target_pairs={{0,2},{1,3},{2,0},{3,1},{4,6},{5,7},{6,4},{7,5},{8,10},{9,11},{10,... | collective-permute-start | bytes 393224 | tf_op jit(solution)/shard_map/ppermute | solution.py:34
  47.8 16.4 %collective-permute-start.9 = (bf16[8,128,128]{2,1,0:T(8,128)(2,1)S(1)}, bf16[8,128,128]{2,1,0:T(8,128)(2,1)S(1)}, u32[]{:S(2)}, u32[]{:S(2)}) collective-permute-start(bf16[8,128,128]{2,1,0:T(8,128)(2,1)S(1)} %collective-permute-done.8.refs_7_), channel_id=1, source_target_pairs={{0,28},{4,0},{8,4},{12,8},{16,12},{20,16},{24,20},{28,24},{32,60},... | collective-permute-start | bytes 786440 | tf_op jit(solution)/shard_map/ppermute | solution.py:30
  50.8 13.5 %collective-permute-start.17 = (bf16[8,128,128]{2,1,0:T(8,128)(2,1)S(1)}, bf16[8,128,128]{2,1,0:T(8,128)(2,1)}, u32[]{:S(2)}, u32[]{:S(2)}) collective-permute-start(bf16[8,128,128]{2,1,0:T(8,128)(2,1)S(1)} %collective-permute-done.16.refs_8_), channel_id=1, source_target_pairs={{0,4},{4,8},{8,12},{12,16},{16,20},{20,24},{24,28},{28,0},{32,36},... | collective-permute-start | bytes 786440 | tf_op jit(solution)/shard_map/ppermute | solution.py:30
  50.8 13.4 %collective-permute-start.10 = (bf16[8,128,128]{2,1,0:T(8,128)(2,1)S(1)}, bf16[8,128,128]{2,1,0:T(8,128)(2,1)}, u32[]{:S(2)}, u32[]{:S(2)}) collective-permute-start(bf16[8,128,128]{2,1,0:T(8,128)(2,1)S(1)} %collective-permute-done.4.refs_2_), channel_id=1, source_target_pairs={{0,28},{4,0},{8,4},{12,8},{16,12},{20,16},{24,20},{28,24},{32,60},... | collective-permute-start | bytes 786440 | tf_op jit(solution)/shard_map/ppermute | solution.py:30
  53.5 11.1 %collective-permute-start.14 = (bf16[8,128,128]{2,1,0:T(8,128)(2,1)S(1)}, bf16[8,128,128]{2,1,0:T(8,128)(2,1)}, u32[]{:S(2)}, u32[]{:S(2)}) collective-permute-start(bf16[8,128,128]{2,1,0:T(8,128)(2,1)S(1)} %collective-permute-done.13.refs_7_), channel_id=1, source_target_pairs={{0,4},{4,8},{8,12},{12,16},{16,20},{20,24},{24,28},{28,0},{32,36},... | collective-permute-start | bytes 786440 | tf_op jit(solution)/shard_map/ppermute | solution.py:30
  54.2 10.1 %collective-permute-start.20 = (bf16[256,256]{1,0:T(8,128)(2,1)S(1)}, bf16[256,256]{1,0:T(8,128)(2,1)}, u32[]{:S(2)}, u32[]{:S(2)}) collective-permute-start(bf16[256,256]{1,0:T(8,128)(2,1)S(1)} %collective-permute-done.18.refs_6_), channel_id=1, source_target_pairs={{0,2},{1,3},{2,0},{3,1},{4,6},{5,7},{6,4},{7,5},{8,10},{9,11},{10,... | collective-permute-start | bytes 393224 | tf_op jit(solution)/shard_map/ppermute | solution.py:34
  68.7 4.7 %collective-permute-start.21 = (bf16[8,128,128]{2,1,0:T(8,128)(2,1)}, bf16[8,128,128]{2,1,0:T(8,128)(2,1)S(1)}, u32[]{:S(2)}, u32[]{:S(2)}) collective-permute-start(bf16[8,128,128]{2,1,0:T(8,128)(2,1)} %forward_far.1), channel_id=1, source_target_pairs={{0,1},{1,0},{2,3},{3,2},{4,5},{5,4},{6,7},{7,6},{8,9},{9,8},{10,11... | collective-permute-start | bytes 786440 | tf_op jit(solution)/shard_map/ppermute | solution.py:34
  74.4 9.1 %collective-permute-start.22 = (bf16[8,128,128]{2,1,0:T(8,128)(2,1)S(1)}, bf16[8,128,128]{2,1,0:T(8,128)(2,1)S(1)}, u32[]{:S(2)}, u32[]{:S(2)}) collective-permute-start(bf16[8,128,128]{2,1,0:T(8,128)(2,1)S(1)} %add_convert_fusion.11.refs_3_), channel_id=1, source_target_pairs={{0,2},{1,3},{2,0},{3,1},{4,6},{5,7},{6,4},{7,5},{8,10},{9,11},{10,... | collective-permute-start | bytes 786440 | tf_op jit(solution)/shard_map/ppermute | solution.py:34
  89.1 14.1 %collective-permute-start.27 = (bf16[8,128,128]{2,1,0:T(8,128)(2,1)}, bf16[8,128,128]{2,1,0:T(8,128)(2,1)S(1)}, u32[]{:S(2)}, u32[]{:S(2)}) collective-permute-start(bf16[8,128,128]{2,1,0:T(8,128)(2,1)} %get-tuple-element.41), channel_id=1, source_target_pairs={{0,28},{4,0},{8,4},{12,8},{16,12},{20,16},{24,20},{28,24},{32,60},... | collective-permute-start | bytes 786440 | tf_op jit(solution)/shard_map/ppermute | solution.py:30
  95.3 11.7 %collective-permute-start.23 = (bf16[8,128,128]{2,1,0:T(8,128)(2,1)}, bf16[8,128,128]{2,1,0:T(8,128)(2,1)S(1)}, u32[]{:S(2)}, u32[]{:S(2)}) collective-permute-start(bf16[8,128,128]{2,1,0:T(8,128)(2,1)} %get-tuple-element.38), channel_id=1, source_target_pairs={{0,4},{4,8},{8,12},{12,16},{16,20},{20,24},{24,28},{28,0},{32,36},... | collective-permute-start | bytes 786440 | tf_op jit(solution)/shard_map/ppermute | solution.py:30
  95.3 45.3 %copy-start.20 = (bf16[1,128,128]{2,1,0:T(8,128)(2,1)S(1)}, bf16[1,128,128]{2,1,0:T(8,128)(2,1)}, u32[]{:S(2)}) copy-start(bf16[1,128,128]{2,1,0:T(8,128)(2,1)} %get-tuple-element.42) | copy-start | bytes 98308
  99.9 40.6 %copy-start.18 = (bf16[8,128,128]{2,1,0:T(8,128)(2,1)S(1)}, bf16[8,128,128]{2,1,0:T(8,128)(2,1)}, u32[]{:S(2)}) copy-start(bf16[8,128,128]{2,1,0:T(8,128)(2,1)} %get-tuple-element.50) | copy-start | bytes 786436
  99.9 11.2 %collective-permute-start.30 = (bf16[9,128,128]{2,1,0:T(8,128)(2,1)S(1)}, bf16[9,128,128]{2,1,0:T(8,128)(2,1)S(1)}, u32[]{:S(2)}, u32[]{:S(2)}) collective-permute-start(bf16[9,128,128]{2,1,0:T(8,128)(2,1)S(1)} %copy-done.21), channel_id=1, source_target_pairs={{0,28},{4,0},{8,4},{12,8},{16,12},{20,16},{24,20},{28,24},{32,60},... | collective-permute-start | bytes 884744 | tf_op jit(solution)/shard_map/ppermute | solution.py:30
  103.2 6.8 %collective-permute-start.34 = (bf16[9,128,128]{2,1,0:T(8,128)(2,1)S(1)}, bf16[9,128,128]{2,1,0:T(8,128)(2,1)S(1)}, u32[]{:S(2)}, u32[]{:S(2)}) collective-permute-start(bf16[9,128,128]{2,1,0:T(8,128)(2,1)S(1)} %copy-done.22), channel_id=1, source_target_pairs={{0,4},{4,8},{8,12},{12,16},{16,20},{20,24},{24,28},{28,0},{32,36},... | collective-permute-start | bytes 884744 | tf_op jit(solution)/shard_map/ppermute | solution.py:30
  104.2 9.7 %collective-permute-start.28 = (bf16[8,128,128]{2,1,0:T(8,128)(2,1)S(1)}, bf16[8,128,128]{2,1,0:T(8,128)(2,1)S(1)}, u32[]{:S(2)}, u32[]{:S(2)}) collective-permute-start(bf16[8,128,128]{2,1,0:T(8,128)(2,1)S(1)} %add_convert_fusion.7), channel_id=1, source_target_pairs={{0,28},{4,0},{8,4},{12,8},{16,12},{20,16},{24,20},{28,24},{32,60},... | collective-permute-start | bytes 786440 | tf_op jit(solution)/shard_map/ppermute | solution.py:30
  107.1 9.2 %collective-permute-start.24 = (bf16[8,128,128]{2,1,0:T(8,128)(2,1)S(1)}, bf16[8,128,128]{2,1,0:T(8,128)(2,1)S(1)}, u32[]{:S(2)}, u32[]{:S(2)}) collective-permute-start(bf16[8,128,128]{2,1,0:T(8,128)(2,1)S(1)} %add_convert_fusion.10), channel_id=1, source_target_pairs={{0,4},{4,8},{8,12},{12,16},{16,20},{20,24},{24,28},{28,0},{32,36},... | collective-permute-start | bytes 786440 | tf_op jit(solution)/shard_map/ppermute | solution.py:30
  111.0 12.6 %collective-permute-start.35 = (bf16[9,128,128]{2,1,0:T(8,128)(2,1)S(1)}, bf16[9,128,128]{2,1,0:T(8,128)(2,1)S(1)}, u32[]{:S(2)}, u32[]{:S(2)}) collective-permute-start(bf16[9,128,128]{2,1,0:T(8,128)(2,1)S(1)} %add_convert_fusion.1), channel_id=1, source_target_pairs={{0,4},{4,8},{8,12},{12,16},{16,20},{20,24},{24,28},{28,0},{32,36},... | collective-permute-start | bytes 884744 | tf_op jit(solution)/shard_map/ppermute | solution.py:30
  111.2 8.2 %collective-permute-start.31 = (bf16[9,128,128]{2,1,0:T(8,128)(2,1)S(1)}, bf16[9,128,128]{2,1,0:T(8,128)(2,1)S(1)}, u32[]{:S(2)}, u32[]{:S(2)}) collective-permute-start(bf16[9,128,128]{2,1,0:T(8,128)(2,1)S(1)} %add_convert_fusion.4), channel_id=1, source_target_pairs={{0,28},{4,0},{8,4},{12,8},{16,12},{20,16},{24,20},{28,24},{32,60},... | collective-permute-start | bytes 884744 | tf_op jit(solution)/shard_map/ppermute | solution.py:30
  115.0 19.8 %collective-permute-start.29 = (bf16[8,128,128]{2,1,0:T(8,128)(2,1)S(1)}, bf16[8,128,128]{2,1,0:T(8,128)(2,1)S(1)}, u32[]{:S(2)}, u32[]{:S(2)}) collective-permute-start(bf16[8,128,128]{2,1,0:T(8,128)(2,1)S(1)} %add_convert_fusion.6), channel_id=1, source_target_pairs={{0,28},{4,0},{8,4},{12,8},{16,12},{20,16},{24,20},{28,24},{32,60},... | collective-permute-start | bytes 786440 | tf_op jit(solution)/shard_map/ppermute | solution.py:30
  117.3 9.9 %collective-permute-start.25 = (bf16[8,128,128]{2,1,0:T(8,128)(2,1)S(1)}, bf16[8,128,128]{2,1,0:T(8,128)(2,1)S(1)}, u32[]{:S(2)}, u32[]{:S(2)}) collective-permute-start(bf16[8,128,128]{2,1,0:T(8,128)(2,1)S(1)} %add_convert_fusion.9), channel_id=1, source_target_pairs={{0,4},{4,8},{8,12},{12,16},{16,20},{20,24},{24,28},{28,0},{32,36},... | collective-permute-start | bytes 786440 | tf_op jit(solution)/shard_map/ppermute | solution.py:30
  120.5 9.7 %collective-permute-start.32 = (bf16[9,128,128]{2,1,0:T(8,128)(2,1)S(1)}, bf16[9,128,128]{2,1,0:T(8,128)(2,1)S(1)}, u32[]{:S(2)}, u32[]{:S(2)}) collective-permute-start(bf16[9,128,128]{2,1,0:T(8,128)(2,1)S(1)} %add_convert_fusion.3), channel_id=1, source_target_pairs={{0,28},{4,0},{8,4},{12,8},{16,12},{20,16},{24,20},{28,24},{32,60},... | collective-permute-start | bytes 884744 | tf_op jit(solution)/shard_map/ppermute | solution.py:30
  124.7 13.1 %collective-permute-start.36 = (bf16[9,128,128]{2,1,0:T(8,128)(2,1)S(1)}, bf16[9,128,128]{2,1,0:T(8,128)(2,1)S(1)}, u32[]{:S(2)}, u32[]{:S(2)}) collective-permute-start(bf16[9,128,128]{2,1,0:T(8,128)(2,1)S(1)} %add_convert_fusion), channel_id=1, source_target_pairs={{0,4},{4,8},{8,12},{12,16},{16,20},{20,24},{24,28},{28,0},{32,36},... | collective-permute-start | bytes 884744 | tf_op jit(solution)/shard_map/ppermute | solution.py:30
  128.3 9.4 %collective-permute-start.26 = (bf16[8,128,128]{2,1,0:T(8,128)(2,1)S(1)}, bf16[8,128,128]{2,1,0:T(8,128)(2,1)S(1)}, u32[]{:S(2)}, u32[]{:S(2)}) collective-permute-start(bf16[8,128,128]{2,1,0:T(8,128)(2,1)S(1)} %add_convert_fusion.8), channel_id=1, source_target_pairs={{0,4},{4,8},{8,12},{12,16},{16,20},{20,24},{24,28},{28,0},{32,36},... | collective-permute-start | bytes 786440 | tf_op jit(solution)/shard_map/ppermute | solution.py:30
  131.3 9.2 %collective-permute-start.33 = (bf16[9,128,128]{2,1,0:T(8,128)(2,1)S(1)}, bf16[9,128,128]{2,1,0:T(8,128)(2,1)S(1)}, u32[]{:S(2)}, u32[]{:S(2)}) collective-permute-start(bf16[9,128,128]{2,1,0:T(8,128)(2,1)S(1)} %add_convert_fusion.2), channel_id=1, source_target_pairs={{0,28},{4,0},{8,4},{12,8},{16,12},{20,16},{24,20},{28,24},{32,60},... | collective-permute-start | bytes 884744 | tf_op jit(solution)/shard_map/ppermute | solution.py:30
  140.7 4.5 %collective-permute-start.39 = (bf16[5,128,128]{2,1,0:T(8,128)(2,1)S(1)}, bf16[5,128,128]{2,1,0:T(8,128)(2,1)S(1)}, u32[]{:S(2)}, u32[]{:S(2)}) collective-permute-start(bf16[5,128,128]{2,1,0:T(8,128)(2,1)S(1)} %get-tuple-element.57), channel_id=1, source_target_pairs={{0,96},{4,100},{8,104},{12,108},{16,112},{20,116},{24,120},{28,124... | collective-permute-start | bytes 491528 | tf_op jit(solution)/shard_map/ppermute | solution.py:30
  141.2 5.8 %collective-permute-start.38 = (bf16[5,128,128]{2,1,0:T(8,128)(2,1)S(1)}, bf16[5,128,128]{2,1,0:T(8,128)(2,1)S(1)}, u32[]{:S(2)}, u32[]{:S(2)}) collective-permute-start(bf16[5,128,128]{2,1,0:T(8,128)(2,1)S(1)} %get-tuple-element.56), channel_id=1, source_target_pairs={{0,64},{4,68},{8,72},{12,76},{16,80},{20,84},{24,88},{28,92},{32,9... | collective-permute-start | bytes 491528 | tf_op jit(solution)/shard_map/ppermute | solution.py:30
  142.4 6.2 %collective-permute-start.37 = (bf16[5,128,128]{2,1,0:T(8,128)(2,1)S(1)}, bf16[5,128,128]{2,1,0:T(8,128)(2,1)S(1)}, u32[]{:S(2)}, u32[]{:S(2)}) collective-permute-start(bf16[5,128,128]{2,1,0:T(8,128)(2,1)S(1)} %get-tuple-element.55), channel_id=1, source_target_pairs={{0,32},{4,36},{8,40},{12,44},{16,48},{20,52},{24,56},{28,60},{32,6... | collective-permute-start | bytes 491528 | tf_op jit(solution)/shard_map/ppermute | solution.py:30
  148.8 11.7 %collective-permute-start.40 = (bf16[3,128,128]{2,1,0:T(8,128)(2,1)S(1)}, bf16[3,128,128]{2,1,0:T(8,128)(2,1)S(1)}, u32[]{:S(2)}, u32[]{:S(2)}) collective-permute-start(bf16[3,128,128]{2,1,0:T(8,128)(2,1)S(1)} %pad_maximum_fusion.5), channel_id=1, source_target_pairs={{0,128},{4,132},{8,136},{12,140},{16,144},{20,148},{24,152},{28,15... | collective-permute-start | bytes 294920 | tf_op jit(solution)/shard_map/ppermute | solution.py:30
  160.5 5.7 %collective-permute-start.41 = (f32[64,256]{1,0:T(8,128)S(1)}, f32[64,256]{1,0:T(8,128)S(1)}, u32[]{:S(2)}, u32[]{:S(2)}) collective-permute-start(f32[64,256]{1,0:T(8,128)S(1)} %pad_maximum_fusion.6), channel_id=1, source_target_pairs={{0,1},{1,0},{2,3},{3,2},{4,5},{5,4},{6,7},{7,6},{8,9},{9,8},{10,11... | collective-permute-start | bytes 196616 | tf_op jit(solution)/shard_map/ppermute | solution.py:34
  (17 other events, 307.1 us)

commit v2 on v1

v2 whole, which is shorter than its diff:
```python
import math

import jax
import jax.numpy as jnp
from jax import lax
from jax.experimental import pallas as pl
from jax.experimental.pallas import tpu as pltpu
from jax.sharding import PartitionSpec as P

NX, NY, NZ = 2, 4, 8
UNROLL = 16
NEAR = (0, 1, 2, 6, 7)
FAR = (3, 4, 5)
F32 = jnp.float32
BF16 = jnp.bfloat16
VMEM_LIMIT = 24 * 2**20


def section_index(x, y, z):
    return ((x % NX) * NY + y % NY) * NZ + z % NZ


def send(value, dx=0, dy=0, dz=0):
    pairs = [
        (section_index(x, y, z), section_index(x + dx, y + dy, z + dz))
        for x in range(NX)
        for y in range(NY)
        for z in range(NZ)
    ]
    return lax.ppermute(value, "section", pairs)


def send_team(value, mask):
    return lax.ppermute(value, "team", [(t, t ^ mask) for t in range(4)])


def fence(*arrays):
    return lax.optimization_barrier(arrays)


def add(*terms):
    total = terms[0].astype(F32)
    for term in terms[1:]:
        total = total + term.astype(F32)
    return total


def join(*arrays):
    return jnp.concatenate(arrays)


def sort_kernel(row_tiles, keys, out):
    slots = keys.shape[0]
    region = slots + UNROLL
    blocks = NY * NX * 2

    def body(step, carry):
        near_n, far_n = carry
        for j in range(8):
            key = keys[step * 8 + j]
            is_near = (key >> 24) & 1
            is_far = key >> 25
            spot = jnp.where(is_far == 1, region + far_n, near_n)
            out[jnp.where(is_near + is_far == 1, spot, 2 * region)] = key
            near_n = near_n + is_near
            far_n = far_n + is_far
        return near_n, far_n

    zero = jnp.int32(0)
    near_n, far_n = lax.fori_loop(0, slots // 8, body, (zero, zero))
    for j in range(UNROLL):
        out[near_n + j] = (row_tiles << 8) + (len(NEAR) * blocks << 12)
        out[region + far_n + j] = (row_tiles << 8) + (len(FAR) * blocks << 12)
    out[2 * region + UNROLL] = (near_n + UNROLL - 1) // UNROLL
    out[2 * region + UNROLL + 1] = (far_n + UNROLL - 1) // UNROLL


def sort_slots(rows, cols, count, me, row_tiles):
    slots = rows.shape[0]
    blocks = NY * NX * 2
    owner = cols // 2
    dx = (owner // (NY * NZ)) ^ (me // (NY * NZ))
    dy = (owner // NZ - me // NZ) % NY
    dz = (owner - me) % NZ
    far = (dz >= FAR[0]) & (dz <= FAR[-1])
    place = jnp.where(dz < FAR[0], dz, dz - FAR[0]) * blocks + dy * (NX * 2) + dx * 2 + cols % 2
    ids = jnp.arange(slots, dtype=jnp.int32)
    group = jnp.where(ids < count, jnp.where(far, 2, 1), 0)
    keys = ids + (rows << 8) + (place << 12) + (group << 24)
    smem = pl.BlockSpec(memory_space=pltpu.SMEM)

    def kernel(*refs):
        sort_kernel(row_tiles, *refs)

    return pl.pallas_call(
        kernel,
        out_shape=jax.ShapeDtypeStruct((2 * (slots + UNROLL) + UNROLL + 2,), jnp.int32),
        in_specs=[smem],
        out_specs=smem,
        name="sort_slots",
    )(keys.astype(jnp.int32))


class Slots:
    def __init__(self, ref, group):
        self.ref = ref
        length = ref.shape[0] - 2
        self.start = group * ((length - UNROLL) // 2)
        self.chunks = ref[length + group]

    def slot(self, i):
        return self.ref[self.start + i] & 255

    def row(self, i):
        return (self.ref[self.start + i] >> 8) & 15

    def col(self, i):
        return (self.ref[self.start + i] >> 12) & 255

    def each(self, fn):
        def body(c, carry):
            for j in range(UNROLL):
                fn(c * UNROLL + j)
            return carry

        lax.fori_loop(0, self.chunks, body, 0)


def forward_kernel(group, spans, slots_ref, member_ref, tiles, *refs):
    n = len(spans)
    pieces = refs[:n]
    before = refs[n] if group else None
    *outs, feat, acc, fsem = refs[n + group :]
    slots = Slots(slots_ref, group)
    copies = []
    for i, (at, size) in enumerate(spans):
        copies.append(pltpu.make_async_copy(pieces[i], feat.at[pl.ds(at, size)], fsem.at[i]))
        copies[-1].start()
    acc[...] = before[...] if group else jnp.zeros_like(acc)
    feat[feat.shape[0] - 1] = jnp.zeros(feat.shape[1:], feat.dtype)
    for copy in copies:
        copy.wait()

    def one(i):
        r = slots.row(i)
        tile = tiles[slots.slot(i)]
        acc[r] = acc[r] + jnp.dot(tile, feat[slots.col(i)], preferred_element_type=F32)

    slots.each(one)
    if group:
        half = outs[0].shape[0]
        core = member_ref[0] % 2
        outs[0][...] = acc[pl.ds(core * half, half)].astype(BF16)
        outs[1][...] = acc[pl.ds((1 - core) * half, half)].astype(BF16)
    else:
        outs[0][...] = acc[...]


def forward_call(group, slot_info, member, tiles, pieces, spans, before, row_tiles):
    tile = tiles.shape[-1]
    fin = pieces[0].shape[-1]
    blocks = sum(size for _, size in spans)
    smem = pl.BlockSpec(memory_space=pltpu.SMEM)
    vmem = pl.BlockSpec(memory_space=pltpu.VMEM)
    hbm = pl.BlockSpec(memory_space=pl.ANY)

    def kernel(*refs):
        forward_kernel(group, spans, *refs)

    if group:
        out_shape = [jax.ShapeDtypeStruct((row_tiles // 2, tile, fin), BF16)] * 2
    else:
        out_shape = [jax.ShapeDtypeStruct((row_tiles + 1, tile, fin), F32)]
    return pl.pallas_call(
        kernel,
        out_shape=out_shape,
        in_specs=[smem] * 2 + [vmem] + [hbm] * len(pieces) + [vmem] * group,
        out_specs=[vmem] * len(out_shape),
        scratch_shapes=[
            pltpu.VMEM((blocks + 1, tile, fin), BF16),
            pltpu.VMEM((row_tiles + 1, tile, fin), F32),
            pltpu.SemaphoreType.DMA((len(pieces),)),
        ],
        compiler_params=pltpu.CompilerParams(vmem_limit_bytes=VMEM_LIMIT),
        cost_estimate=pl.CostEstimate(
            flops=blocks * 2 * 2 * tile**3, bytes_accessed=blocks * 4 * tile**2, transcendentals=0
        ),
        name="forward_far" if group else "forward_near",
    )(slot_info, member, tiles, *pieces, *([before] if group else []))


def backward_tiles(slots, layout, tiles, backs, outs, rider, acc):
    def one(i):
        c = slots.col(i)
        tile = tiles[slots.slot(i)]
        acc[c] = acc[c] + jnp.dot(backs[slots.row(i)], tile, preferred_element_type=F32)

    slots.each(one)
    size = acc.shape[0] // len(layout)
    for i, kind in enumerate(layout):
        outs[i][pl.ds(0, size)] = acc[pl.ds(i * size, size)].astype(BF16)
        if kind:
            extra = rider[...] if kind == "rider" else jnp.zeros_like(outs[i][pl.ds(size, 1)])
            outs[i][pl.ds(size, 1)] = extra


def piece_shapes(layout, size, fin, tile):
    return [
        jax.ShapeDtypeStruct((size + 1 if kind else size, fin, tile), BF16) for kind in layout
    ]


def backward_far_kernel(
    layout, slots_ref, member_ref, tiles, sum_a, sum_b, c0, c1, c2, c3, weight,
    out, rider, backs, *refs,
):
    n = len(layout)
    outs = refs[:n]
    acc, agg, gpre, wfull = refs[n:]
    member = member_ref[0]
    slots = Slots(slots_ref, 1)
    half, tile, fin = sum_a.shape
    node_dev = out.shape[0]
    per_dev = node_dev // tile
    nodes = half * tile
    for source, which in ((sum_a, member % 2), (sum_b, 1 - member % 2)):
        part = pl.ds(pl.multiple_of(which * nodes, nodes), nodes)
        agg[part, :] = source[...].reshape(nodes, fin)
    acc[...] = jnp.zeros_like(acc)
    for d, cot in enumerate((c0, c1, c2, c3)):
        who = member ^ d
        at = pl.multiple_of(who * node_dev, node_dev)
        mine = agg[pl.ds(at, node_dev), :]
        pre = jnp.dot(mine, weight[...], preferred_element_type=F32)
        sig = jax.nn.sigmoid(pre)
        if d == 0:
            out[...] = (pre * sig).astype(BF16)
        grad = (cot[...].astype(F32) * sig * (1.0 + pre * (1.0 - sig))).astype(BF16)
        gpre[pl.ds(at, node_dev), :] = grad
        back = lax.dot_general(
            weight[...], grad, (((1,), (1,)), ((), ())), preferred_element_type=F32
        ).astype(BF16)
        for j in range(per_dev):
            backs[who * per_dev + j] = back[:, j * tile : (j + 1) * tile]
    backs[backs.shape[0] - 1] = jnp.zeros(backs.shape[1:], BF16)
    wfull[...] = lax.dot_general(
        agg[...], gpre[...], (((0,), (0,)), ((), ())), preferred_element_type=F32
    )
    fin, fout = wfull.shape
    share = fin // 2
    part = wfull[pl.ds(pl.multiple_of(member % 2 * share, share), share), :].astype(BF16)
    rider[0, pl.ds(0, share), :] = part[:, : fout // 2]
    rider[0, pl.ds(share, share), :] = part[:, fout // 2 :]
    backward_tiles(slots, layout, tiles, backs, outs, rider, acc)


def backward_far_call(slot_info, member, tiles, sum_a, sum_b, cots, weight, size):
    tile = tiles.shape[-1]
    half, _, fin = sum_a.shape
    row_tiles = 2 * half
    node_dev, fout = cots[0].shape
    nodes = row_tiles * tile
    layout = (None, "rider", None, "rider", None, "none")
    blocks = size * len(layout)
    smem = pl.BlockSpec(memory_space=pltpu.SMEM)
    vmem = pl.BlockSpec(memory_space=pltpu.VMEM)

    def kernel(*refs):
        backward_far_kernel(layout, *refs)

    return pl.pallas_call(
        kernel,
        out_shape=[
            jax.ShapeDtypeStruct((node_dev, fout), BF16),
            jax.ShapeDtypeStruct((1, fin, tile), BF16),
            jax.ShapeDtypeStruct((row_tiles + 1, fin, tile), BF16),
            *piece_shapes(layout, size, fin, tile),
        ],
        in_specs=[smem] * 2 + [vmem] * 8,
        out_specs=[vmem] * (3 + len(layout)),
        scratch_shapes=[
            pltpu.VMEM((blocks + 1, fin, tile), F32),
            pltpu.VMEM((nodes, fin), BF16),
            pltpu.VMEM((nodes, fout), BF16),
            pltpu.VMEM((fin, fout), F32),
        ],
        compiler_params=pltpu.CompilerParams(vmem_limit_bytes=VMEM_LIMIT),
        cost_estimate=pl.CostEstimate(
            flops=blocks * 2 * 2 * tile**3, bytes_accessed=blocks * 6 * tile**2, transcendentals=0
        ),
        name="dense_and_backward_far",
    )(slot_info, member, tiles, sum_a, sum_b, *cots, weight)


def backward_near_kernel(layout, slots_ref, tiles, backs, *refs):
    n = len(layout)
    outs = refs[:n]
    (acc,) = refs[n:]
    slots = Slots(slots_ref, 0)
    acc[...] = jnp.zeros_like(acc)
    backward_tiles(slots, layout, tiles, backs, outs, None, acc)


def backward_near_call(slot_info, tiles, backs, size):
    tile = tiles.shape[-1]
    fin = backs.shape[1]
    layout = (None, None) + (None, "none") * 4
    blocks = size * len(layout)
    smem = pl.BlockSpec(memory_space=pltpu.SMEM)
    vmem = pl.BlockSpec(memory_space=pltpu.VMEM)

    def kernel(*refs):
        backward_near_kernel(layout, *refs)

    return pl.pallas_call(
        kernel,
        out_shape=piece_shapes(layout, size, fin, tile),
        in_specs=[smem, vmem, vmem],
        out_specs=[vmem] * len(layout),
        scratch_shapes=[
            pltpu.VMEM((blocks + 1, fin, tile), F32),
        ],
        compiler_params=pltpu.CompilerParams(vmem_limit_bytes=VMEM_LIMIT),
        cost_estimate=pl.CostEstimate(
            flops=blocks * 2 * 2 * tile**3, bytes_accessed=blocks * 6 * tile**2, transcendentals=0
        ),
        name="backward_near",
    )(slot_info, tiles, backs)


def gather_features(features, cotangent, slot_info, tile, near_call):
    fin = features.shape[1]
    mine = features.reshape(-1, tile, fin)
    other, cot1 = fence(send(mine, dx=1), send_team(cotangent, 1))
    own = join(mine, other)
    y1 = send(own, dy=-1)
    y3 = send(own, dy=1)
    y2 = send(own, dy=-2)
    y1, y3, slot_info = fence(y1, y3, slot_info)
    up0, up1 = [join(own, y1)], [join(y2, y3)]
    down0, down1 = [up0[0]], [up1[0]]
    for step in range(4):
        up0.append(send(up0[-1], dz=-1))
        down1.append(send(down1[-1], dz=1))
        if step < 3:
            down0.append(send(down0[-1], dz=1))
            up1.append(send(up1[-1], dz=-1))
    cot2 = send_team(cotangent, 2)
    cot3 = send_team(cot1, 2)
    near = [up0[0], up1[0], up0[1], up1[1], up0[2], up1[2]]
    near += [down0[2], down1[2], down0[1], down1[1]]
    near_sum = near_call(slot_info, near)
    near_sum, cot2, cot3 = fence(near_sum, cot2, cot3)
    far = [up0[3], up1[3], up0[4], down1[4], down0[3], down1[3]]
    return near_sum, far, (cotangent, cot1, cot2, cot3), slot_info


def spans_of(pieces):
    spans, at = [], 0
    for piece in pieces:
        spans.append((at, piece.shape[0]))
        at += piece.shape[0]
    return spans


def add_pair(a, b, c, d):
    vmem = pl.BlockSpec(memory_space=pltpu.VMEM)

    def kernel(a_ref, b_ref, c_ref, d_ref, ab_ref, cd_ref):
        for x, y, out in ((a_ref, b_ref, ab_ref), (c_ref, d_ref, cd_ref)):
            out[...] = (x[...].astype(F32) + y[...].astype(F32)).astype(BF16)

    return pl.pallas_call(
        kernel,
        out_shape=[jax.ShapeDtypeStruct(a.shape, BF16), jax.ShapeDtypeStruct(c.shape, BF16)],
        in_specs=[vmem] * 4,
        out_specs=[vmem] * 2,
        compiler_params=pltpu.CompilerParams(vmem_limit_bytes=8 * 2**20),
        name="add_pair",
    )(a, b, c, d)


def ring_sums(arrived, long, short, dz):
    ahead, back = [arrived], []
    for i, (term, other) in enumerate(zip(long, short)):
        if i:
            message, reply = add_pair(term, ahead[-1], other, back[-1])
        else:
            message, reply = add(term, ahead[-1]).astype(BF16), other
        message, reply = fence(send(message, dz=dz), send(reply, dz=-dz))
        ahead.append(message)
        back.append(reply)
    return ahead, back


def scatter_sums(near_call, far, rider):
    g3, g4, g5 = [far[2 * i : 2 * i + 2] for i in range(3)]
    first0, first1 = send(g4[0], dz=1), send(g4[1], dz=-1)
    first0, *near = fence(first0, *near_call())
    g0, g1, g2, g6, g7 = [near[2 * i : 2 * i + 2] for i in range(5)]
    up0, down0 = ring_sums(first0, (g3[0], g2[0], g1[0]), (g5[0], g6[0], g7[0]), 1)
    down1, up1 = ring_sums(first1, (g5[1], g6[1], g7[1]), (g3[1], g2[1], g1[1]), -1)
    size = g0[0].shape[0]
    plane0 = add(g0[0], up0[-1], down0[-1])
    plane1 = add(g0[1], up1[-1][:size], down1[-1][:size]).astype(BF16)
    u1, u2, u3 = [part[size:] for part in up1]
    d1, d2, d3, d4 = [part[size:] for part in down1]
    rider = ((add(rider, d4) + add(u2, d2)) + (add(u1, d3) + add(u3, d1))).astype(BF16)
    half = size // 2
    got1 = send(join(plane0[half:].astype(BF16), rider), dy=1)
    got2 = send(join(plane1[:half], rider), dy=2)
    got3 = send(join(plane1[half:], rider), dy=-1)
    line = add(plane0[:half], got1[:half], got2[:half], got3[:half])
    rider = (add(rider, got2[half:]) + add(got1[half:], got3[half:])).astype(BF16)
    size = half
    half = size // 2
    got = send(join(line[half:].astype(BF16), rider), dx=1)
    total = add(line[:half], got[:half])
    weight = add(rider, got[half:])[0]
    share = weight.shape[0] // 2
    weight = jnp.concatenate([weight[:share], weight[share:]], axis=1)
    other = send_team(weight, 1)
    low = lax.axis_index("team") % 2 == 0
    return total, jnp.where(low, join(weight, other), join(other, weight))


def per_device(features, weight, tiles, tile_rows, tile_cols, tile_count, cotangent):
    node_dev, fin = features.shape
    tile = tiles.shape[-1]
    slots = tiles.shape[2]
    sections = lax.axis_size("section")
    teams = lax.axis_size("team")
    row_tiles = node_dev // tile * teams
    scale = 1.0 / math.sqrt(node_dev * sections * teams)
    slab = tiles.reshape(slots, tile, tile)
    slot_info = sort_slots(
        tile_rows.reshape(slots),
        tile_cols.reshape(slots),
        tile_count.reshape(()),
        lax.axis_index("section"),
        row_tiles,
    )
    member = lax.axis_index("team").astype(jnp.int32).reshape(1)


    def near_call(info, pieces):
        return forward_call(0, info, member, slab, pieces, spans_of(pieces), None, row_tiles)[0]

    near_sum, far, cots, slot_info = gather_features(
        features, cotangent, slot_info, tile, near_call
    )
    mine, theirs = forward_call(
        1, slot_info, member, slab, far, spans_of(far), near_sum, row_tiles
    )
    pair = add(mine, send_team(theirs, 1)).astype(BF16)
    mine = add(pair, send_team(pair, 2)).astype(BF16)
    size = far[0].shape[0]
    output, rider, backs, *far_terms = backward_far_call(
        slot_info, member, slab, mine, send_team(mine, 1), cots, weight, size
    )
    total, weight_sum = scatter_sums(
        lambda: backward_near_call(slot_info, slab, backs, size), far_terms, rider
    )
    grad_features = total.transpose(0, 2, 1).reshape(node_dev, fin).astype(BF16)
    return output, grad_features, weight_sum * scale


def solution(mesh):
    in_specs = (
        P(("section", "team"), None),
        P(),
        P("section", "team", None, None, None),
        P("section", "team", None),
        P("section", "team", None),
        P("section", "team"),
        P(("section", "team"), None),
    )
    out_specs = (P(("section", "team"), None), P(("section", "team"), None), P())
    return jax.shard_map(
        per_device, mesh=mesh, in_specs=in_specs, out_specs=out_specs, check_vma=False
    )
```

time: 168 us -> 153 us (0.911)
  Pallas kernels: 22.1 us -> 11.5 us
  waiting for transfers between devices: 42.6 us -> 52.2 us
  starting transfers between devices: 85.4 us -> 76.2 us
  other arithmetic: 12.9 us -> 4.98 us
  local copies, waits for them, and re-layouts: 1.94 us -> 5.58 us
    ppermute x36, waiting for transfers between devices: 32.3 us -> 46.8 us  [send(): return lax.ppermute(value, 'section', pairs)]
    ppermute x36, starting transfers between devices: 64.9 us -> 55.3 us  [send(): return lax.ppermute(value, 'section', pairs)]
    convert_element_type x11 -> x4, other arithmetic: 9.44 us -> 0.23 us  [the longest x2 0.15 us: ring_sums(): message, reply = (add(term, ahead[-1]).astype(BF16), other)]
    pallas_call x3 -> x7, Pallas kernels: 12.6 us -> 6.71 us  [the longest x2 3.72 us: forward_call(): pl.pallas_call(kernel, out_shape=out_shape, in_specs=[smem] * 2 + [vmem]...]
    ppermute x6 -> x7, waiting for transfers between devices: 10.3 us -> 5.47 us  [send_team(): return lax.ppermute(value, 'team', [(t, t ^ mask) for t in range(4)])]
    unnamed x47 -> x17, local copies, waits for them, and re-layouts: 1.12 us -> 4.76 us
    pallas_call x1, Pallas kernels: 4.57 us -> 1.8 us  [backward_near_call(): pl.pallas_call(kernel, out_shape=piece_shapes(layout, size, fin, tile), i...]
    pallas_call x1, Pallas kernels: 4.9 us -> 2.99 us  [backward_far_call(): pl.pallas_call(kernel, out_shape=[jax.ShapeDtypeStruct((node_dev, fout),...]
  transfers between devices with their start and end apart: 42 -> 43, of which waited for: 20 -> 25; matrix products, arithmetic and copies ran while one was open for 6% -> 3% of each run, Pallas kernels for 8% -> 4%
where the time goes in v2:
time: 153 us; the launch traced here: 152 us
  starting transfers between devices  76.2 us (50%)
  waiting for transfers between devices  52.2 us (34%)
  Pallas kernels  11.5 us (8%)
  local copies, waits for them, and re-layouts  5.58 us (4%)
  other arithmetic  4.98 us (3%)
  between operations  1.69 us (1%)
    ppermute x36, starting transfers between devices, send(): return lax.ppermute(value, 'section', pairs)  55.3 us
    ppermute x36, waiting for transfers between devices, send(): return lax.ppermute(value, 'section', pairs)  46.8 us
    ppermute x7, starting transfers between devices, send_team(): return lax.ppermute(value, 'team', [(t, t ^ mask) for t in range(4)])  21 us
    ppermute x7, waiting for transfers between devices, send_team(): return lax.ppermute(value, 'team', [(t, t ^ mask) for t in range(4)])  5.47 us
    unnamed x17, local copies, waits for them, and re-layouts  4.76 us
    pallas_call x2, Pallas kernels, forward_call(): pl.pallas_call(kernel, out_shape=out_shape, in_specs=[smem] * 2 + [vmem]...  3.72 us
  transfers between devices with their start and end apart: 43, of which 25 were waited for; matrix products, arithmetic and copies ran while one was open for 3% of the time, Pallas kernels for 4%

profile of v2, /device:TPU:1, one launch (start us, length us, event | category | flops | bytes accessed | tf_op | source)
XLA Modules:
  0.0 152.2 jit_solution(1541469501840571278)
XLA Ops:
  0.6 2.1 %collective-permute-start = (bf16[2,128,128]{2,1,0:T(8,128)(2,1)}, bf16[2,128,128]{2,1,0:T(8,128)(2,1)S(1)}, u32[]{:S(2)}, u32[]{:S(2)}) collective-permute-start(bf16[2,128,128]{2,1,0:T(8,128)(2,1)} %bitcast.20), channel_id=1, source_target_pairs={{0,128},{4,132},{8,136},{12,140},{16,144},{20,148},{24,152},{28,15... | collective-permute-start | bytes 196616 | tf_op jit(solution)/shard_map/ppermute | solution.py:30
  2.8 1.3 collective-permute-start.1
  6.3 2.5 %collective-permute-start.2 = (bf16[4,128,128]{2,1,0:T(8,128)(2,1)S(1)}, bf16[4,128,128]{2,1,0:T(8,128)(2,1)S(1)}, u32[]{:S(2)}, u32[]{:S(2)}) collective-permute-start(bf16[4,128,128]{2,1,0:T(8,128)(2,1)S(1)} %pad_maximum_fusion.4), channel_id=1, source_target_pairs={{0,96},{4,100},{8,104},{12,108},{16,112},{20,116},{24,120},{28,124... | collective-permute-start | bytes 393224 | tf_op jit(solution)/shard_map/ppermute | solution.py:30
  8.8 1.6 %collective-permute-start.7 = (bf16[4,128,128]{2,1,0:T(8,128)(2,1)S(1)}, bf16[4,128,128]{2,1,0:T(8,128)(2,1)S(1)}, u32[]{:S(2)}, u32[]{:S(2)}) collective-permute-start(bf16[4,128,128]{2,1,0:T(8,128)(2,1)S(1)} %pad_maximum_fusion.4), channel_id=1, source_target_pairs={{0,64},{4,68},{8,72},{12,76},{16,80},{20,84},{24,88},{28,92},{32,9... | collective-permute-start | bytes 393224 | tf_op jit(solution)/shard_map/ppermute | solution.py:30
  10.4 1.3 fusion.10.refs_0_
  11.7 2.5 %sort_slots.1.refs_0_ = s32[562]{0:T(1024)} custom-call(s32[256]{0:T(256)} %fusion.10.refs_0_), custom_call_target="tpu_custom_call" | custom-call | tf_op jit(solution)/shard_map/sort_slots/pallas_call | solution.py:95
  14.2 1.7 %collective-permute-done.3 = bf16[4,128,128]{2,1,0:T(8,128)(2,1)S(1)} collective-permute-done((bf16[4,128,128]{2,1,0:T(8,128)(2,1)S(1)}, bf16[4,128,128]{2,1,0:T(8,128)(2,1)S(1)}, u32[]{:S(2)}, u32[]{:S(2)}) %collective-permute-start.3) | collective-permute-done | bytes 131104 | tf_op jit(solution)/shard_map/ppermute | solution.py:30
  16.7 5.7 %collective-permute-start.4 = (bf16[8,128,128]{2,1,0:T(8,128)(2,1)S(1)}, bf16[8,128,128]{2,1,0:T(8,128)(2,1)S(1)}, u32[]{:S(2)}, u32[]{:S(2)}) collective-permute-start(bf16[8,128,128]{2,1,0:T(8,128)(2,1)S(1)} %pad_maximum_fusion.refs_3_), channel_id=1, source_target_pairs={{0,28},{4,0},{8,4},{12,8},{16,12},{20,16},{24,20},{28,24},{32,60},... | collective-permute-start | bytes 786440 | tf_op jit(solution)/shard_map/ppermute | solution.py:30
  22.5 2.7 %collective-permute-start.8 = (bf16[8,128,128]{2,1,0:T(8,128)(2,1)S(1)}, bf16[8,128,128]{2,1,0:T(8,128)(2,1)S(1)}, u32[]{:S(2)}, u32[]{:S(2)}) collective-permute-start(bf16[8,128,128]{2,1,0:T(8,128)(2,1)S(1)} %constant_dynamic-update-slice_fusion.refs_4_), channel_id=1, source_target_pairs={{0,28},{4,0},{8,4},{12,8},{16,12},{20,16},{24,20},{28,24},{32,60},... | collective-permute-start | bytes 786440 | tf_op jit(solution)/shard_map/ppermute | solution.py:30
  25.7 3.1 %collective-permute-start.5 = (bf16[8,128,128]{2,1,0:T(8,128)(2,1)S(1)}, bf16[8,128,128]{2,1,0:T(8,128)(2,1)S(1)}, u32[]{:S(2)}, u32[]{:S(2)}) collective-permute-start(bf16[8,128,128]{2,1,0:T(8,128)(2,1)S(1)} %collective-permute-done.4.refs_5_), channel_id=1, source_target_pairs={{0,28},{4,0},{8,4},{12,8},{16,12},{20,16},{24,20},{28,24},{32,60},... | collective-permute-start | bytes 786440 | tf_op jit(solution)/shard_map/ppermute | solution.py:30
  28.9 1.8 %collective-permute-done.8.refs_6_ = bf16[8,128,128]{2,1,0:T(8,128)(2,1)S(1)} collective-permute-done((bf16[8,128,128]{2,1,0:T(8,128)(2,1)S(1)}, bf16[8,128,128]{2,1,0:T(8,128)(2,1)S(1)}, u32[]{:S(2)}, u32[]{:S(2)}) %collective-permute-start.8) | collective-permute-done | bytes 262176 | tf_op jit(solution)/shard_map/ppermute | solution.py:30
  30.8 3.4 %collective-permute-start.9 = (bf16[8,128,128]{2,1,0:T(8,128)(2,1)S(1)}, bf16[8,128,128]{2,1,0:T(8,128)(2,1)S(1)}, u32[]{:S(2)}, u32[]{:S(2)}) collective-permute-start(bf16[8,128,128]{2,1,0:T(8,128)(2,1)S(1)} %collective-permute-done.8.refs_6_), channel_id=1, source_target_pairs={{0,28},{4,0},{8,4},{12,8},{16,12},{20,16},{24,20},{28,24},{32,60},... | collective-permute-start | bytes 786440 | tf_op jit(solution)/shard_map/ppermute | solution.py:30
  34.2 2.2 %collective-permute-done.5.refs_7_ = bf16[8,128,128]{2,1,0:T(8,128)(2,1)S(1)} collective-permute-done((bf16[8,128,128]{2,1,0:T(8,128)(2,1)S(1)}, bf16[8,128,128]{2,1,0:T(8,128)(2,1)S(1)}, u32[]{:S(2)}, u32[]{:S(2)}) %collective-permute-start.5) | collective-permute-done | bytes 262176 | tf_op jit(solution)/shard_map/ppermute | solution.py:30
  36.4 3.4 %collective-permute-start.6 = (bf16[8,128,128]{2,1,0:T(8,128)(2,1)S(1)}, bf16[8,128,128]{2,1,0:T(8,128)(2,1)S(1)}, u32[]{:S(2)}, u32[]{:S(2)}) collective-permute-start(bf16[8,128,128]{2,1,0:T(8,128)(2,1)S(1)} %collective-permute-done.5.refs_7_), channel_id=1, source_target_pairs={{0,28},{4,0},{8,4},{12,8},{16,12},{20,16},{24,20},{28,24},{32,60},... | collective-permute-start | bytes 786440 | tf_op jit(solution)/shard_map/ppermute | solution.py:30
  39.8 2.1 %collective-permute-start.19 = (bf16[256,256]{1,0:T(8,128)(2,1)}, bf16[256,256]{1,0:T(8,128)(2,1)S(1)}, u32[]{:S(2)}, u32[]{:S(2)}) collective-permute-start(bf16[256,256]{1,0:T(8,128)(2,1)} %refs_5_.1), channel_id=1, source_target_pairs={{0,2},{1,3},{2,0},{3,1},{4,6},{5,7},{6,4},{7,5},{8,10},{9,11},{10,... | collective-permute-start | bytes 393224 | tf_op jit(solution)/shard_map/ppermute | solution.py:34
  42.0 3.4 %collective-permute-start.10 = (bf16[8,128,128]{2,1,0:T(8,128)(2,1)S(1)}, bf16[8,128,128]{2,1,0:T(8,128)(2,1)S(1)}, u32[]{:S(2)}, u32[]{:S(2)}) collective-permute-start(bf16[8,128,128]{2,1,0:T(8,128)(2,1)S(1)} %collective-permute-done.9.refs_8_), channel_id=1, source_target_pairs={{0,28},{4,0},{8,4},{12,8},{16,12},{20,16},{24,20},{28,24},{32,60},... | collective-permute-start | bytes 786440 | tf_op jit(solution)/shard_map/ppermute | solution.py:30
  45.4 2.2 %collective-permute-done.6.refs_3_ = bf16[8,128,128]{2,1,0:T(8,128)(2,1)S(1)} collective-permute-done((bf16[8,128,128]{2,1,0:T(8,128)(2,1)S(1)}, bf16[8,128,128]{2,1,0:T(8,128)(2,1)S(1)}, u32[]{:S(2)}, u32[]{:S(2)}) %collective-permute-start.6) | collective-permute-done | bytes 262176 | tf_op jit(solution)/shard_map/ppermute | solution.py:30
  47.6 3.4 %collective-permute-start.11 = (bf16[8,128,128]{2,1,0:T(8,128)(2,1)S(1)}, bf16[8,128,128]{2,1,0:T(8,128)(2,1)}, u32[]{:S(2)}, u32[]{:S(2)}) collective-permute-start(bf16[8,128,128]{2,1,0:T(8,128)(2,1)S(1)} %collective-permute-done.6.refs_3_), channel_id=1, source_target_pairs={{0,28},{4,0},{8,4},{12,8},{16,12},{20,16},{24,20},{28,24},{32,60},... | collective-permute-start | bytes 786440 | tf_op jit(solution)/shard_map/ppermute | solution.py:30
  51.7 2.1 %collective-permute-start.20 = (bf16[256,256]{1,0:T(8,128)(2,1)S(1)}, bf16[256,256]{1,0:T(8,128)(2,1)}, u32[]{:S(2)}, u32[]{:S(2)}) collective-permute-start(bf16[256,256]{1,0:T(8,128)(2,1)S(1)} %collective-permute-done.1.refs_6_), channel_id=1, source_target_pairs={{0,2},{1,3},{2,0},{3,1},{4,6},{5,7},{6,4},{7,5},{8,10},{9,11},{10,... | collective-permute-start | bytes 393224 | tf_op jit(solution)/shard_map/ppermute | solution.py:34
  53.8 3.4 %copy-done = bf16[1,1,256,128,128]{4,3,2,1,0:T(8,128)(2,1)S(1)} copy-done((bf16[1,1,256,128,128]{4,3,2,1,0:T(8,128)(2,1)S(1)}, bf16[1,1,256,128,128]{4,3,2,1,0:T(8,128)(2,1)}, u32[]{:S(2)}) %copy-start) | copy-done | bytes 8388632
  57.9 1.6 %forward_near.1.refs_9_ = f32[9,128,128]{2,1,0:T(8,128)S(1)} custom-call(s32[562]{0:T(1024)S(1)} %copy-done.4, s32[1]{0:T(128)} %bitcast.4.refs_1_, bf16[256,128,128]{2,1,0:T(8,128)(2,1)S(1)} %bitcast.14, bf16[8,128,128]{2,1,0:T(8,128)(2,1)S(1)} %pad_maximum_fusion.refs_3_, bf16[8,128,128]{2,1,0:T(8,128)(2,1)S(1)} %constant_dynamic-update-slice_fusion.refs_4_, ...), custom_call_target="tpu_custom_call" | custom-call | flops 671088640 | bytes 5242880 | tf_op jit(solution)/shard_map/forward_near/pallas_call | solution.py:174
  59.6 2.6 %collective-permute-done.15.refs_6_ = bf16[8,128,128]{2,1,0:T(8,128)(2,1)} collective-permute-done((bf16[8,128,128]{2,1,0:T(8,128)(2,1)S(1)}, bf16[8,128,128]{2,1,0:T(8,128)(2,1)}, u32[]{:S(2)}, u32[]{:S(2)}) %collective-permute-start.15) | collective-permute-done | bytes 262176 | tf_op jit(solution)/shard_map/ppermute | solution.py:30
  62.2 2.1 %forward_far.1 = (bf16[4,128,128]{2,1,0:T(8,128)(2,1)S(1)}, bf16[4,128,128]{2,1,0:T(8,128)(2,1)S(1)}) custom-call(s32[562]{0:T(1024)S(1)} %copy-done.4, s32[1]{0:T(128)} %bitcast.4.refs_1_, bf16[256,128,128]{2,1,0:T(8,128)(2,1)S(1)} %bitcast.15, bf16[8,128,128]{2,1,0:T(8,128)(2,1)S(1)} %collective-permute-done.6.refs_3_, ...), custom_call_target="tpu_custom_call" | custom-call | flops 402653184 | bytes 3145728 | tf_op jit(solution)/shard_map/forward_far/pallas_call | solution.py:174
  64.4 6.5 %collective-permute-start.21 = (bf16[4,128,128]{2,1,0:T(8,128)(2,1)S(1)}, bf16[4,128,128]{2,1,0:T(8,128)(2,1)S(1)}, u32[]{:S(2)}, u32[]{:S(2)}) collective-permute-start(bf16[4,128,128]{2,1,0:T(8,128)(2,1)S(1)} %get-tuple-element.70), channel_id=1, source_target_pairs={{0,1},{1,0},{2,3},{3,2},{4,5},{5,4},{6,7},{7,6},{8,9},{9,8},{10,11... | collective-permute-start | bytes 393224 | tf_op jit(solution)/shard_map/ppermute | solution.py:34
  71.9 3.1 %collective-permute-start.22 = (bf16[4,128,128]{2,1,0:T(8,128)(2,1)S(1)}, bf16[4,128,128]{2,1,0:T(8,128)(2,1)S(1)}, u32[]{:S(2)}, u32[]{:S(2)}) collective-permute-start(bf16[4,128,128]{2,1,0:T(8,128)(2,1)S(1)} %add_convert_fusion.4), channel_id=1, source_target_pairs={{0,2},{1,3},{2,0},{3,1},{4,6},{5,7},{6,4},{7,5},{8,10},{9,11},{10,... | collective-permute-start | bytes 393224 | tf_op jit(solution)/shard_map/ppermute | solution.py:34
  75.0 3.4 %collective-permute-done.22 = bf16[4,128,128]{2,1,0:T(8,128)(2,1)S(1)} collective-permute-done((bf16[4,128,128]{2,1,0:T(8,128)(2,1)S(1)}, bf16[4,128,128]{2,1,0:T(8,128)(2,1)S(1)}, u32[]{:S(2)}, u32[]{:S(2)}) %collective-permute-start.22) | collective-permute-done | bytes 131104 | tf_op jit(solution)/shard_map/ppermute | solution.py:34
  80.6 3.0 %dense_and_backward_far.1 = (bf16[256,256]{1,0:T(8,128)(2,1)}, bf16[1,128,128]{2,1,0:T(8,128)(2,1)S(1)}, bf16[9,128,128]{2,1,0:T(8,128)(2,1)S(1)}, bf16[8,128,12...) custom-call(s32[562]{0:T(1024)S(1)} %copy-done.4, ...), custom_call_target="tpu_custom_call" | custom-call | flops 402653184 | bytes 4718592 | tf_op jit(solution)/shard_map/dense_and_backward_far/pallas_call | solution.py:271
  84.3 3.1 %collective-permute-start.26 = (bf16[8,128,128]{2,1,0:T(8,128)(2,1)S(1)}, bf16[8,128,128]{2,1,0:T(8,128)(2,1)S(1)}, u32[]{:S(2)}, u32[]{:S(2)}) collective-permute-start(bf16[8,128,128]{2,1,0:T(8,128)(2,1)S(1)} %get-tuple-element.91), channel_id=1, source_target_pairs={{0,28},{4,0},{8,4},{12,8},{16,12},{20,16},{24,20},{28,24},{32,60},... | collective-permute-start | bytes 786440 | tf_op jit(solution)/shard_map/ppermute | solution.py:30
  87.4 1.5 collective-permute-start.31
  88.9 1.8 %backward_near.1 = (bf16[8,128,128]{2,1,0:T(8,128)(2,1)S(1)}, bf16[8,128,128]{2,1,0:T(8,128)(2,1)S(1)}, bf16[8,128,128]{2,1,0:T(8,128)(2,1)S(1)}, bf16[9,128,128...) custom-call(s32[562]{0:T(1024)S(1)} %copy-done.4, ...), custom_call_target="tpu_custom_call" | custom-call | flops 671088640 | bytes 7864320 | tf_op jit(solution)/shard_map/backward_near/pallas_call | solution.py:315
  90.7 3.5 %collective-permute-done.24 = bf16[8,128,128]{2,1,0:T(8,128)(2,1)S(1)} collective-permute-done((bf16[8,128,128]{2,1,0:T(8,128)(2,1)S(1)}, bf16[8,128,128]{2,1,0:T(8,128)(2,1)S(1)}, u32[]{:S(2)}, u32[]{:S(2)}) %collective-permute-start.24) | collective-permute-done | bytes 262176 | tf_op jit(solution)/shard_map/ppermute | solution.py:30
  94.4 5.1 %collective-permute-done.31 = bf16[9,128,128]{2,1,0:T(8,128)(2,1)S(1)} collective-permute-done((bf16[9,128,128]{2,1,0:T(8,128)(2,1)S(1)}, bf16[9,128,128]{2,1,0:T(8,128)(2,1)S(1)}, u32[]{:S(2)}, u32[]{:S(2)}) %collective-permute-start.31) | collective-permute-done | bytes 294944 | tf_op jit(solution)/shard_map/ppermute | solution.py:30
  99.6 3.7 %collective-permute-start.32 = (bf16[9,128,128]{2,1,0:T(8,128)(2,1)S(1)}, bf16[9,128,128]{2,1,0:T(8,128)(2,1)S(1)}, u32[]{:S(2)}, u32[]{:S(2)}) collective-permute-start(bf16[9,128,128]{2,1,0:T(8,128)(2,1)S(1)} %add_convert_fusion), channel_id=1, source_target_pairs={{0,28},{4,0},{8,4},{12,8},{16,12},{20,16},{24,20},{28,24},{32,60},... | collective-permute-start | bytes 884744 | tf_op jit(solution)/shard_map/ppermute | solution.py:30
  103.3 2.8 %collective-permute-done.25.b_ref = bf16[8,128,128]{2,1,0:T(8,128)(2,1)S(1)} collective-permute-done((bf16[8,128,128]{2,1,0:T(8,128)(2,1)S(1)}, bf16[8,128,128]{2,1,0:T(8,128)(2,1)S(1)}, u32[]{:S(2)}, u32[]{:S(2)}) %collective-permute-start.25) | collective-permute-done | bytes 262176 | tf_op jit(solution)/shard_map/ppermute | solution.py:30
  106.4 2.7 %collective-permute-start.28 = (bf16[8,128,128]{2,1,0:T(8,128)(2,1)S(1)}, bf16[8,128,128]{2,1,0:T(8,128)(2,1)S(1)}, u32[]{:S(2)}, u32[]{:S(2)}) collective-permute-start(bf16[8,128,128]{2,1,0:T(8,128)(2,1)S(1)} %get-tuple-element.96), channel_id=1, source_target_pairs={{0,28},{4,0},{8,4},{12,8},{16,12},{20,16},{24,20},{28,24},{32,60},... | collective-permute-start | bytes 786440 | tf_op jit(solution)/shard_map/ppermute | solution.py:30
  109.2 3.4 %collective-permute-start.34 = (bf16[9,128,128]{2,1,0:T(8,128)(2,1)S(1)}, bf16[9,128,128]{2,1,0:T(8,128)(2,1)S(1)}, u32[]{:S(2)}, u32[]{:S(2)}) collective-permute-start(bf16[9,128,128]{2,1,0:T(8,128)(2,1)S(1)} %get-tuple-element.113), channel_id=1, source_target_pairs={{0,28},{4,0},{8,4},{12,8},{16,12},{20,16},{24,20},{28,24},{32,60},... | collective-permute-start | bytes 884744 | tf_op jit(solution)/shard_map/ppermute | solution.py:30
  112.6 2.4 %collective-permute-done.27.b_ref = bf16[8,128,128]{2,1,0:T(8,128)(2,1)S(1)} collective-permute-done((bf16[8,128,128]{2,1,0:T(8,128)(2,1)S(1)}, bf16[8,128,128]{2,1,0:T(8,128)(2,1)S(1)}, u32[]{:S(2)}, u32[]{:S(2)}) %collective-permute-start.27) | collective-permute-done | bytes 262176 | tf_op jit(solution)/shard_map/ppermute | solution.py:30
  115.4 3.5 %collective-permute-start.30 = (bf16[8,128,128]{2,1,0:T(8,128)(2,1)S(1)}, bf16[8,128,128]{2,1,0:T(8,128)(2,1)S(1)}, u32[]{:S(2)}, u32[]{:S(2)}) collective-permute-start(bf16[8,128,128]{2,1,0:T(8,128)(2,1)S(1)} %get-tuple-element.101), channel_id=1, source_target_pairs={{0,28},{4,0},{8,4},{12,8},{16,12},{20,16},{24,20},{28,24},{32,60},... | collective-permute-start | bytes 786440 | tf_op jit(solution)/shard_map/ppermute | solution.py:30
  118.8 2.6 %collective-permute-done.34.b_ref = bf16[9,128,128]{2,1,0:T(8,128)(2,1)S(1)} collective-permute-done((bf16[9,128,128]{2,1,0:T(8,128)(2,1)S(1)}, bf16[9,128,128]{2,1,0:T(8,128)(2,1)S(1)}, u32[]{:S(2)}, u32[]{:S(2)}) %collective-permute-start.34) | collective-permute-done | bytes 294944 | tf_op jit(solution)/shard_map/ppermute | solution.py:30
  121.6 3.5 %collective-permute-start.36 = (bf16[9,128,128]{2,1,0:T(8,128)(2,1)S(1)}, bf16[9,128,128]{2,1,0:T(8,128)(2,1)S(1)}, u32[]{:S(2)}, u32[]{:S(2)}) collective-permute-start(bf16[9,128,128]{2,1,0:T(8,128)(2,1)S(1)} %get-tuple-element.118), channel_id=1, source_target_pairs={{0,28},{4,0},{8,4},{12,8},{16,12},{20,16},{24,20},{28,24},{32,60},... | collective-permute-start | bytes 884744 | tf_op jit(solution)/shard_map/ppermute | solution.py:30
  125.6 1.5 collective-permute-done.30
  127.2 6.2 %collective-permute-done.36 = bf16[9,128,128]{2,1,0:T(8,128)(2,1)S(1)} collective-permute-done((bf16[9,128,128]{2,1,0:T(8,128)(2,1)S(1)}, bf16[9,128,128]{2,1,0:T(8,128)(2,1)S(1)}, u32[]{:S(2)}, u32[]{:S(2)}) %collective-permute-start.36) | collective-permute-done | bytes 294944 | tf_op jit(solution)/shard_map/ppermute | solution.py:30
  133.8 1.4 collective-permute-start.38
  135.2 2.7 %collective-permute-done.40 = bf16[5,128,128]{2,1,0:T(8,128)(2,1)S(1)} collective-permute-done((bf16[5,128,128]{2,1,0:T(8,128)(2,1)S(1)}, bf16[5,128,128]{2,1,0:T(8,128)(2,1)S(1)}, u32[]{:S(2)}, u32[]{:S(2)}) %collective-permute-start.40) | collective-permute-done | bytes 163872 | tf_op jit(solution)/shard_map/ppermute | solution.py:30
  137.9 1.7 %collective-permute-done.39 = bf16[5,128,128]{2,1,0:T(8,128)(2,1)S(1)} collective-permute-done((bf16[5,128,128]{2,1,0:T(8,128)(2,1)S(1)}, bf16[5,128,128]{2,1,0:T(8,128)(2,1)S(1)}, u32[]{:S(2)}, u32[]{:S(2)}) %collective-permute-start.39) | collective-permute-done | bytes 163872 | tf_op jit(solution)/shard_map/ppermute | solution.py:30
  139.6 2.7 %collective-permute-done.38 = bf16[5,128,128]{2,1,0:T(8,128)(2,1)S(1)} collective-permute-done((bf16[5,128,128]{2,1,0:T(8,128)(2,1)S(1)}, bf16[5,128,128]{2,1,0:T(8,128)(2,1)S(1)}, u32[]{:S(2)}, u32[]{:S(2)}) %collective-permute-start.38) | collective-permute-done | bytes 163872 | tf_op jit(solution)/shard_map/ppermute | solution.py:30
  142.5 3.4 %collective-permute-done.41 = bf16[3,128,128]{2,1,0:T(8,128)(2,1)S(1)} collective-permute-done((bf16[3,128,128]{2,1,0:T(8,128)(2,1)S(1)}, bf16[3,128,128]{2,1,0:T(8,128)(2,1)S(1)}, u32[]{:S(2)}, u32[]{:S(2)}) %collective-permute-start.41) | collective-permute-done | bytes 98336 | tf_op jit(solution)/shard_map/ppermute | solution.py:30
  146.0 4.6 %collective-permute-start.42 = (f32[64,256]{1,0:T(8,128)S(1)}, f32[64,256]{1,0:T(8,128)S(1)}, u32[]{:S(2)}, u32[]{:S(2)}) collective-permute-start(f32[64,256]{1,0:T(8,128)S(1)} %pad_maximum_fusion.6), channel_id=1, source_target_pairs={{0,1},{1,0},{2,3},{3,2},{4,5},{5,4},{6,7},{7,6},{8,9},{9,8},{10,11... | collective-permute-start | bytes 196616 | tf_op jit(solution)/shard_map/ppermute | solution.py:34
  (90 shorter events, 12.4 us)
Async XLA Ops:
  0.6 4.8 %collective-permute-start = (bf16[2,128,128]{2,1,0:T(8,128)(2,1)}, bf16[2,128,128]{2,1,0:T(8,128)(2,1)S(1)}, u32[]{:S(2)}, u32[]{:S(2)}) collective-permute-start(bf16[2,128,128]{2,1,0:T(8,128)(2,1)} %bitcast.20), channel_id=1, source_target_pairs={{0,128},{4,132},{8,136},{12,140},{16,144},{20,148},{24,152},{28,15... | collective-permute-start | bytes 196616 | tf_op jit(solution)/shard_map/ppermute | solution.py:30
  2.8 2.7 %collective-permute-start.1 = (bf16[256,256]{1,0:T(8,128)(2,1)}, bf16[256,256]{1,0:T(8,128)(2,1)S(1)}, u32[]{:S(2)}, u32[]{:S(2)}) collective-permute-start(bf16[256,256]{1,0:T(8,128)(2,1)} %refs_5_.1), channel_id=1, source_target_pairs={{0,1},{1,0},{2,3},{3,2},{4,5},{5,4},{6,7},{7,6},{8,9},{9,8},{10,11... | collective-permute-start | bytes 393224 | tf_op jit(solution)/shard_map/ppermute | solution.py:34
  6.3 7.9 %collective-permute-start.2 = (bf16[4,128,128]{2,1,0:T(8,128)(2,1)S(1)}, bf16[4,128,128]{2,1,0:T(8,128)(2,1)S(1)}, u32[]{:S(2)}, u32[]{:S(2)}) collective-permute-start(bf16[4,128,128]{2,1,0:T(8,128)(2,1)S(1)} %pad_maximum_fusion.4), channel_id=1, source_target_pairs={{0,96},{4,100},{8,104},{12,108},{16,112},{20,116},{24,120},{28,124... | collective-permute-start | bytes 393224 | tf_op jit(solution)/shard_map/ppermute | solution.py:30
  8.8 7.1 %collective-permute-start.3 = (bf16[4,128,128]{2,1,0:T(8,128)(2,1)S(1)}, bf16[4,128,128]{2,1,0:T(8,128)(2,1)S(1)}, u32[]{:S(2)}, u32[]{:S(2)}) collective-permute-start(bf16[4,128,128]{2,1,0:T(8,128)(2,1)S(1)} %pad_maximum_fusion.4), channel_id=1, source_target_pairs={{0,32},{4,36},{8,40},{12,44},{16,48},{20,52},{24,56},{28,60},{32,6... | collective-permute-start | bytes 393224 | tf_op jit(solution)/shard_map/ppermute | solution.py:30
  8.8 13.6 %collective-permute-start.7 = (bf16[4,128,128]{2,1,0:T(8,128)(2,1)S(1)}, bf16[4,128,128]{2,1,0:T(8,128)(2,1)S(1)}, u32[]{:S(2)}, u32[]{:S(2)}) collective-permute-start(bf16[4,128,128]{2,1,0:T(8,128)(2,1)S(1)} %pad_maximum_fusion.4), channel_id=1, source_target_pairs={{0,64},{4,68},{8,72},{12,76},{16,80},{20,84},{24,88},{28,92},{32,9... | collective-permute-start | bytes 393224 | tf_op jit(solution)/shard_map/ppermute | solution.py:30
  16.7 9.0 %collective-permute-start.4 = (bf16[8,128,128]{2,1,0:T(8,128)(2,1)S(1)}, bf16[8,128,128]{2,1,0:T(8,128)(2,1)S(1)}, u32[]{:S(2)}, u32[]{:S(2)}) collective-permute-start(bf16[8,128,128]{2,1,0:T(8,128)(2,1)S(1)} %pad_maximum_fusion.refs_3_), channel_id=1, source_target_pairs={{0,28},{4,0},{8,4},{12,8},{16,12},{20,16},{24,20},{28,24},{32,60},... | collective-permute-start | bytes 786440 | tf_op jit(solution)/shard_map/ppermute | solution.py:30
  22.4 6.5 %collective-permute-start.12 = (bf16[8,128,128]{2,1,0:T(8,128)(2,1)S(1)}, bf16[8,128,128]{2,1,0:T(8,128)(2,1)S(1)}, u32[]{:S(2)}, u32[]{:S(2)}) collective-permute-start(bf16[8,128,128]{2,1,0:T(8,128)(2,1)S(1)} %constant_dynamic-update-slice_fusion.refs_4_), channel_id=1, source_target_pairs={{0,4},{4,8},{8,12},{12,16},{16,20},{20,24},{24,28},{28,0},{32,36},... | collective-permute-start | bytes 786440 | tf_op jit(solution)/shard_map/ppermute | solution.py:30
  22.5 8.3 %collective-permute-start.8 = (bf16[8,128,128]{2,1,0:T(8,128)(2,1)S(1)}, bf16[8,128,128]{2,1,0:T(8,128)(2,1)S(1)}, u32[]{:S(2)}, u32[]{:S(2)}) collective-permute-start(bf16[8,128,128]{2,1,0:T(8,128)(2,1)S(1)} %constant_dynamic-update-slice_fusion.refs_4_), channel_id=1, source_target_pairs={{0,28},{4,0},{8,4},{12,8},{16,12},{20,16},{24,20},{28,24},{32,60},... | collective-permute-start | bytes 786440 | tf_op jit(solution)/shard_map/ppermute | solution.py:30
  25.2 9.0 %collective-permute-start.16 = (bf16[8,128,128]{2,1,0:T(8,128)(2,1)S(1)}, bf16[8,128,128]{2,1,0:T(8,128)(2,1)S(1)}, u32[]{:S(2)}, u32[]{:S(2)}) collective-permute-start(bf16[8,128,128]{2,1,0:T(8,128)(2,1)S(1)} %pad_maximum_fusion.refs_3_), channel_id=1, source_target_pairs={{0,4},{4,8},{8,12},{12,16},{16,20},{20,24},{24,28},{28,0},{32,36},... | collective-permute-start | bytes 786440 | tf_op jit(solution)/shard_map/ppermute | solution.py:30
  25.7 10.7 %collective-permute-start.5 = (bf16[8,128,128]{2,1,0:T(8,128)(2,1)S(1)}, bf16[8,128,128]{2,1,0:T(8,128)(2,1)S(1)}, u32[]{:S(2)}, u32[]{:S(2)}) collective-permute-start(bf16[8,128,128]{2,1,0:T(8,128)(2,1)S(1)} %collective-permute-done.4.refs_5_), channel_id=1, source_target_pairs={{0,28},{4,0},{8,4},{12,8},{16,12},{20,16},{24,20},{28,24},{32,60},... | collective-permute-start | bytes 786440 | tf_op jit(solution)/shard_map/ppermute | solution.py:30
  28.9 10.9 %collective-permute-start.13 = (bf16[8,128,128]{2,1,0:T(8,128)(2,1)S(1)}, bf16[8,128,128]{2,1,0:T(8,128)(2,1)S(1)}, u32[]{:S(2)}, u32[]{:S(2)}) collective-permute-start(bf16[8,128,128]{2,1,0:T(8,128)(2,1)S(1)} %collective-permute-done.12.refs_12_), channel_id=1, source_target_pairs={{0,4},{4,8},{8,12},{12,16},{16,20},{20,24},{24,28},{28,0},{32,36},... | collective-permute-start | bytes 786440 | tf_op jit(solution)/shard_map/ppermute | solution.py:30
  30.8 11.2 %collective-permute-start.9 = (bf16[8,128,128]{2,1,0:T(8,128)(2,1)S(1)}, bf16[8,128,128]{2,1,0:T(8,128)(2,1)S(1)}, u32[]{:S(2)}, u32[]{:S(2)}) collective-permute-start(bf16[8,128,128]{2,1,0:T(8,128)(2,1)S(1)} %collective-permute-done.8.refs_6_), channel_id=1, source_target_pairs={{0,28},{4,0},{8,4},{12,8},{16,12},{20,16},{24,20},{28,24},{32,60},... | collective-permute-start | bytes 786440 | tf_op jit(solution)/shard_map/ppermute | solution.py:30
  34.2 11.2 %collective-permute-start.17 = (bf16[8,128,128]{2,1,0:T(8,128)(2,1)S(1)}, bf16[8,128,128]{2,1,0:T(8,128)(2,1)S(1)}, u32[]{:S(2)}, u32[]{:S(2)}) collective-permute-start(bf16[8,128,128]{2,1,0:T(8,128)(2,1)S(1)} %collective-permute-done.16.refs_11_), channel_id=1, source_target_pairs={{0,4},{4,8},{8,12},{12,16},{16,20},{20,24},{24,28},{28,0},{32,36},... | collective-permute-start | bytes 786440 | tf_op jit(solution)/shard_map/ppermute | solution.py:30
  36.4 11.2 %collective-permute-start.6 = (bf16[8,128,128]{2,1,0:T(8,128)(2,1)S(1)}, bf16[8,128,128]{2,1,0:T(8,128)(2,1)S(1)}, u32[]{:S(2)}, u32[]{:S(2)}) collective-permute-start(bf16[8,128,128]{2,1,0:T(8,128)(2,1)S(1)} %collective-permute-done.5.refs_7_), channel_id=1, source_target_pairs={{0,28},{4,0},{8,4},{12,8},{16,12},{20,16},{24,20},{28,24},{32,60},... | collective-permute-start | bytes 786440 | tf_op jit(solution)/shard_map/ppermute | solution.py:30
  39.8 11.2 %collective-permute-start.14 = (bf16[8,128,128]{2,1,0:T(8,128)(2,1)S(1)}, bf16[8,128,128]{2,1,0:T(8,128)(2,1)S(1)}, u32[]{:S(2)}, u32[]{:S(2)}) collective-permute-start(bf16[8,128,128]{2,1,0:T(8,128)(2,1)S(1)} %collective-permute-done.13.refs_10_), channel_id=1, source_target_pairs={{0,4},{4,8},{8,12},{12,16},{16,20},{20,24},{24,28},{28,0},{32,36},... | collective-permute-start | bytes 786440 | tf_op jit(solution)/shard_map/ppermute | solution.py:30
  39.8 11.2 %collective-permute-start.19 = (bf16[256,256]{1,0:T(8,128)(2,1)}, bf16[256,256]{1,0:T(8,128)(2,1)S(1)}, u32[]{:S(2)}, u32[]{:S(2)}) collective-permute-start(bf16[256,256]{1,0:T(8,128)(2,1)} %refs_5_.1), channel_id=1, source_target_pairs={{0,2},{1,3},{2,0},{3,1},{4,6},{5,7},{6,4},{7,5},{8,10},{9,11},{10,... | collective-permute-start | bytes 393224 | tf_op jit(solution)/shard_map/ppermute | solution.py:34
  42.0 17.6 %collective-permute-start.10 = (bf16[8,128,128]{2,1,0:T(8,128)(2,1)S(1)}, bf16[8,128,128]{2,1,0:T(8,128)(2,1)S(1)}, u32[]{:S(2)}, u32[]{:S(2)}) collective-permute-start(bf16[8,128,128]{2,1,0:T(8,128)(2,1)S(1)} %collective-permute-done.9.refs_8_), channel_id=1, source_target_pairs={{0,28},{4,0},{8,4},{12,8},{16,12},{20,16},{24,20},{28,24},{32,60},... | collective-permute-start | bytes 786440 | tf_op jit(solution)/shard_map/ppermute | solution.py:30
  45.4 14.1 %collective-permute-start.18 = (bf16[8,128,128]{2,1,0:T(8,128)(2,1)S(1)}, bf16[8,128,128]{2,1,0:T(8,128)(2,1)}, u32[]{:S(2)}, u32[]{:S(2)}) collective-permute-start(bf16[8,128,128]{2,1,0:T(8,128)(2,1)S(1)} %collective-permute-done.17.refs_9_), channel_id=1, source_target_pairs={{0,4},{4,8},{8,12},{12,16},{16,20},{20,24},{24,28},{28,0},{32,36},... | collective-permute-start | bytes 786440 | tf_op jit(solution)/shard_map/ppermute | solution.py:30
  47.6 12.0 %collective-permute-start.11 = (bf16[8,128,128]{2,1,0:T(8,128)(2,1)S(1)}, bf16[8,128,128]{2,1,0:T(8,128)(2,1)}, u32[]{:S(2)}, u32[]{:S(2)}) collective-permute-start(bf16[8,128,128]{2,1,0:T(8,128)(2,1)S(1)} %collective-permute-done.6.refs_3_), channel_id=1, source_target_pairs={{0,28},{4,0},{8,4},{12,8},{16,12},{20,16},{24,20},{28,24},{32,60},... | collective-permute-start | bytes 786440 | tf_op jit(solution)/shard_map/ppermute | solution.py:30
  51.1 11.2 %collective-permute-start.15 = (bf16[8,128,128]{2,1,0:T(8,128)(2,1)S(1)}, bf16[8,128,128]{2,1,0:T(8,128)(2,1)}, u32[]{:S(2)}, u32[]{:S(2)}) collective-permute-start(bf16[8,128,128]{2,1,0:T(8,128)(2,1)S(1)} %collective-permute-done.14.refs_8_), channel_id=1, source_target_pairs={{0,4},{4,8},{8,12},{12,16},{16,20},{20,24},{24,28},{28,0},{32,36},... | collective-permute-start | bytes 786440 | tf_op jit(solution)/shard_map/ppermute | solution.py:30
  51.7 7.8 %collective-permute-start.20 = (bf16[256,256]{1,0:T(8,128)(2,1)S(1)}, bf16[256,256]{1,0:T(8,128)(2,1)}, u32[]{:S(2)}, u32[]{:S(2)}) collective-permute-start(bf16[256,256]{1,0:T(8,128)(2,1)S(1)} %collective-permute-done.1.refs_6_), channel_id=1, source_target_pairs={{0,2},{1,3},{2,0},{3,1},{4,6},{5,7},{6,4},{7,5},{8,10},{9,11},{10,... | collective-permute-start | bytes 393224 | tf_op jit(solution)/shard_map/ppermute | solution.py:34
  57.9 30.9 %slice-start = ((s8[8388608]{0:T(1024)(128)(4,1)}), s8[4194304]{0:T(1024)(128)(4,1)S(1)}, s32[]{:S(2)}) async-start(s8[8388608]{0:T(1024)(128)(4,1)} %bitcast.17), calls=%async_computation | async-start | bytes 8388608
  59.5 21.1 %copy-start.1 = (bf16[256,256]{1,0:T(8,128)(2,1)S(1)}, bf16[256,256]{1,0:T(8,128)(2,1)}, u32[]{:S(2)}) copy-start(bf16[256,256]{1,0:T(8,128)(2,1)} %refs_5_.1) | copy-start | bytes 393220
  59.5 21.1 %copy-start.3 = (bf16[256,256]{1,0:T(8,128)(2,1)S(1)}, bf16[256,256]{1,0:T(8,128)(2,1)}, u32[]{:S(2)}) copy-start(bf16[256,256]{1,0:T(8,128)(2,1)} %copy-done.2) | copy-start | bytes 393220
  59.5 21.1 %copy-start.5 = (bf16[128,256]{1,0:T(8,128)(2,1)S(1)}, bf16[128,256]{1,0:T(8,128)(2,1)}, u32[]{:S(2)}) copy-start(bf16[128,256]{1,0:T(8,128)(2,1)} %refs_9_.1) | copy-start | bytes 196612
  59.5 29.3 %slice-start.1 = ((s8[8388608]{0:T(1024)(128)(4,1)}), s8[4194304]{0:T(1024)(128)(4,1)S(1)}, s32[]{:S(2)}) async-start(s8[8388608]{0:T(1024)(128)(4,1)} %bitcast.17), calls=%async_computation.1 | async-start | bytes 8388608
  64.4 7.5 %collective-permute-start.21 = (bf16[4,128,128]{2,1,0:T(8,128)(2,1)S(1)}, bf16[4,128,128]{2,1,0:T(8,128)(2,1)S(1)}, u32[]{:S(2)}, u32[]{:S(2)}) collective-permute-start(bf16[4,128,128]{2,1,0:T(8,128)(2,1)S(1)} %get-tuple-element.70), channel_id=1, source_target_pairs={{0,1},{1,0},{2,3},{3,2},{4,5},{5,4},{6,7},{7,6},{8,9},{9,8},{10,11... | collective-permute-start | bytes 393224 | tf_op jit(solution)/shard_map/ppermute | solution.py:34
  71.9 6.5 %collective-permute-start.22 = (bf16[4,128,128]{2,1,0:T(8,128)(2,1)S(1)}, bf16[4,128,128]{2,1,0:T(8,128)(2,1)S(1)}, u32[]{:S(2)}, u32[]{:S(2)}) collective-permute-start(bf16[4,128,128]{2,1,0:T(8,128)(2,1)S(1)} %add_convert_fusion.4), channel_id=1, source_target_pairs={{0,2},{1,3},{2,0},{3,1},{4,6},{5,7},{6,4},{7,5},{8,10},{9,11},{10,... | collective-permute-start | bytes 393224 | tf_op jit(solution)/shard_map/ppermute | solution.py:34
  78.4 2.2 %collective-permute-start.23 = (bf16[4,128,128]{2,1,0:T(8,128)(2,1)S(1)}, bf16[4,128,128]{2,1,0:T(8,128)(2,1)S(1)}, u32[]{:S(2)}, u32[]{:S(2)}) collective-permute-start(bf16[4,128,128]{2,1,0:T(8,128)(2,1)S(1)} %add_convert_fusion.3.refs_3_), channel_id=1, source_target_pairs={{0,1},{1,0},{2,3},{3,2},{4,5},{5,4},{6,7},{7,6},{8,9},{9,8},{10,11... | collective-permute-start | bytes 393224 | tf_op jit(solution)/shard_map/ppermute | solution.py:34
  83.6 10.6 %collective-permute-start.24 = (bf16[8,128,128]{2,1,0:T(8,128)(2,1)S(1)}, bf16[8,128,128]{2,1,0:T(8,128)(2,1)S(1)}, u32[]{:S(2)}, u32[]{:S(2)}) collective-permute-start(bf16[8,128,128]{2,1,0:T(8,128)(2,1)S(1)} %get-tuple-element.74), channel_id=1, source_target_pairs={{0,4},{4,8},{8,12},{12,16},{16,20},{20,24},{24,28},{28,0},{32,36},... | collective-permute-start | bytes 786440 | tf_op jit(solution)/shard_map/ppermute | solution.py:30
  84.3 19.0 %collective-permute-start.26 = (bf16[8,128,128]{2,1,0:T(8,128)(2,1)S(1)}, bf16[8,128,128]{2,1,0:T(8,128)(2,1)S(1)}, u32[]{:S(2)}, u32[]{:S(2)}) collective-permute-start(bf16[8,128,128]{2,1,0:T(8,128)(2,1)S(1)} %get-tuple-element.91), channel_id=1, source_target_pairs={{0,28},{4,0},{8,4},{12,8},{16,12},{20,16},{24,20},{28,24},{32,60},... | collective-permute-start | bytes 786440 | tf_op jit(solution)/shard_map/ppermute | solution.py:30
  87.4 12.1 %collective-permute-start.31 = (bf16[9,128,128]{2,1,0:T(8,128)(2,1)S(1)}, bf16[9,128,128]{2,1,0:T(8,128)(2,1)S(1)}, u32[]{:S(2)}, u32[]{:S(2)}) collective-permute-start(bf16[9,128,128]{2,1,0:T(8,128)(2,1)S(1)} %get-tuple-element.108), channel_id=1, source_target_pairs={{0,28},{4,0},{8,4},{12,8},{16,12},{20,16},{24,20},{28,24},{32,60},... | collective-permute-start | bytes 884744 | tf_op jit(solution)/shard_map/ppermute | solution.py:30
  88.9 20.2 %collective-permute-start.33 = (bf16[9,128,128]{2,1,0:T(8,128)(2,1)S(1)}, bf16[9,128,128]{2,1,0:T(8,128)(2,1)S(1)}, u32[]{:S(2)}, u32[]{:S(2)}) collective-permute-start(bf16[9,128,128]{2,1,0:T(8,128)(2,1)S(1)} %get-tuple-element.109), channel_id=1, source_target_pairs={{0,4},{4,8},{8,12},{12,16},{16,20},{20,24},{24,28},{28,0},{32,36},... | collective-permute-start | bytes 884744 | tf_op jit(solution)/shard_map/ppermute | solution.py:30
  94.3 11.9 %collective-permute-start.25 = (bf16[8,128,128]{2,1,0:T(8,128)(2,1)S(1)}, bf16[8,128,128]{2,1,0:T(8,128)(2,1)S(1)}, u32[]{:S(2)}, u32[]{:S(2)}) collective-permute-start(bf16[8,128,128]{2,1,0:T(8,128)(2,1)S(1)} %add_convert_fusion.2), channel_id=1, source_target_pairs={{0,4},{4,8},{8,12},{12,16},{16,20},{20,24},{24,28},{28,0},{32,36},... | collective-permute-start | bytes 786440 | tf_op jit(solution)/shard_map/ppermute | solution.py:30
  99.6 9.4 %collective-permute-start.32 = (bf16[9,128,128]{2,1,0:T(8,128)(2,1)S(1)}, bf16[9,128,128]{2,1,0:T(8,128)(2,1)S(1)}, u32[]{:S(2)}, u32[]{:S(2)}) collective-permute-start(bf16[9,128,128]{2,1,0:T(8,128)(2,1)S(1)} %add_convert_fusion), channel_id=1, source_target_pairs={{0,28},{4,0},{8,4},{12,8},{16,12},{20,16},{24,20},{28,24},{32,60},... | collective-permute-start | bytes 884744 | tf_op jit(solution)/shard_map/ppermute | solution.py:30
  106.3 8.7 %collective-permute-start.27 = (bf16[8,128,128]{2,1,0:T(8,128)(2,1)S(1)}, bf16[8,128,128]{2,1,0:T(8,128)(2,1)S(1)}, u32[]{:S(2)}, u32[]{:S(2)}) collective-permute-start(bf16[8,128,128]{2,1,0:T(8,128)(2,1)S(1)} %get-tuple-element.95), channel_id=1, source_target_pairs={{0,4},{4,8},{8,12},{12,16},{16,20},{20,24},{24,28},{28,0},{32,36},... | collective-permute-start | bytes 786440 | tf_op jit(solution)/shard_map/ppermute | solution.py:30
  106.4 8.8 %collective-permute-start.28 = (bf16[8,128,128]{2,1,0:T(8,128)(2,1)S(1)}, bf16[8,128,128]{2,1,0:T(8,128)(2,1)S(1)}, u32[]{:S(2)}, u32[]{:S(2)}) collective-permute-start(bf16[8,128,128]{2,1,0:T(8,128)(2,1)S(1)} %get-tuple-element.96), channel_id=1, source_target_pairs={{0,28},{4,0},{8,4},{12,8},{16,12},{20,16},{24,20},{28,24},{32,60},... | collective-permute-start | bytes 786440 | tf_op jit(solution)/shard_map/ppermute | solution.py:30
  109.2 12.3 %collective-permute-start.34 = (bf16[9,128,128]{2,1,0:T(8,128)(2,1)S(1)}, bf16[9,128,128]{2,1,0:T(8,128)(2,1)S(1)}, u32[]{:S(2)}, u32[]{:S(2)}) collective-permute-start(bf16[9,128,128]{2,1,0:T(8,128)(2,1)S(1)} %get-tuple-element.113), channel_id=1, source_target_pairs={{0,28},{4,0},{8,4},{12,8},{16,12},{20,16},{24,20},{28,24},{32,60},... | collective-permute-start | bytes 884744 | tf_op jit(solution)/shard_map/ppermute | solution.py:30
  112.5 8.9 %collective-permute-start.35 = (bf16[9,128,128]{2,1,0:T(8,128)(2,1)S(1)}, bf16[9,128,128]{2,1,0:T(8,128)(2,1)S(1)}, u32[]{:S(2)}, u32[]{:S(2)}) collective-permute-start(bf16[9,128,128]{2,1,0:T(8,128)(2,1)S(1)} %get-tuple-element.114), channel_id=1, source_target_pairs={{0,4},{4,8},{8,12},{12,16},{16,20},{20,24},{24,28},{28,0},{32,36},... | collective-permute-start | bytes 884744 | tf_op jit(solution)/shard_map/ppermute | solution.py:30
  115.3 10.3 %collective-permute-start.29 = (bf16[8,128,128]{2,1,0:T(8,128)(2,1)S(1)}, bf16[8,128,128]{2,1,0:T(8,128)(2,1)S(1)}, u32[]{:S(2)}, u32[]{:S(2)}) collective-permute-start(bf16[8,128,128]{2,1,0:T(8,128)(2,1)S(1)} %get-tuple-element.100), channel_id=1, source_target_pairs={{0,4},{4,8},{8,12},{12,16},{16,20},{20,24},{24,28},{28,0},{32,36},... | collective-permute-start | bytes 786440 | tf_op jit(solution)/shard_map/ppermute | solution.py:30
  115.4 11.7 %collective-permute-start.30 = (bf16[8,128,128]{2,1,0:T(8,128)(2,1)S(1)}, bf16[8,128,128]{2,1,0:T(8,128)(2,1)S(1)}, u32[]{:S(2)}, u32[]{:S(2)}) collective-permute-start(bf16[8,128,128]{2,1,0:T(8,128)(2,1)S(1)} %get-tuple-element.101), channel_id=1, source_target_pairs={{0,28},{4,0},{8,4},{12,8},{16,12},{20,16},{24,20},{28,24},{32,60},... | collective-permute-start | bytes 786440 | tf_op jit(solution)/shard_map/ppermute | solution.py:30
  121.6 11.8 %collective-permute-start.36 = (bf16[9,128,128]{2,1,0:T(8,128)(2,1)S(1)}, bf16[9,128,128]{2,1,0:T(8,128)(2,1)S(1)}, u32[]{:S(2)}, u32[]{:S(2)}) collective-permute-start(bf16[9,128,128]{2,1,0:T(8,128)(2,1)S(1)} %get-tuple-element.118), channel_id=1, source_target_pairs={{0,28},{4,0},{8,4},{12,8},{16,12},{20,16},{24,20},{28,24},{32,60},... | collective-permute-start | bytes 884744 | tf_op jit(solution)/shard_map/ppermute | solution.py:30
  125.1 8.3 %collective-permute-start.37 = (bf16[9,128,128]{2,1,0:T(8,128)(2,1)S(1)}, bf16[9,128,128]{2,1,0:T(8,128)(2,1)S(1)}, u32[]{:S(2)}, u32[]{:S(2)}) collective-permute-start(bf16[9,128,128]{2,1,0:T(8,128)(2,1)S(1)} %get-tuple-element.119), channel_id=1, source_target_pairs={{0,4},{4,8},{8,12},{12,16},{16,20},{20,24},{24,28},{28,0},{32,36},... | collective-permute-start | bytes 884744 | tf_op jit(solution)/shard_map/ppermute | solution.py:30
  133.6 4.2 %collective-permute-start.40 = (bf16[5,128,128]{2,1,0:T(8,128)(2,1)S(1)}, bf16[5,128,128]{2,1,0:T(8,128)(2,1)S(1)}, u32[]{:S(2)}, u32[]{:S(2)}) collective-permute-start(bf16[5,128,128]{2,1,0:T(8,128)(2,1)S(1)} %get-tuple-element.129), channel_id=1, source_target_pairs={{0,96},{4,100},{8,104},{12,108},{16,112},{20,116},{24,120},{28,124... | collective-permute-start | bytes 491528 | tf_op jit(solution)/shard_map/ppermute | solution.py:30
  133.7 5.9 %collective-permute-start.39 = (bf16[5,128,128]{2,1,0:T(8,128)(2,1)S(1)}, bf16[5,128,128]{2,1,0:T(8,128)(2,1)S(1)}, u32[]{:S(2)}, u32[]{:S(2)}) collective-permute-start(bf16[5,128,128]{2,1,0:T(8,128)(2,1)S(1)} %get-tuple-element.128), channel_id=1, source_target_pairs={{0,64},{4,68},{8,72},{12,76},{16,80},{20,84},{24,88},{28,92},{32,9... | collective-permute-start | bytes 491528 | tf_op jit(solution)/shard_map/ppermute | solution.py:30
  133.8 8.5 %collective-permute-start.38 = (bf16[5,128,128]{2,1,0:T(8,128)(2,1)S(1)}, bf16[5,128,128]{2,1,0:T(8,128)(2,1)S(1)}, u32[]{:S(2)}, u32[]{:S(2)}) collective-permute-start(bf16[5,128,128]{2,1,0:T(8,128)(2,1)S(1)} %get-tuple-element.127), channel_id=1, source_target_pairs={{0,32},{4,36},{8,40},{12,44},{16,48},{20,52},{24,56},{28,60},{32,6... | collective-permute-start | bytes 491528 | tf_op jit(solution)/shard_map/ppermute | solution.py:30
  142.4 3.6 %collective-permute-start.41 = (bf16[3,128,128]{2,1,0:T(8,128)(2,1)S(1)}, bf16[3,128,128]{2,1,0:T(8,128)(2,1)S(1)}, u32[]{:S(2)}, u32[]{:S(2)}) collective-permute-start(bf16[3,128,128]{2,1,0:T(8,128)(2,1)S(1)} %pad_maximum_fusion.5), channel_id=1, source_target_pairs={{0,128},{4,132},{8,136},{12,140},{16,144},{20,148},{24,152},{28,15... | collective-permute-start | bytes 294920 | tf_op jit(solution)/shard_map/ppermute | solution.py:30
  146.0 5.5 %collective-permute-start.42 = (f32[64,256]{1,0:T(8,128)S(1)}, f32[64,256]{1,0:T(8,128)S(1)}, u32[]{:S(2)}, u32[]{:S(2)}) collective-permute-start(f32[64,256]{1,0:T(8,128)S(1)} %pad_maximum_fusion.6), channel_id=1, source_target_pairs={{0,1},{1,0},{2,3},{3,2},{4,5},{5,4},{6,7},{7,6},{8,9},{9,8},{10,11... | collective-permute-start | bytes 196616 | tf_op jit(solution)/shard_map/ppermute | solution.py:34
  (3 other events, 4.7 us)

commit v3 on v2

--- a/solution.py
+++ b/solution.py
@@ -75,7 +75,7 @@
     out[2 * region + UNROLL + 1] = (far_n + UNROLL - 1) // UNROLL
 
 
-def sort_slots(rows, cols, count, me, row_tiles):
+def slot_keys(rows, cols, count, me):
     slots = rows.shape[0]
     blocks = NY * NX * 2
     owner = cols // 2
@@ -86,7 +86,11 @@
     place = jnp.where(dz < FAR[0], dz, dz - FAR[0]) * blocks + dy * (NX * 2) + dx * 2 + cols % 2
     ids = jnp.arange(slots, dtype=jnp.int32)
     group = jnp.where(ids < count, jnp.where(far, 2, 1), 0)
-    keys = ids + (rows << 8) + (place << 12) + (group << 24)
+    return (ids + (rows << 8) + (place << 12) + (group << 24)).astype(jnp.int32)
+
+
+def sort_slots(keys, row_tiles):
+    slots = keys.shape[0]
     smem = pl.BlockSpec(memory_space=pltpu.SMEM)
 
     def kernel(*refs):
@@ -97,8 +101,9 @@
         out_shape=jax.ShapeDtypeStruct((2 * (slots + UNROLL) + UNROLL + 2,), jnp.int32),
         in_specs=[smem],
         out_specs=smem,
+        cost_estimate=pl.CostEstimate(flops=4 * 10**9, bytes_accessed=4096, transcendentals=0),
         name="sort_slots",
-    )(keys.astype(jnp.int32))
+    )(keys)
 
 
 class Slots:
@@ -130,16 +135,12 @@
     n = len(spans)
     pieces = refs[:n]
     before = refs[n] if group else None
-    *outs, feat, acc, fsem = refs[n + group :]
+    *outs, feat, acc = refs[n + group :]
     slots = Slots(slots_ref, group)
-    copies = []
-    for i, (at, size) in enumerate(spans):
-        copies.append(pltpu.make_async_copy(pieces[i], feat.at[pl.ds(at, size)], fsem.at[i]))
-        copies[-1].start()
+    for piece, (at, size) in zip(pieces, spans):
+        feat[pl.ds(at, size)] = piece[...]
     acc[...] = before[...] if group else jnp.zeros_like(acc)
     feat[feat.shape[0] - 1] = jnp.zeros(feat.shape[1:], feat.dtype)
-    for copy in copies:
-        copy.wait()
 
     def one(i):
         r = slots.row(i)
@@ -162,7 +163,6 @@
     blocks = sum(size for _, size in spans)
     smem = pl.BlockSpec(memory_space=pltpu.SMEM)
     vmem = pl.BlockSpec(memory_space=pltpu.VMEM)
-    hbm = pl.BlockSpec(memory_space=pl.ANY)
 
     def kernel(*refs):
         forward_kernel(group, spans, *refs)
@@ -174,12 +174,11 @@
     return pl.pallas_call(
         kernel,
         out_shape=out_shape,
-        in_specs=[smem] * 2 + [vmem] + [hbm] * len(pieces) + [vmem] * group,
+        in_specs=[smem] * 2 + [vmem] * (1 + len(pieces) + group),
         out_specs=[vmem] * len(out_shape),
         scratch_shapes=[
             pltpu.VMEM((blocks + 1, tile, fin), BF16),
             pltpu.VMEM((row_tiles + 1, tile, fin), F32),
-            pltpu.SemaphoreType.DMA((len(pieces),)),
         ],
         compiler_params=pltpu.CompilerParams(vmem_limit_bytes=VMEM_LIMIT),
         cost_estimate=pl.CostEstimate(
@@ -260,7 +259,7 @@
     row_tiles = 2 * half
     node_dev, fout = cots[0].shape
     nodes = row_tiles * tile
-    layout = (None, "rider", None, "rider", None, "none")
+    layout = ("none", None, "rider", None, "rider", None)
     blocks = size * len(layout)
     smem = pl.BlockSpec(memory_space=pltpu.SMEM)
     vmem = pl.BlockSpec(memory_space=pltpu.VMEM)
@@ -304,7 +303,7 @@
 def backward_near_call(slot_info, tiles, backs, size):
     tile = tiles.shape[-1]
     fin = backs.shape[1]
-    layout = (None, None) + (None, "none") * 4
+    layout = (None, None) + ("none", None) * 4
     blocks = size * len(layout)
     smem = pl.BlockSpec(memory_space=pltpu.SMEM)
     vmem = pl.BlockSpec(memory_space=pltpu.VMEM)
@@ -328,19 +327,20 @@
     )(slot_info, tiles, backs)
 
 
-def gather_features(features, cotangent, slot_info, tile, near_call):
+def gather_features(features, cotangent, keys, row_tiles, tile, near_call):
     fin = features.shape[1]
     mine = features.reshape(-1, tile, fin)
-    other, cot1 = fence(send(mine, dx=1), send_team(cotangent, 1))
+    other, cot1, keys = fence(send(mine, dx=1), send_team(cotangent, 1), keys)
     own = join(mine, other)
     y1 = send(own, dy=-1)
     y3 = send(own, dy=1)
     y2 = send(own, dy=-2)
-    y1, y3, slot_info = fence(y1, y3, slot_info)
     up0, up1 = [join(own, y1)], [join(y2, y3)]
     down0, down1 = [up0[0]], [up1[0]]
     for step in range(4):
         up0.append(send(up0[-1], dz=-1))
+        if step == 0:
+            up0[1], slot_info = fence(up0[1], sort_slots(keys, row_tiles))
         down1.append(send(down1[-1], dz=1))
         if step < 3:
             down0.append(send(down0[-1], dz=1))
@@ -380,32 +380,30 @@
     )(a, b, c, d)
 
 
-def ring_sums(arrived, long, short, dz):
-    ahead, back = [arrived], []
-    for i, (term, other) in enumerate(zip(long, short)):
+def ring_sums(long, short, dz):
+    ahead, back = [], []
+    message, reply = long[0], short[0]
+    for i in range(len(short)):
         if i:
-            message, reply = add_pair(term, ahead[-1], other, back[-1])
-        else:
-            message, reply = add(term, ahead[-1]).astype(BF16), other
+            message, reply = add_pair(long[i], ahead[-1], short[i], back[-1])
         message, reply = fence(send(message, dz=dz), send(reply, dz=-dz))
         ahead.append(message)
         back.append(reply)
+    ahead.append(send(add(long[-1], ahead[-1]).astype(BF16), dz=dz))
     return ahead, back
 
 
-def scatter_sums(near_call, far, rider):
+def scatter_sums(near, far, rider):
     g3, g4, g5 = [far[2 * i : 2 * i + 2] for i in range(3)]
-    first0, first1 = send(g4[0], dz=1), send(g4[1], dz=-1)
-    first0, *near = fence(first0, *near_call())
     g0, g1, g2, g6, g7 = [near[2 * i : 2 * i + 2] for i in range(5)]
-    up0, down0 = ring_sums(first0, (g3[0], g2[0], g1[0]), (g5[0], g6[0], g7[0]), 1)
-    down1, up1 = ring_sums(first1, (g5[1], g6[1], g7[1]), (g3[1], g2[1], g1[1]), -1)
+    up0, down0 = ring_sums((g4[0], g3[0], g2[0], g1[0]), (g5[0], g6[0], g7[0]), 1)
+    down1, up1 = ring_sums((g4[1], g5[1], g6[1], g7[1]), (g3[1], g2[1], g1[1]), -1)
     size = g0[0].shape[0]
-    plane0 = add(g0[0], up0[-1], down0[-1])
-    plane1 = add(g0[1], up1[-1][:size], down1[-1][:size]).astype(BF16)
-    u1, u2, u3 = [part[size:] for part in up1]
-    d1, d2, d3, d4 = [part[size:] for part in down1]
-    rider = ((add(rider, d4) + add(u2, d2)) + (add(u1, d3) + add(u3, d1))).astype(BF16)
+    plane0 = add(g0[0], up0[-1][:size], down0[-1][:size])
+    plane1 = add(g0[1], up1[-1], down1[-1]).astype(BF16)
+    u1, u2, u3, u4 = [part[size:] for part in up0]
+    d1, d2, d3 = [part[size:] for part in down0]
+    rider = ((add(rider, u4) + add(u2, d2)) + (add(u1, d3) + add(u3, d1))).astype(BF16)
     half = size // 2
     got1 = send(join(plane0[half:].astype(BF16), rider), dy=1)
     got2 = send(join(plane1[:half], rider), dy=2)
@@ -433,12 +431,11 @@
     row_tiles = node_dev // tile * teams
     scale = 1.0 / math.sqrt(node_dev * sections * teams)
     slab = tiles.reshape(slots, tile, tile)
-    slot_info = sort_slots(
+    keys = slot_keys(
         tile_rows.reshape(slots),
         tile_cols.reshape(slots),
         tile_count.reshape(()),
         lax.axis_index("section"),
-        row_tiles,
     )
     member = lax.axis_index("team").astype(jnp.int32).reshape(1)
 
@@ -447,7 +444,7 @@
         return forward_call(0, info, member, slab, pieces, spans_of(pieces), None, row_tiles)[0]
 
     near_sum, far, cots, slot_info = gather_features(
-        features, cotangent, slot_info, tile, near_call
+        features, cotangent, keys, row_tiles, tile, near_call
     )
     mine, theirs = forward_call(
         1, slot_info, member, slab, far, spans_of(far), near_sum, row_tiles
@@ -458,9 +455,8 @@
     output, rider, backs, *far_terms = backward_far_call(
         slot_info, member, slab, mine, send_team(mine, 1), cots, weight, size
     )
-    total, weight_sum = scatter_sums(
-        lambda: backward_near_call(slot_info, slab, backs, size), far_terms, rider
-    )
+    near_terms = backward_near_call(slot_info, slab, backs, size)
+    total, weight_sum = scatter_sums(near_terms, far_terms, rider)
     grad_features = total.transpose(0, 2, 1).reshape(node_dev, fin).astype(BF16)
     return output, grad_features, weight_sum * scale
 

time: 153 us -> 154 us (level); the launches traced: 152 us -> 155 us
  starting transfers between devices: 76.2 us -> 64.7 us
  waiting for transfers between devices: 52.2 us -> 61.6 us
  Pallas kernels: 11.5 us -> 16.3 us
    ppermute x36, waiting for transfers between devices: 46.8 us -> 55.4 us  [send(): return lax.ppermute(value, 'section', pairs)]
    ppermute x7, starting transfers between devices: 21 us -> 13.9 us  [send_team(): return lax.ppermute(value, 'team', [(t, t ^ mask) for t in range(4)])]
    ppermute x36, starting transfers between devices: 55.3 us -> 50.8 us  [send(): return lax.ppermute(value, 'section', pairs)]
    pallas_call x2, Pallas kernels: 3.72 us -> 5.84 us  [forward_call(): pl.pallas_call(kernel, out_shape=out_shape, in_specs=[smem] * 2 + [vmem]...]
    unnamed x17 -> x23, local copies, waits for them, and re-layouts: 4.76 us -> 4.78 us
  transfers between devices with their start and end apart: 43 -> 43, of which waited for: 25 -> 23; matrix products, arithmetic and copies ran while one was open for 3% -> 3% of each run, Pallas kernels for 4% -> 6%
where the time goes in v3:
time: 154 us; the launch traced here: 155 us
  starting transfers between devices  64.7 us (42%)
  waiting for transfers between devices  61.6 us (40%)
  Pallas kernels  16.3 us (11%)
  local copies, waits for them, and re-layouts  5.6 us (4%)
  other arithmetic  5.04 us (3%)
  between operations  1.65 us (1%)
    ppermute x36, waiting for transfers between devices, send(): return lax.ppermute(value, 'section', pairs)  55.4 us
    ppermute x36, starting transfers between devices, send(): return lax.ppermute(value, 'section', pairs)  50.8 us
    ppermute x7, starting transfers between devices, send_team(): return lax.ppermute(value, 'team', [(t, t ^ mask) for t in range(4)])  13.9 us
    ppermute x7, waiting for transfers between devices, send_team(): return lax.ppermute(value, 'team', [(t, t ^ mask) for t in range(4)])  6.13 us
    pallas_call x2, Pallas kernels, forward_call(): pl.pallas_call(kernel, out_shape=out_shape, in_specs=[smem] * 2 + [vmem]...  5.84 us
    unnamed x23, local copies, waits for them, and re-layouts  4.78 us
    pallas_call x1, Pallas kernels, backward_far_call(): pl.pallas_call(kernel, out_shape=[jax.ShapeDtypeStruct((node_dev, fout),...  4.18 us
    pallas_call x1, Pallas kernels, backward_near_call(): pl.pallas_call(kernel, out_shape=piece_shapes(layout, size, fin, tile), i...  3.31 us
  transfers between devices with their start and end apart: 43, of which 23 were waited for; matrix products, arithmetic and copies ran while one was open for 3% of the time, Pallas kernels for 6%

profile of v3, /device:TPU:1, one launch (start us, length us, event | category | flops | bytes accessed | tf_op | source)
XLA Modules:
  0.0 154.9 jit_solution(1248894045306966366)
XLA Ops:
  0.6 2.1 %collective-permute-start = (bf16[2,128,128]{2,1,0:T(8,128)(2,1)}, bf16[2,128,128]{2,1,0:T(8,128)(2,1)S(1)}, u32[]{:S(2)}, u32[]{:S(2)}) collective-permute-start(bf16[2,128,128]{2,1,0:T(8,128)(2,1)} %bitcast.20), channel_id=1, source_target_pairs={{0,128},{4,132},{8,136},{12,140},{16,144},{20,148},{24,152},{28,15... | collective-permute-start | bytes 196616 | tf_op jit(solution)/shard_map/ppermute | solution.py:30
  2.8 1.3 collective-permute-start.1
  5.4 1.3 fusion.10.refs_0_
  7.6 2.5 %collective-permute-start.2 = (bf16[4,128,128]{2,1,0:T(8,128)(2,1)S(1)}, bf16[4,128,128]{2,1,0:T(8,128)(2,1)S(1)}, u32[]{:S(2)}, u32[]{:S(2)}) collective-permute-start(bf16[4,128,128]{2,1,0:T(8,128)(2,1)S(1)} %pad_maximum_fusion.4), channel_id=1, source_target_pairs={{0,96},{4,100},{8,104},{12,108},{16,112},{20,116},{24,120},{28,124... | collective-permute-start | bytes 393224 | tf_op jit(solution)/shard_map/ppermute | solution.py:30
  11.1 2.5 %collective-permute-done.2 = bf16[4,128,128]{2,1,0:T(8,128)(2,1)S(1)} collective-permute-done((bf16[4,128,128]{2,1,0:T(8,128)(2,1)S(1)}, bf16[4,128,128]{2,1,0:T(8,128)(2,1)S(1)}, u32[]{:S(2)}, u32[]{:S(2)}) %collective-permute-start.2) | collective-permute-done | bytes 131104 | tf_op jit(solution)/shard_map/ppermute | solution.py:30
  14.5 7.3 %collective-permute-start.3 = (bf16[8,128,128]{2,1,0:T(8,128)(2,1)S(1)}, bf16[8,128,128]{2,1,0:T(8,128)(2,1)S(1)}, u32[]{:S(2)}, u32[]{:S(2)}) collective-permute-start(bf16[8,128,128]{2,1,0:T(8,128)(2,1)S(1)} %pad_maximum_fusion.refs_3_), channel_id=1, source_target_pairs={{0,28},{4,0},{8,4},{12,8},{16,12},{20,16},{24,20},{28,24},{32,60},... | collective-permute-start | bytes 786440 | tf_op jit(solution)/shard_map/ppermute | solution.py:30
  21.9 2.5 %sort_slots.1.refs_0_ = s32[562]{0:T(1024)} custom-call(s32[256]{0:T(256)} %fusion.10.refs_0_), custom_call_target="tpu_custom_call" | custom-call | flops 4000000000 | bytes 4096 | tf_op jit(solution)/shard_map/sort_slots/pallas_call | solution.py:99
  24.4 1.3 collective-permute-start.16
  25.7 2.4 %collective-permute-start.8 = (bf16[8,128,128]{2,1,0:T(8,128)(2,1)S(1)}, bf16[8,128,128]{2,1,0:T(8,128)(2,1)S(1)}, u32[]{:S(2)}, u32[]{:S(2)}) collective-permute-start(bf16[8,128,128]{2,1,0:T(8,128)(2,1)S(1)} %constant_dynamic-update-slice_fusion.refs_4_), channel_id=1, source_target_pairs={{0,28},{4,0},{8,4},{12,8},{16,12},{20,16},{24,20},{28,24},{32,60},... | collective-permute-start | bytes 786440 | tf_op jit(solution)/shard_map/ppermute | solution.py:30
  28.1 1.5 collective-permute-start.4
  29.6 1.5 collective-permute-done.12.refs_12_
  31.1 5.6 %collective-permute-done.16.refs_11_ = bf16[8,128,128]{2,1,0:T(8,128)(2,1)S(1)} collective-permute-done((bf16[8,128,128]{2,1,0:T(8,128)(2,1)S(1)}, bf16[8,128,128]{2,1,0:T(8,128)(2,1)S(1)}, u32[]{:S(2)}, u32[]{:S(2)}) %collective-permute-start.16) | collective-permute-done | bytes 262176 | tf_op jit(solution)/shard_map/ppermute | solution.py:30
  36.8 2.7 %collective-permute-start.9 = (bf16[8,128,128]{2,1,0:T(8,128)(2,1)S(1)}, bf16[8,128,128]{2,1,0:T(8,128)(2,1)S(1)}, u32[]{:S(2)}, u32[]{:S(2)}) collective-permute-start(bf16[8,128,128]{2,1,0:T(8,128)(2,1)S(1)} %collective-permute-done.8.refs_6_), channel_id=1, source_target_pairs={{0,28},{4,0},{8,4},{12,8},{16,12},{20,16},{24,20},{28,24},{32,60},... | collective-permute-start | bytes 786440 | tf_op jit(solution)/shard_map/ppermute | solution.py:30
  39.4 2.4 %collective-permute-start.5 = (bf16[8,128,128]{2,1,0:T(8,128)(2,1)S(1)}, bf16[8,128,128]{2,1,0:T(8,128)(2,1)S(1)}, u32[]{:S(2)}, u32[]{:S(2)}) collective-permute-start(bf16[8,128,128]{2,1,0:T(8,128)(2,1)S(1)} %collective-permute-done.4.refs_7_), channel_id=1, source_target_pairs={{0,28},{4,0},{8,4},{12,8},{16,12},{20,16},{24,20},{28,24},{32,60},... | collective-permute-start | bytes 786440 | tf_op jit(solution)/shard_map/ppermute | solution.py:30
  42.4 2.2 %collective-permute-start.19 = (bf16[256,256]{1,0:T(8,128)(2,1)S(1)}, bf16[256,256]{1,0:T(8,128)(2,1)S(1)}, u32[]{:S(2)}, u32[]{:S(2)}) collective-permute-start(bf16[256,256]{1,0:T(8,128)(2,1)S(1)} %copy-done.1), channel_id=1, source_target_pairs={{0,2},{1,3},{2,0},{3,1},{4,6},{5,7},{6,4},{7,5},{8,10},{9,11},{10,... | collective-permute-start | bytes 393224 | tf_op jit(solution)/shard_map/ppermute | solution.py:34
  44.6 3.4 %collective-permute-done.17.refs_9_ = bf16[8,128,128]{2,1,0:T(8,128)(2,1)S(1)} collective-permute-done((bf16[8,128,128]{2,1,0:T(8,128)(2,1)S(1)}, bf16[8,128,128]{2,1,0:T(8,128)(2,1)S(1)}, u32[]{:S(2)}, u32[]{:S(2)}) %collective-permute-start.17) | collective-permute-done | bytes 262176 | tf_op jit(solution)/shard_map/ppermute | solution.py:30
  48.0 2.7 %collective-permute-start.10 = (bf16[8,128,128]{2,1,0:T(8,128)(2,1)S(1)}, bf16[8,128,128]{2,1,0:T(8,128)(2,1)}, u32[]{:S(2)}, u32[]{:S(2)}) collective-permute-start(bf16[8,128,128]{2,1,0:T(8,128)(2,1)S(1)} %collective-permute-done.9.refs_8_), channel_id=1, source_target_pairs={{0,28},{4,0},{8,4},{12,8},{16,12},{20,16},{24,20},{28,24},{32,60},... | collective-permute-start | bytes 786440 | tf_op jit(solution)/shard_map/ppermute | solution.py:30
  51.2 2.4 %collective-permute-done.14.refs_8_ = bf16[8,128,128]{2,1,0:T(8,128)(2,1)S(1)} collective-permute-done((bf16[8,128,128]{2,1,0:T(8,128)(2,1)S(1)}, bf16[8,128,128]{2,1,0:T(8,128)(2,1)S(1)}, u32[]{:S(2)}, u32[]{:S(2)}) %collective-permute-start.14) | collective-permute-done | bytes 262176 | tf_op jit(solution)/shard_map/ppermute | solution.py:30
  54.3 2.2 %collective-permute-start.20 = (bf16[256,256]{1,0:T(8,128)(2,1)}, bf16[256,256]{1,0:T(8,128)(2,1)}, u32[]{:S(2)}, u32[]{:S(2)}) collective-permute-start(bf16[256,256]{1,0:T(8,128)(2,1)} %copy-done.2), channel_id=1, source_target_pairs={{0,2},{1,3},{2,0},{3,1},{4,6},{5,7},{6,4},{7,5},{8,10},{9,11},{10,... | collective-permute-start | bytes 393224 | tf_op jit(solution)/shard_map/ppermute | solution.py:34
  56.5 3.4 %copy-done = bf16[1,1,256,128,128]{4,3,2,1,0:T(8,128)(2,1)S(1)} copy-done((bf16[1,1,256,128,128]{4,3,2,1,0:T(8,128)(2,1)S(1)}, bf16[1,1,256,128,128]{4,3,2,1,0:T(8,128)(2,1)}, u32[]{:S(2)}) %copy-start) | copy-done | bytes 8388632
  60.6 3.0 %forward_near.1.refs_9_ = f32[9,128,128]{2,1,0:T(8,128)S(1)} custom-call(s32[562]{0:T(1024)S(1)} %copy-done.6, s32[1]{0:T(128)} %bitcast.4.refs_1_, bf16[256,128,128]{2,1,0:T(8,128)(2,1)S(1)} %bitcast.14, bf16[8,128,128]{2,1,0:T(8,128)(2,1)S(1)} %pad_maximum_fusion.refs_3_, bf16[8,128,128]{2,1,0:T(8,128)(2,1)S(1)} %constant_dynamic-update-slice_fusion.refs_4_, ...), custom_call_target="tpu_custom_call" | custom-call | flops 671088640 | bytes 5242880 | tf_op jit(solution)/shard_map/forward_near/pallas_call | solution.py:174
  63.6 1.3 collective-permute-done.15.refs_6_
  64.9 2.9 %forward_far.1 = (bf16[4,128,128]{2,1,0:T(8,128)(2,1)S(1)}, bf16[4,128,128]{2,1,0:T(8,128)(2,1)S(1)}) custom-call(s32[562]{0:T(1024)S(1)} %copy-done.7, s32[1]{0:T(128)} %bitcast.4.refs_1_, bf16[256,128,128]{2,1,0:T(8,128)(2,1)S(1)} %bitcast.15, bf16[8,128,128]{2,1,0:T(8,128)(2,1)S(1)} %collective-permute-done.5.refs_3_, ...), custom_call_target="tpu_custom_call" | custom-call | flops 402653184 | bytes 3145728 | tf_op jit(solution)/shard_map/forward_far/pallas_call | solution.py:174
  68.7 1.0 collective-permute-done.21
  69.7 2.3 %collective-permute-start.22 = (bf16[4,128,128]{2,1,0:T(8,128)(2,1)S(1)}, bf16[4,128,128]{2,1,0:T(8,128)(2,1)S(1)}, u32[]{:S(2)}, u32[]{:S(2)}) collective-permute-start(bf16[4,128,128]{2,1,0:T(8,128)(2,1)S(1)} %add_convert_fusion.4), channel_id=1, source_target_pairs={{0,2},{1,3},{2,0},{3,1},{4,6},{5,7},{6,4},{7,5},{8,10},{9,11},{10,... | collective-permute-start | bytes 393224 | tf_op jit(solution)/shard_map/ppermute | solution.py:34
  72.0 4.0 %collective-permute-done.22 = bf16[4,128,128]{2,1,0:T(8,128)(2,1)S(1)} collective-permute-done((bf16[4,128,128]{2,1,0:T(8,128)(2,1)S(1)}, bf16[4,128,128]{2,1,0:T(8,128)(2,1)S(1)}, u32[]{:S(2)}, u32[]{:S(2)}) %collective-permute-start.22) | collective-permute-done | bytes 131104 | tf_op jit(solution)/shard_map/ppermute | solution.py:34
  76.1 1.3 collective-permute-start.23
  77.3 1.0 collective-permute-done.23.refs_4_
  78.3 4.2 %dense_and_backward_far.1 = (bf16[256,256]{1,0:T(8,128)(2,1)}, bf16[1,128,128]{2,1,0:T(8,128)(2,1)S(1)}, bf16[9,128,128]{2,1,0:T(8,128)(2,1)S(1)}, bf16[9,128,12...) custom-call(s32[562]{0:T(1024)S(1)} %copy-done.7, ...), custom_call_target="tpu_custom_call" | custom-call | flops 402653184 | bytes 4718592 | tf_op jit(solution)/shard_map/dense_and_backward_far/pallas_call | solution.py:270
  82.5 3.7 %collective-permute-start.32 = (bf16[8,128,128]{2,1,0:T(8,128)(2,1)S(1)}, bf16[8,128,128]{2,1,0:T(8,128)(2,1)S(1)}, u32[]{:S(2)}, u32[]{:S(2)}) collective-permute-start(bf16[8,128,128]{2,1,0:T(8,128)(2,1)S(1)} %get-tuple-element.86), channel_id=1, source_target_pairs={{0,28},{4,0},{8,4},{12,8},{16,12},{20,16},{24,20},{28,24},{32,60},... | collective-permute-start | bytes 786440 | tf_op jit(solution)/shard_map/ppermute | solution.py:30
  86.2 2.7 %collective-permute-start.25 = (bf16[9,128,128]{2,1,0:T(8,128)(2,1)S(1)}, bf16[9,128,128]{2,1,0:T(8,128)(2,1)S(1)}, u32[]{:S(2)}, u32[]{:S(2)}) collective-permute-start(bf16[9,128,128]{2,1,0:T(8,128)(2,1)S(1)} %get-tuple-element.69), channel_id=1, source_target_pairs={{0,28},{4,0},{8,4},{12,8},{16,12},{20,16},{24,20},{28,24},{32,60},... | collective-permute-start | bytes 884744 | tf_op jit(solution)/shard_map/ppermute | solution.py:30
  89.0 3.3 %backward_near.1 = (bf16[8,128,128]{2,1,0:T(8,128)(2,1)S(1)}, bf16[8,128,128]{2,1,0:T(8,128)(2,1)S(1)}, bf16[9,128,128]{2,1,0:T(8,128)(2,1)S(1)}, bf16[8,128,128...) custom-call(s32[562]{0:T(1024)S(1)} %copy-done.7, ...), custom_call_target="tpu_custom_call" | custom-call | flops 671088640 | bytes 7864320 | tf_op jit(solution)/shard_map/backward_near/pallas_call | solution.py:314
  92.3 1.4 collective-permute-done.33.d_ref
  95.3 4.7 %collective-permute-done.24.b_ref = bf16[9,128,128]{2,1,0:T(8,128)(2,1)S(1)} collective-permute-done((bf16[9,128,128]{2,1,0:T(8,128)(2,1)S(1)}, bf16[9,128,128]{2,1,0:T(8,128)(2,1)S(1)}, u32[]{:S(2)}, u32[]{:S(2)}) %collective-permute-start.24) | collective-permute-done | bytes 294944 | tf_op jit(solution)/shard_map/ppermute | solution.py:30
  100.2 2.7 %collective-permute-start.27 = (bf16[9,128,128]{2,1,0:T(8,128)(2,1)S(1)}, bf16[9,128,128]{2,1,0:T(8,128)(2,1)S(1)}, u32[]{:S(2)}, u32[]{:S(2)}) collective-permute-start(bf16[9,128,128]{2,1,0:T(8,128)(2,1)S(1)} %get-tuple-element.74), channel_id=1, source_target_pairs={{0,28},{4,0},{8,4},{12,8},{16,12},{20,16},{24,20},{28,24},{32,60},... | collective-permute-start | bytes 884744 | tf_op jit(solution)/shard_map/ppermute | solution.py:30
  102.9 2.7 %collective-permute-done.35.d_ref = bf16[8,128,128]{2,1,0:T(8,128)(2,1)S(1)} collective-permute-done((bf16[8,128,128]{2,1,0:T(8,128)(2,1)S(1)}, bf16[8,128,128]{2,1,0:T(8,128)(2,1)S(1)}, u32[]{:S(2)}, u32[]{:S(2)}) %collective-permute-start.35) | collective-permute-done | bytes 262176 | tf_op jit(solution)/shard_map/ppermute | solution.py:30
  107.3 4.7 %collective-permute-done.26.b_ref = bf16[9,128,128]{2,1,0:T(8,128)(2,1)S(1)} collective-permute-done((bf16[9,128,128]{2,1,0:T(8,128)(2,1)S(1)}, bf16[9,128,128]{2,1,0:T(8,128)(2,1)S(1)}, u32[]{:S(2)}, u32[]{:S(2)}) %collective-permute-start.26) | collective-permute-done | bytes 294944 | tf_op jit(solution)/shard_map/ppermute | solution.py:30
  112.2 2.7 %collective-permute-start.29 = (bf16[9,128,128]{2,1,0:T(8,128)(2,1)S(1)}, bf16[9,128,128]{2,1,0:T(8,128)(2,1)S(1)}, u32[]{:S(2)}, u32[]{:S(2)}) collective-permute-start(bf16[9,128,128]{2,1,0:T(8,128)(2,1)S(1)} %get-tuple-element.79), channel_id=1, source_target_pairs={{0,28},{4,0},{8,4},{12,8},{16,12},{20,16},{24,20},{28,24},{32,60},... | collective-permute-start | bytes 884744 | tf_op jit(solution)/shard_map/ppermute | solution.py:30
  114.8 2.7 %collective-permute-done.37 = bf16[8,128,128]{2,1,0:T(8,128)(2,1)S(1)} collective-permute-done((bf16[8,128,128]{2,1,0:T(8,128)(2,1)S(1)}, bf16[8,128,128]{2,1,0:T(8,128)(2,1)S(1)}, u32[]{:S(2)}, u32[]{:S(2)}) %collective-permute-start.37) | collective-permute-done | bytes 262176 | tf_op jit(solution)/shard_map/ppermute | solution.py:30
  118.5 5.3 %collective-permute-done.28 = bf16[9,128,128]{2,1,0:T(8,128)(2,1)S(1)} collective-permute-done((bf16[9,128,128]{2,1,0:T(8,128)(2,1)S(1)}, bf16[9,128,128]{2,1,0:T(8,128)(2,1)S(1)}, u32[]{:S(2)}, u32[]{:S(2)}) %collective-permute-start.28) | collective-permute-done | bytes 294944 | tf_op jit(solution)/shard_map/ppermute | solution.py:30
  124.0 1.9 %collective-permute-done.38 = bf16[8,128,128]{2,1,0:T(8,128)(2,1)S(1)} collective-permute-done((bf16[8,128,128]{2,1,0:T(8,128)(2,1)S(1)}, bf16[8,128,128]{2,1,0:T(8,128)(2,1)S(1)}, u32[]{:S(2)}, u32[]{:S(2)}) %collective-permute-start.38) | collective-permute-done | bytes 262176 | tf_op jit(solution)/shard_map/ppermute | solution.py:30
  126.1 5.1 %collective-permute-done.30 = bf16[9,128,128]{2,1,0:T(8,128)(2,1)S(1)} collective-permute-done((bf16[9,128,128]{2,1,0:T(8,128)(2,1)S(1)}, bf16[9,128,128]{2,1,0:T(8,128)(2,1)S(1)}, u32[]{:S(2)}, u32[]{:S(2)}) %collective-permute-start.30) | collective-permute-done | bytes 294944 | tf_op jit(solution)/shard_map/ppermute | solution.py:30
  131.4 1.8 %collective-permute-start.31 = (bf16[5,128,128]{2,1,0:T(8,128)(2,1)S(1)}, bf16[5,128,128]{2,1,0:T(8,128)(2,1)S(1)}, u32[]{:S(2)}, u32[]{:S(2)}) collective-permute-start(bf16[5,128,128]{2,1,0:T(8,128)(2,1)S(1)} %get-tuple-element.105), channel_id=1, source_target_pairs={{0,32},{4,36},{8,40},{12,44},{16,48},{20,52},{24,56},{28,60},{32,6... | collective-permute-start | bytes 491528 | tf_op jit(solution)/shard_map/ppermute | solution.py:30
  133.2 6.4 %collective-permute-start.39 = (bf16[5,128,128]{2,1,0:T(8,128)(2,1)S(1)}, bf16[5,128,128]{2,1,0:T(8,128)(2,1)S(1)}, u32[]{:S(2)}, u32[]{:S(2)}) collective-permute-start(bf16[5,128,128]{2,1,0:T(8,128)(2,1)S(1)} %get-tuple-element.106), channel_id=1, source_target_pairs={{0,64},{4,68},{8,72},{12,76},{16,80},{20,84},{24,88},{28,92},{32,9... | collective-permute-start | bytes 491528 | tf_op jit(solution)/shard_map/ppermute | solution.py:30
  139.7 1.9 %collective-permute-done.31 = bf16[5,128,128]{2,1,0:T(8,128)(2,1)S(1)} collective-permute-done((bf16[5,128,128]{2,1,0:T(8,128)(2,1)S(1)}, bf16[5,128,128]{2,1,0:T(8,128)(2,1)S(1)}, u32[]{:S(2)}, u32[]{:S(2)}) %collective-permute-start.31) | collective-permute-done | bytes 163872 | tf_op jit(solution)/shard_map/ppermute | solution.py:30
  141.5 4.1 %collective-permute-done.39 = bf16[5,128,128]{2,1,0:T(8,128)(2,1)S(1)} collective-permute-done((bf16[5,128,128]{2,1,0:T(8,128)(2,1)S(1)}, bf16[5,128,128]{2,1,0:T(8,128)(2,1)S(1)}, u32[]{:S(2)}, u32[]{:S(2)}) %collective-permute-start.39) | collective-permute-done | bytes 163872 | tf_op jit(solution)/shard_map/ppermute | solution.py:30
  146.1 3.4 %collective-permute-done.41 = bf16[3,128,128]{2,1,0:T(8,128)(2,1)S(1)} collective-permute-done((bf16[3,128,128]{2,1,0:T(8,128)(2,1)S(1)}, bf16[3,128,128]{2,1,0:T(8,128)(2,1)S(1)}, u32[]{:S(2)}, u32[]{:S(2)}) %collective-permute-start.41) | collective-permute-done | bytes 98336 | tf_op jit(solution)/shard_map/ppermute | solution.py:30
  149.6 3.7 %collective-permute-start.42 = (f32[64,256]{1,0:T(8,128)S(1)}, f32[64,256]{1,0:T(8,128)S(1)}, u32[]{:S(2)}, u32[]{:S(2)}) collective-permute-start(f32[64,256]{1,0:T(8,128)S(1)} %pad_maximum_fusion.6), channel_id=1, source_target_pairs={{0,1},{1,0},{2,3},{3,2},{4,5},{5,4},{6,7},{7,6},{8,9},{9,8},{10,11... | collective-permute-start | bytes 196616 | tf_op jit(solution)/shard_map/ppermute | solution.py:34
  (96 shorter events, 14.4 us)
Async XLA Ops:
  0.6 41.7 %copy-start.1 = (bf16[256,256]{1,0:T(8,128)(2,1)S(1)}, bf16[256,256]{1,0:T(8,128)(2,1)}, u32[]{:S(2)}) copy-start(bf16[256,256]{1,0:T(8,128)(2,1)} %refs_5_.1) | copy-start | bytes 393220
  0.6 6.0 %collective-permute-start = (bf16[2,128,128]{2,1,0:T(8,128)(2,1)}, bf16[2,128,128]{2,1,0:T(8,128)(2,1)S(1)}, u32[]{:S(2)}, u32[]{:S(2)}) collective-permute-start(bf16[2,128,128]{2,1,0:T(8,128)(2,1)} %bitcast.20), channel_id=1, source_target_pairs={{0,128},{4,132},{8,136},{12,140},{16,144},{20,148},{24,152},{28,15... | collective-permute-start | bytes 196616 | tf_op jit(solution)/shard_map/ppermute | solution.py:30
  2.8 3.9 %collective-permute-start.1 = (bf16[256,256]{1,0:T(8,128)(2,1)}, bf16[256,256]{1,0:T(8,128)(2,1)S(1)}, u32[]{:S(2)}, u32[]{:S(2)}) collective-permute-start(bf16[256,256]{1,0:T(8,128)(2,1)} %refs_5_.1), channel_id=1, source_target_pairs={{0,1},{1,0},{2,3},{3,2},{4,5},{5,4},{6,7},{7,6},{8,9},{9,8},{10,11... | collective-permute-start | bytes 393224 | tf_op jit(solution)/shard_map/ppermute | solution.py:34
  7.6 6.0 %collective-permute-start.2 = (bf16[4,128,128]{2,1,0:T(8,128)(2,1)S(1)}, bf16[4,128,128]{2,1,0:T(8,128)(2,1)S(1)}, u32[]{:S(2)}, u32[]{:S(2)}) collective-permute-start(bf16[4,128,128]{2,1,0:T(8,128)(2,1)S(1)} %pad_maximum_fusion.4), channel_id=1, source_target_pairs={{0,96},{4,100},{8,104},{12,108},{16,112},{20,116},{24,120},{28,124... | collective-permute-start | bytes 393224 | tf_op jit(solution)/shard_map/ppermute | solution.py:30
  10.1 11.7 %collective-permute-start.6 = (bf16[4,128,128]{2,1,0:T(8,128)(2,1)S(1)}, bf16[4,128,128]{2,1,0:T(8,128)(2,1)S(1)}, u32[]{:S(2)}, u32[]{:S(2)}) collective-permute-start(bf16[4,128,128]{2,1,0:T(8,128)(2,1)S(1)} %pad_maximum_fusion.4), channel_id=1, source_target_pairs={{0,64},{4,68},{8,72},{12,76},{16,80},{20,84},{24,88},{28,92},{32,9... | collective-permute-start | bytes 393224 | tf_op jit(solution)/shard_map/ppermute | solution.py:30
  10.4 11.4 %collective-permute-start.7 = (bf16[4,128,128]{2,1,0:T(8,128)(2,1)S(1)}, bf16[4,128,128]{2,1,0:T(8,128)(2,1)S(1)}, u32[]{:S(2)}, u32[]{:S(2)}) collective-permute-start(bf16[4,128,128]{2,1,0:T(8,128)(2,1)S(1)} %pad_maximum_fusion.4), channel_id=1, source_target_pairs={{0,32},{4,36},{8,40},{12,44},{16,48},{20,52},{24,56},{28,60},{32,6... | collective-permute-start | bytes 393224 | tf_op jit(solution)/shard_map/ppermute | solution.py:30
  14.5 13.7 %collective-permute-start.3 = (bf16[8,128,128]{2,1,0:T(8,128)(2,1)S(1)}, bf16[8,128,128]{2,1,0:T(8,128)(2,1)S(1)}, u32[]{:S(2)}, u32[]{:S(2)}) collective-permute-start(bf16[8,128,128]{2,1,0:T(8,128)(2,1)S(1)} %pad_maximum_fusion.refs_3_), channel_id=1, source_target_pairs={{0,28},{4,0},{8,4},{12,8},{16,12},{20,16},{24,20},{28,24},{32,60},... | collective-permute-start | bytes 786440 | tf_op jit(solution)/shard_map/ppermute | solution.py:30
  21.8 9.3 %collective-permute-start.12 = (bf16[8,128,128]{2,1,0:T(8,128)(2,1)S(1)}, bf16[8,128,128]{2,1,0:T(8,128)(2,1)S(1)}, u32[]{:S(2)}, u32[]{:S(2)}) collective-permute-start(bf16[8,128,128]{2,1,0:T(8,128)(2,1)S(1)} %constant_dynamic-update-slice_fusion.refs_4_), channel_id=1, source_target_pairs={{0,4},{4,8},{8,12},{12,16},{16,20},{20,24},{24,28},{28,0},{32,36},... | collective-permute-start | bytes 786440 | tf_op jit(solution)/shard_map/ppermute | solution.py:30
  24.4 40.5 %copy-start.7 = (s32[562]{0:T(1024)S(1)}, s32[562]{0:T(1024)}, u32[]{:S(2)}) copy-start(s32[562]{0:T(1024)} %sort_slots.1.refs_0_) | copy-start | bytes 6748
  24.4 12.3 %collective-permute-start.16 = (bf16[8,128,128]{2,1,0:T(8,128)(2,1)S(1)}, bf16[8,128,128]{2,1,0:T(8,128)(2,1)S(1)}, u32[]{:S(2)}, u32[]{:S(2)}) collective-permute-start(bf16[8,128,128]{2,1,0:T(8,128)(2,1)S(1)} %pad_maximum_fusion.refs_3_), channel_id=1, source_target_pairs={{0,4},{4,8},{8,12},{12,16},{16,20},{20,24},{24,28},{28,0},{32,36},... | collective-permute-start | bytes 786440 | tf_op jit(solution)/shard_map/ppermute | solution.py:30
  25.7 11.0 %collective-permute-start.8 = (bf16[8,128,128]{2,1,0:T(8,128)(2,1)S(1)}, bf16[8,128,128]{2,1,0:T(8,128)(2,1)S(1)}, u32[]{:S(2)}, u32[]{:S(2)}) collective-permute-start(bf16[8,128,128]{2,1,0:T(8,128)(2,1)S(1)} %constant_dynamic-update-slice_fusion.refs_4_), channel_id=1, source_target_pairs={{0,28},{4,0},{8,4},{12,8},{16,12},{20,16},{24,20},{28,24},{32,60},... | collective-permute-start | bytes 786440 | tf_op jit(solution)/shard_map/ppermute | solution.py:30
  28.1 11.3 %collective-permute-start.4 = (bf16[8,128,128]{2,1,0:T(8,128)(2,1)S(1)}, bf16[8,128,128]{2,1,0:T(8,128)(2,1)S(1)}, u32[]{:S(2)}, u32[]{:S(2)}) collective-permute-start(bf16[8,128,128]{2,1,0:T(8,128)(2,1)S(1)} %collective-permute-done.3.refs_5_), channel_id=1, source_target_pairs={{0,28},{4,0},{8,4},{12,8},{16,12},{20,16},{24,20},{28,24},{32,60},... | collective-permute-start | bytes 786440 | tf_op jit(solution)/shard_map/ppermute | solution.py:30
  31.1 11.2 %collective-permute-start.13 = (bf16[8,128,128]{2,1,0:T(8,128)(2,1)S(1)}, bf16[8,128,128]{2,1,0:T(8,128)(2,1)S(1)}, u32[]{:S(2)}, u32[]{:S(2)}) collective-permute-start(bf16[8,128,128]{2,1,0:T(8,128)(2,1)S(1)} %collective-permute-done.12.refs_12_), channel_id=1, source_target_pairs={{0,4},{4,8},{8,12},{12,16},{16,20},{20,24},{24,28},{28,0},{32,36},... | collective-permute-start | bytes 786440 | tf_op jit(solution)/shard_map/ppermute | solution.py:30
  36.7 11.2 %collective-permute-start.17 = (bf16[8,128,128]{2,1,0:T(8,128)(2,1)S(1)}, bf16[8,128,128]{2,1,0:T(8,128)(2,1)S(1)}, u32[]{:S(2)}, u32[]{:S(2)}) collective-permute-start(bf16[8,128,128]{2,1,0:T(8,128)(2,1)S(1)} %collective-permute-done.16.refs_11_), channel_id=1, source_target_pairs={{0,4},{4,8},{8,12},{12,16},{16,20},{20,24},{24,28},{28,0},{32,36},... | collective-permute-start | bytes 786440 | tf_op jit(solution)/shard_map/ppermute | solution.py:30
  36.8 11.2 %collective-permute-start.9 = (bf16[8,128,128]{2,1,0:T(8,128)(2,1)S(1)}, bf16[8,128,128]{2,1,0:T(8,128)(2,1)S(1)}, u32[]{:S(2)}, u32[]{:S(2)}) collective-permute-start(bf16[8,128,128]{2,1,0:T(8,128)(2,1)S(1)} %collective-permute-done.8.refs_6_), channel_id=1, source_target_pairs={{0,28},{4,0},{8,4},{12,8},{16,12},{20,16},{24,20},{28,24},{32,60},... | collective-permute-start | bytes 786440 | tf_op jit(solution)/shard_map/ppermute | solution.py:30
  39.4 11.2 %collective-permute-start.5 = (bf16[8,128,128]{2,1,0:T(8,128)(2,1)S(1)}, bf16[8,128,128]{2,1,0:T(8,128)(2,1)S(1)}, u32[]{:S(2)}, u32[]{:S(2)}) collective-permute-start(bf16[8,128,128]{2,1,0:T(8,128)(2,1)S(1)} %collective-permute-done.4.refs_7_), channel_id=1, source_target_pairs={{0,28},{4,0},{8,4},{12,8},{16,12},{20,16},{24,20},{28,24},{32,60},... | collective-permute-start | bytes 786440 | tf_op jit(solution)/shard_map/ppermute | solution.py:30
  42.4 11.2 %collective-permute-start.14 = (bf16[8,128,128]{2,1,0:T(8,128)(2,1)S(1)}, bf16[8,128,128]{2,1,0:T(8,128)(2,1)S(1)}, u32[]{:S(2)}, u32[]{:S(2)}) collective-permute-start(bf16[8,128,128]{2,1,0:T(8,128)(2,1)S(1)} %collective-permute-done.13.refs_10_), channel_id=1, source_target_pairs={{0,4},{4,8},{8,12},{12,16},{16,20},{20,24},{24,28},{28,0},{32,36},... | collective-permute-start | bytes 786440 | tf_op jit(solution)/shard_map/ppermute | solution.py:30
  42.4 11.2 %collective-permute-start.19 = (bf16[256,256]{1,0:T(8,128)(2,1)S(1)}, bf16[256,256]{1,0:T(8,128)(2,1)S(1)}, u32[]{:S(2)}, u32[]{:S(2)}) collective-permute-start(bf16[256,256]{1,0:T(8,128)(2,1)S(1)} %copy-done.1), channel_id=1, source_target_pairs={{0,2},{1,3},{2,0},{3,1},{4,6},{5,7},{6,4},{7,5},{8,10},{9,11},{10,... | collective-permute-start | bytes 393224 | tf_op jit(solution)/shard_map/ppermute | solution.py:34
  48.0 15.6 %collective-permute-start.18 = (bf16[8,128,128]{2,1,0:T(8,128)(2,1)S(1)}, bf16[8,128,128]{2,1,0:T(8,128)(2,1)S(1)}, u32[]{:S(2)}, u32[]{:S(2)}) collective-permute-start(bf16[8,128,128]{2,1,0:T(8,128)(2,1)S(1)} %collective-permute-done.17.refs_9_), channel_id=1, source_target_pairs={{0,4},{4,8},{8,12},{12,16},{16,20},{20,24},{24,28},{28,0},{32,36},... | collective-permute-start | bytes 786440 | tf_op jit(solution)/shard_map/ppermute | solution.py:30
  48.0 15.6 %collective-permute-start.10 = (bf16[8,128,128]{2,1,0:T(8,128)(2,1)S(1)}, bf16[8,128,128]{2,1,0:T(8,128)(2,1)}, u32[]{:S(2)}, u32[]{:S(2)}) collective-permute-start(bf16[8,128,128]{2,1,0:T(8,128)(2,1)S(1)} %collective-permute-done.9.refs_8_), channel_id=1, source_target_pairs={{0,28},{4,0},{8,4},{12,8},{16,12},{20,16},{24,20},{28,24},{32,60},... | collective-permute-start | bytes 786440 | tf_op jit(solution)/shard_map/ppermute | solution.py:30
  50.7 13.0 %collective-permute-start.11 = (bf16[8,128,128]{2,1,0:T(8,128)(2,1)S(1)}, bf16[8,128,128]{2,1,0:T(8,128)(2,1)}, u32[]{:S(2)}, u32[]{:S(2)}) collective-permute-start(bf16[8,128,128]{2,1,0:T(8,128)(2,1)S(1)} %collective-permute-done.5.refs_3_), channel_id=1, source_target_pairs={{0,28},{4,0},{8,4},{12,8},{16,12},{20,16},{24,20},{28,24},{32,60},... | collective-permute-start | bytes 786440 | tf_op jit(solution)/shard_map/ppermute | solution.py:30
  53.6 11.3 %collective-permute-start.15 = (bf16[8,128,128]{2,1,0:T(8,128)(2,1)S(1)}, bf16[8,128,128]{2,1,0:T(8,128)(2,1)}, u32[]{:S(2)}, u32[]{:S(2)}) collective-permute-start(bf16[8,128,128]{2,1,0:T(8,128)(2,1)S(1)} %collective-permute-done.14.refs_8_), channel_id=1, source_target_pairs={{0,4},{4,8},{8,12},{12,16},{16,20},{20,24},{24,28},{28,0},{32,36},... | collective-permute-start | bytes 786440 | tf_op jit(solution)/shard_map/ppermute | solution.py:30
  54.3 9.3 %collective-permute-start.20 = (bf16[256,256]{1,0:T(8,128)(2,1)}, bf16[256,256]{1,0:T(8,128)(2,1)}, u32[]{:S(2)}, u32[]{:S(2)}) collective-permute-start(bf16[256,256]{1,0:T(8,128)(2,1)} %copy-done.2), channel_id=1, source_target_pairs={{0,2},{1,3},{2,0},{3,1},{4,6},{5,7},{6,4},{7,5},{8,10},{9,11},{10,... | collective-permute-start | bytes 393224 | tf_op jit(solution)/shard_map/ppermute | solution.py:34
  60.6 28.4 %slice-start = ((s8[8388608]{0:T(1024)(128)(4,1)}), s8[4194304]{0:T(1024)(128)(4,1)S(1)}, s32[]{:S(2)}) async-start(s8[8388608]{0:T(1024)(128)(4,1)} %bitcast.17), calls=%async_computation | async-start | bytes 8388608
  63.6 14.8 %copy-start.3 = (bf16[256,256]{1,0:T(8,128)(2,1)S(1)}, bf16[256,256]{1,0:T(8,128)(2,1)}, u32[]{:S(2)}) copy-start(bf16[256,256]{1,0:T(8,128)(2,1)} %copy-done.2) | copy-start | bytes 393220
  63.6 25.4 %slice-start.1 = ((s8[8388608]{0:T(1024)(128)(4,1)}), s8[4194304]{0:T(1024)(128)(4,1)S(1)}, s32[]{:S(2)}) async-start(s8[8388608]{0:T(1024)(128)(4,1)} %bitcast.17), calls=%async_computation.1 | async-start | bytes 8388608
  67.8 1.8 %collective-permute-start.21 = (bf16[4,128,128]{2,1,0:T(8,128)(2,1)S(1)}, bf16[4,128,128]{2,1,0:T(8,128)(2,1)S(1)}, u32[]{:S(2)}, u32[]{:S(2)}) collective-permute-start(bf16[4,128,128]{2,1,0:T(8,128)(2,1)S(1)} %get-tuple-element.59), channel_id=1, source_target_pairs={{0,1},{1,0},{2,3},{3,2},{4,5},{5,4},{6,7},{7,6},{8,9},{9,8},{10,11... | collective-permute-start | bytes 393224 | tf_op jit(solution)/shard_map/ppermute | solution.py:34
  69.7 6.3 %collective-permute-start.22 = (bf16[4,128,128]{2,1,0:T(8,128)(2,1)S(1)}, bf16[4,128,128]{2,1,0:T(8,128)(2,1)S(1)}, u32[]{:S(2)}, u32[]{:S(2)}) collective-permute-start(bf16[4,128,128]{2,1,0:T(8,128)(2,1)S(1)} %add_convert_fusion.4), channel_id=1, source_target_pairs={{0,2},{1,3},{2,0},{3,1},{4,6},{5,7},{6,4},{7,5},{8,10},{9,11},{10,... | collective-permute-start | bytes 393224 | tf_op jit(solution)/shard_map/ppermute | solution.py:34
  76.1 2.3 %collective-permute-start.23 = (bf16[4,128,128]{2,1,0:T(8,128)(2,1)S(1)}, bf16[4,128,128]{2,1,0:T(8,128)(2,1)S(1)}, u32[]{:S(2)}, u32[]{:S(2)}) collective-permute-start(bf16[4,128,128]{2,1,0:T(8,128)(2,1)S(1)} %add_convert_fusion.3.refs_3_), channel_id=1, source_target_pairs={{0,1},{1,0},{2,3},{3,2},{4,5},{5,4},{6,7},{7,6},{8,9},{9,8},{10,11... | collective-permute-start | bytes 393224 | tf_op jit(solution)/shard_map/ppermute | solution.py:34
  82.5 9.8 %collective-permute-start.32 = (bf16[8,128,128]{2,1,0:T(8,128)(2,1)S(1)}, bf16[8,128,128]{2,1,0:T(8,128)(2,1)S(1)}, u32[]{:S(2)}, u32[]{:S(2)}) collective-permute-start(bf16[8,128,128]{2,1,0:T(8,128)(2,1)S(1)} %get-tuple-element.86), channel_id=1, source_target_pairs={{0,28},{4,0},{8,4},{12,8},{16,12},{20,16},{24,20},{28,24},{32,60},... | collective-permute-start | bytes 786440 | tf_op jit(solution)/shard_map/ppermute | solution.py:30
  86.2 7.4 %collective-permute-start.33 = (bf16[8,128,128]{2,1,0:T(8,128)(2,1)S(1)}, bf16[8,128,128]{2,1,0:T(8,128)(2,1)S(1)}, u32[]{:S(2)}, u32[]{:S(2)}) collective-permute-start(bf16[8,128,128]{2,1,0:T(8,128)(2,1)S(1)} %get-tuple-element.87), channel_id=1, source_target_pairs={{0,4},{4,8},{8,12},{12,16},{16,20},{20,24},{24,28},{28,0},{32,36},... | collective-permute-start | bytes 786440 | tf_op jit(solution)/shard_map/ppermute | solution.py:30
  86.2 13.7 %collective-permute-start.24 = (bf16[9,128,128]{2,1,0:T(8,128)(2,1)S(1)}, bf16[9,128,128]{2,1,0:T(8,128)(2,1)S(1)}, u32[]{:S(2)}, u32[]{:S(2)}) collective-permute-start(bf16[9,128,128]{2,1,0:T(8,128)(2,1)S(1)} %get-tuple-element.68), channel_id=1, source_target_pairs={{0,4},{4,8},{8,12},{12,16},{16,20},{20,24},{24,28},{28,0},{32,36},... | collective-permute-start | bytes 884744 | tf_op jit(solution)/shard_map/ppermute | solution.py:30
  86.2 13.7 %collective-permute-start.25 = (bf16[9,128,128]{2,1,0:T(8,128)(2,1)S(1)}, bf16[9,128,128]{2,1,0:T(8,128)(2,1)S(1)}, u32[]{:S(2)}, u32[]{:S(2)}) collective-permute-start(bf16[9,128,128]{2,1,0:T(8,128)(2,1)S(1)} %get-tuple-element.69), channel_id=1, source_target_pairs={{0,28},{4,0},{8,4},{12,8},{16,12},{20,16},{24,20},{28,24},{32,60},... | collective-permute-start | bytes 884744 | tf_op jit(solution)/shard_map/ppermute | solution.py:30
  93.8 9.1 %collective-permute-start.34 = (bf16[8,128,128]{2,1,0:T(8,128)(2,1)S(1)}, bf16[8,128,128]{2,1,0:T(8,128)(2,1)S(1)}, u32[]{:S(2)}, u32[]{:S(2)}) collective-permute-start(bf16[8,128,128]{2,1,0:T(8,128)(2,1)S(1)} %get-tuple-element.91), channel_id=1, source_target_pairs={{0,28},{4,0},{8,4},{12,8},{16,12},{20,16},{24,20},{28,24},{32,60},... | collective-permute-start | bytes 786440 | tf_op jit(solution)/shard_map/ppermute | solution.py:30
  94.7 10.9 %collective-permute-start.35 = (bf16[8,128,128]{2,1,0:T(8,128)(2,1)S(1)}, bf16[8,128,128]{2,1,0:T(8,128)(2,1)S(1)}, u32[]{:S(2)}, u32[]{:S(2)}) collective-permute-start(bf16[8,128,128]{2,1,0:T(8,128)(2,1)S(1)} %get-tuple-element.92), channel_id=1, source_target_pairs={{0,4},{4,8},{8,12},{12,16},{16,20},{20,24},{24,28},{28,0},{32,36},... | collective-permute-start | bytes 786440 | tf_op jit(solution)/shard_map/ppermute | solution.py:30
  100.1 11.8 %collective-permute-start.26 = (bf16[9,128,128]{2,1,0:T(8,128)(2,1)S(1)}, bf16[9,128,128]{2,1,0:T(8,128)(2,1)S(1)}, u32[]{:S(2)}, u32[]{:S(2)}) collective-permute-start(bf16[9,128,128]{2,1,0:T(8,128)(2,1)S(1)} %get-tuple-element.73), channel_id=1, source_target_pairs={{0,4},{4,8},{8,12},{12,16},{16,20},{20,24},{24,28},{28,0},{32,36},... | collective-permute-start | bytes 884744 | tf_op jit(solution)/shard_map/ppermute | solution.py:30
  100.2 11.7 %collective-permute-start.27 = (bf16[9,128,128]{2,1,0:T(8,128)(2,1)S(1)}, bf16[9,128,128]{2,1,0:T(8,128)(2,1)S(1)}, u32[]{:S(2)}, u32[]{:S(2)}) collective-permute-start(bf16[9,128,128]{2,1,0:T(8,128)(2,1)S(1)} %get-tuple-element.74), channel_id=1, source_target_pairs={{0,28},{4,0},{8,4},{12,8},{16,12},{20,16},{24,20},{28,24},{32,60},... | collective-permute-start | bytes 884744 | tf_op jit(solution)/shard_map/ppermute | solution.py:30
  105.7 9.1 %collective-permute-start.36 = (bf16[8,128,128]{2,1,0:T(8,128)(2,1)S(1)}, bf16[8,128,128]{2,1,0:T(8,128)(2,1)S(1)}, u32[]{:S(2)}, u32[]{:S(2)}) collective-permute-start(bf16[8,128,128]{2,1,0:T(8,128)(2,1)S(1)} %get-tuple-element.96), channel_id=1, source_target_pairs={{0,28},{4,0},{8,4},{12,8},{16,12},{20,16},{24,20},{28,24},{32,60},... | collective-permute-start | bytes 786440 | tf_op jit(solution)/shard_map/ppermute | solution.py:30
  106.6 10.9 %collective-permute-start.37 = (bf16[8,128,128]{2,1,0:T(8,128)(2,1)S(1)}, bf16[8,128,128]{2,1,0:T(8,128)(2,1)S(1)}, u32[]{:S(2)}, u32[]{:S(2)}) collective-permute-start(bf16[8,128,128]{2,1,0:T(8,128)(2,1)S(1)} %get-tuple-element.97), channel_id=1, source_target_pairs={{0,4},{4,8},{8,12},{12,16},{16,20},{20,24},{24,28},{28,0},{32,36},... | collective-permute-start | bytes 786440 | tf_op jit(solution)/shard_map/ppermute | solution.py:30
  112.1 11.8 %collective-permute-start.28 = (bf16[9,128,128]{2,1,0:T(8,128)(2,1)S(1)}, bf16[9,128,128]{2,1,0:T(8,128)(2,1)S(1)}, u32[]{:S(2)}, u32[]{:S(2)}) collective-permute-start(bf16[9,128,128]{2,1,0:T(8,128)(2,1)S(1)} %get-tuple-element.78), channel_id=1, source_target_pairs={{0,4},{4,8},{8,12},{12,16},{16,20},{20,24},{24,28},{28,0},{32,36},... | collective-permute-start | bytes 884744 | tf_op jit(solution)/shard_map/ppermute | solution.py:30
  112.2 11.7 %collective-permute-start.29 = (bf16[9,128,128]{2,1,0:T(8,128)(2,1)S(1)}, bf16[9,128,128]{2,1,0:T(8,128)(2,1)S(1)}, u32[]{:S(2)}, u32[]{:S(2)}) collective-permute-start(bf16[9,128,128]{2,1,0:T(8,128)(2,1)S(1)} %get-tuple-element.79), channel_id=1, source_target_pairs={{0,28},{4,0},{8,4},{12,8},{16,12},{20,16},{24,20},{28,24},{32,60},... | collective-permute-start | bytes 884744 | tf_op jit(solution)/shard_map/ppermute | solution.py:30
  117.6 8.3 %collective-permute-start.38 = (bf16[8,128,128]{2,1,0:T(8,128)(2,1)S(1)}, bf16[8,128,128]{2,1,0:T(8,128)(2,1)S(1)}, u32[]{:S(2)}, u32[]{:S(2)}) collective-permute-start(bf16[8,128,128]{2,1,0:T(8,128)(2,1)S(1)} %add_convert_fusion.2), channel_id=1, source_target_pairs={{0,28},{4,0},{8,4},{12,8},{16,12},{20,16},{24,20},{28,24},{32,60},... | collective-permute-start | bytes 786440 | tf_op jit(solution)/shard_map/ppermute | solution.py:30
  123.9 7.3 %collective-permute-start.30 = (bf16[9,128,128]{2,1,0:T(8,128)(2,1)S(1)}, bf16[9,128,128]{2,1,0:T(8,128)(2,1)S(1)}, u32[]{:S(2)}, u32[]{:S(2)}) collective-permute-start(bf16[9,128,128]{2,1,0:T(8,128)(2,1)S(1)} %add_convert_fusion), channel_id=1, source_target_pairs={{0,4},{4,8},{8,12},{12,16},{16,20},{20,24},{24,28},{28,0},{32,36},... | collective-permute-start | bytes 884744 | tf_op jit(solution)/shard_map/ppermute | solution.py:30
  131.4 10.1 %collective-permute-start.31 = (bf16[5,128,128]{2,1,0:T(8,128)(2,1)S(1)}, bf16[5,128,128]{2,1,0:T(8,128)(2,1)S(1)}, u32[]{:S(2)}, u32[]{:S(2)}) collective-permute-start(bf16[5,128,128]{2,1,0:T(8,128)(2,1)S(1)} %get-tuple-element.105), channel_id=1, source_target_pairs={{0,32},{4,36},{8,40},{12,44},{16,48},{20,52},{24,56},{28,60},{32,6... | collective-permute-start | bytes 491528 | tf_op jit(solution)/shard_map/ppermute | solution.py:30
  133.2 12.4 %collective-permute-start.39 = (bf16[5,128,128]{2,1,0:T(8,128)(2,1)S(1)}, bf16[5,128,128]{2,1,0:T(8,128)(2,1)S(1)}, u32[]{:S(2)}, u32[]{:S(2)}) collective-permute-start(bf16[5,128,128]{2,1,0:T(8,128)(2,1)S(1)} %get-tuple-element.106), channel_id=1, source_target_pairs={{0,64},{4,68},{8,72},{12,76},{16,80},{20,84},{24,88},{28,92},{32,9... | collective-permute-start | bytes 491528 | tf_op jit(solution)/shard_map/ppermute | solution.py:30
  139.7 6.2 %collective-permute-start.40 = (bf16[5,128,128]{2,1,0:T(8,128)(2,1)S(1)}, bf16[5,128,128]{2,1,0:T(8,128)(2,1)S(1)}, u32[]{:S(2)}, u32[]{:S(2)}) collective-permute-start(bf16[5,128,128]{2,1,0:T(8,128)(2,1)S(1)} %get-tuple-element.107), channel_id=1, source_target_pairs={{0,96},{4,100},{8,104},{12,108},{16,112},{20,116},{24,120},{28,124... | collective-permute-start | bytes 491528 | tf_op jit(solution)/shard_map/ppermute | solution.py:30
  146.0 3.6 %collective-permute-start.41 = (bf16[3,128,128]{2,1,0:T(8,128)(2,1)S(1)}, bf16[3,128,128]{2,1,0:T(8,128)(2,1)S(1)}, u32[]{:S(2)}, u32[]{:S(2)}) collective-permute-start(bf16[3,128,128]{2,1,0:T(8,128)(2,1)S(1)} %pad_maximum_fusion.5), channel_id=1, source_target_pairs={{0,128},{4,132},{8,136},{12,140},{16,144},{20,148},{24,152},{28,15... | collective-permute-start | bytes 294920 | tf_op jit(solution)/shard_map/ppermute | solution.py:30
  149.6 4.6 %collective-permute-start.42 = (f32[64,256]{1,0:T(8,128)S(1)}, f32[64,256]{1,0:T(8,128)S(1)}, u32[]{:S(2)}, u32[]{:S(2)}) collective-permute-start(f32[64,256]{1,0:T(8,128)S(1)} %pad_maximum_fusion.6), channel_id=1, source_target_pairs={{0,1},{1,0},{2,3},{3,2},{4,5},{5,4},{6,7},{7,6},{8,9},{9,8},{10,11... | collective-permute-start | bytes 196616 | tf_op jit(solution)/shard_map/ppermute | solution.py:34
  (6 other events, 38.7 us)

commit v4 on v3

--- a/solution.py
+++ b/solution.py
@@ -363,33 +363,28 @@
     return spans
 
 
-def add_pair(a, b, c, d):
+def add_rounded(a, b):
     vmem = pl.BlockSpec(memory_space=pltpu.VMEM)
 
-    def kernel(a_ref, b_ref, c_ref, d_ref, ab_ref, cd_ref):
-        for x, y, out in ((a_ref, b_ref, ab_ref), (c_ref, d_ref, cd_ref)):
-            out[...] = (x[...].astype(F32) + y[...].astype(F32)).astype(BF16)
+    def kernel(a_ref, b_ref, out):
+        out[...] = (a_ref[...].astype(F32) + b_ref[...].astype(F32)).astype(BF16)
 
     return pl.pallas_call(
         kernel,
-        out_shape=[jax.ShapeDtypeStruct(a.shape, BF16), jax.ShapeDtypeStruct(c.shape, BF16)],
-        in_specs=[vmem] * 4,
-        out_specs=[vmem] * 2,
+        out_shape=jax.ShapeDtypeStruct(a.shape, BF16),
+        in_specs=[vmem] * 2,
+        out_specs=vmem,
         compiler_params=pltpu.CompilerParams(vmem_limit_bytes=8 * 2**20),
-        name="add_pair",
-    )(a, b, c, d)
+        name="add_rounded",
+    )(a, b)
 
 
 def ring_sums(long, short, dz):
-    ahead, back = [], []
-    message, reply = long[0], short[0]
-    for i in range(len(short)):
-        if i:
-            message, reply = add_pair(long[i], ahead[-1], short[i], back[-1])
-        message, reply = fence(send(message, dz=dz), send(reply, dz=-dz))
-        ahead.append(message)
-        back.append(reply)
-    ahead.append(send(add(long[-1], ahead[-1]).astype(BF16), dz=dz))
+    ahead, back = [send(long[0], dz=dz)], [send(short[0], dz=-dz)]
+    for i in range(1, len(long)):
+        ahead.append(send(add_rounded(long[i], ahead[-1]), dz=dz))
+        if i < len(short):
+            back.append(send(add_rounded(short[i], back[-1]), dz=-dz))
     return ahead, back
 
 

time: 154 us -> 149 us (0.968)
  waiting for transfers between devices: 61.6 us -> 50.4 us
  starting transfers between devices: 64.7 us -> 75.4 us
  Pallas kernels: 16.3 us -> 11.3 us
    ppermute x36, waiting for transfers between devices: 55.4 us -> 43.4 us  [send(): return lax.ppermute(value, 'section', pairs)]
    ppermute x7, starting transfers between devices: 13.9 us -> 23.5 us  [send_team(): return lax.ppermute(value, 'team', [(t, t ^ mask) for t in range(4)])]
    pallas_call x2, Pallas kernels: 5.84 us -> 3.19 us  [forward_call(): pl.pallas_call(kernel, out_shape=out_shape, in_specs=[smem] * 2 + [vmem]...]
  transfers between devices with their start and end apart: 43 -> 43, of which waited for: 23 -> 24; matrix products, arithmetic and copies ran while one was open for 3% -> 3% of each run, Pallas kernels for 6% -> 4%
where the time goes in v4:
time: 149 us
  starting transfers between devices  75.4 us (51%)
  waiting for transfers between devices  50.4 us (34%)
  Pallas kernels  11.3 us (8%)
  local copies, waits for them, and re-layouts  5.6 us (4%)
  other arithmetic  4.88 us (3%)
  between operations  1.66 us (1%)
    ppermute x36, starting transfers between devices, send(): return lax.ppermute(value, 'section', pairs)  51.9 us
    ppermute x36, waiting for transfers between devices, send(): return lax.ppermute(value, 'section', pairs)  43.4 us
    ppermute x7, starting transfers between devices, send_team(): return lax.ppermute(value, 'team', [(t, t ^ mask) for t in range(4)])  23.5 us
    ppermute x7, waiting for transfers between devices, send_team(): return lax.ppermute(value, 'team', [(t, t ^ mask) for t in range(4)])  7.03 us
    unnamed x23, local copies, waits for them, and re-layouts  4.78 us
    pallas_call x2, Pallas kernels, forward_call(): pl.pallas_call(kernel, out_shape=out_shape, in_specs=[smem] * 2 + [vmem]...  3.19 us
  transfers between devices with their start and end apart: 43, of which 24 were waited for; matrix products, arithmetic and copies ran while one was open for 3% of the time, Pallas kernels for 4%

profile of v4, /device:TPU:1, one launch (start us, length us, event | category | flops | bytes accessed | tf_op | source)
XLA Modules:
  0.0 149.2 jit_solution(15355329983843235261)
XLA Ops:
  0.6 2.1 %collective-permute-start = (bf16[2,128,128]{2,1,0:T(8,128)(2,1)}, bf16[2,128,128]{2,1,0:T(8,128)(2,1)S(1)}, u32[]{:S(2)}, u32[]{:S(2)}) collective-permute-start(bf16[2,128,128]{2,1,0:T(8,128)(2,1)} %bitcast.20), channel_id=1, source_target_pairs={{0,128},{4,132},{8,136},{12,140},{16,144},{20,148},{24,152},{28,15... | collective-permute-start | bytes 196616 | tf_op jit(solution)/shard_map/ppermute | solution.py:30
  2.8 1.3 collective-permute-start.1
  5.4 1.3 fusion.10.refs_0_
  7.6 2.7 %collective-permute-start.6 = (bf16[4,128,128]{2,1,0:T(8,128)(2,1)S(1)}, bf16[4,128,128]{2,1,0:T(8,128)(2,1)S(1)}, u32[]{:S(2)}, u32[]{:S(2)}) collective-permute-start(bf16[4,128,128]{2,1,0:T(8,128)(2,1)S(1)} %pad_maximum_fusion.4), channel_id=1, source_target_pairs={{0,64},{4,68},{8,72},{12,76},{16,80},{20,84},{24,88},{28,92},{32,9... | collective-permute-start | bytes 393224 | tf_op jit(solution)/shard_map/ppermute | solution.py:30
  10.7 2.3 %collective-permute-start.2 = (bf16[4,128,128]{2,1,0:T(8,128)(2,1)S(1)}, bf16[4,128,128]{2,1,0:T(8,128)(2,1)S(1)}, u32[]{:S(2)}, u32[]{:S(2)}) collective-permute-start(bf16[4,128,128]{2,1,0:T(8,128)(2,1)S(1)} %pad_maximum_fusion.4), channel_id=1, source_target_pairs={{0,96},{4,100},{8,104},{12,108},{16,112},{20,116},{24,120},{28,124... | collective-permute-start | bytes 393224 | tf_op jit(solution)/shard_map/ppermute | solution.py:30
  13.0 4.7 %collective-permute-done.7 = bf16[4,128,128]{2,1,0:T(8,128)(2,1)S(1)} collective-permute-done((bf16[4,128,128]{2,1,0:T(8,128)(2,1)S(1)}, bf16[4,128,128]{2,1,0:T(8,128)(2,1)S(1)}, u32[]{:S(2)}, u32[]{:S(2)}) %collective-permute-start.7) | collective-permute-done | bytes 131104 | tf_op jit(solution)/shard_map/ppermute | solution.py:30
  19.5 4.0 %collective-permute-start.3 = (bf16[8,128,128]{2,1,0:T(8,128)(2,1)S(1)}, bf16[8,128,128]{2,1,0:T(8,128)(2,1)S(1)}, u32[]{:S(2)}, u32[]{:S(2)}) collective-permute-start(bf16[8,128,128]{2,1,0:T(8,128)(2,1)S(1)} %pad_maximum_fusion.refs_3_), channel_id=1, source_target_pairs={{0,28},{4,0},{8,4},{12,8},{16,12},{20,16},{24,20},{28,24},{32,60},... | collective-permute-start | bytes 786440 | tf_op jit(solution)/shard_map/ppermute | solution.py:30
  23.5 2.5 %sort_slots.1.refs_0_ = s32[562]{0:T(1024)} custom-call(s32[256]{0:T(256)} %fusion.10.refs_0_), custom_call_target="tpu_custom_call" | custom-call | flops 4000000000 | bytes 4096 | tf_op jit(solution)/shard_map/sort_slots/pallas_call | solution.py:99
  26.0 1.5 %collective-permute-start.8 = (bf16[8,128,128]{2,1,0:T(8,128)(2,1)S(1)}, bf16[8,128,128]{2,1,0:T(8,128)(2,1)S(1)}, u32[]{:S(2)}, u32[]{:S(2)}) collective-permute-start(bf16[8,128,128]{2,1,0:T(8,128)(2,1)S(1)} %constant_dynamic-update-slice_fusion.refs_4_), channel_id=1, source_target_pairs={{0,28},{4,0},{8,4},{12,8},{16,12},{20,16},{24,20},{28,24},{32,60},... | collective-permute-start | bytes 786440 | tf_op jit(solution)/shard_map/ppermute | solution.py:30
  28.2 3.3 %collective-permute-start.4 = (bf16[8,128,128]{2,1,0:T(8,128)(2,1)S(1)}, bf16[8,128,128]{2,1,0:T(8,128)(2,1)S(1)}, u32[]{:S(2)}, u32[]{:S(2)}) collective-permute-start(bf16[8,128,128]{2,1,0:T(8,128)(2,1)S(1)} %collective-permute-done.3.refs_5_), channel_id=1, source_target_pairs={{0,28},{4,0},{8,4},{12,8},{16,12},{20,16},{24,20},{28,24},{32,60},... | collective-permute-start | bytes 786440 | tf_op jit(solution)/shard_map/ppermute | solution.py:30
  31.5 2.2 %collective-permute-done.8.refs_6_ = bf16[8,128,128]{2,1,0:T(8,128)(2,1)S(1)} collective-permute-done((bf16[8,128,128]{2,1,0:T(8,128)(2,1)S(1)}, bf16[8,128,128]{2,1,0:T(8,128)(2,1)S(1)}, u32[]{:S(2)}, u32[]{:S(2)}) %collective-permute-start.8) | collective-permute-done | bytes 262176 | tf_op jit(solution)/shard_map/ppermute | solution.py:30
  33.7 3.4 %collective-permute-start.9 = (bf16[8,128,128]{2,1,0:T(8,128)(2,1)S(1)}, bf16[8,128,128]{2,1,0:T(8,128)(2,1)S(1)}, u32[]{:S(2)}, u32[]{:S(2)}) collective-permute-start(bf16[8,128,128]{2,1,0:T(8,128)(2,1)S(1)} %collective-permute-done.8.refs_6_), channel_id=1, source_target_pairs={{0,28},{4,0},{8,4},{12,8},{16,12},{20,16},{24,20},{28,24},{32,60},... | collective-permute-start | bytes 786440 | tf_op jit(solution)/shard_map/ppermute | solution.py:30
  37.1 3.2 %collective-permute-done.13.refs_10_ = bf16[8,128,128]{2,1,0:T(8,128)(2,1)S(1)} collective-permute-done((bf16[8,128,128]{2,1,0:T(8,128)(2,1)S(1)}, bf16[8,128,128]{2,1,0:T(8,128)(2,1)S(1)}, u32[]{:S(2)}, u32[]{:S(2)}) %collective-permute-start.13) | collective-permute-done | bytes 262176 | tf_op jit(solution)/shard_map/ppermute | solution.py:30
  40.3 2.7 %collective-permute-start.5 = (bf16[8,128,128]{2,1,0:T(8,128)(2,1)S(1)}, bf16[8,128,128]{2,1,0:T(8,128)(2,1)S(1)}, u32[]{:S(2)}, u32[]{:S(2)}) collective-permute-start(bf16[8,128,128]{2,1,0:T(8,128)(2,1)S(1)} %collective-permute-done.4.refs_7_), channel_id=1, source_target_pairs={{0,28},{4,0},{8,4},{12,8},{16,12},{20,16},{24,20},{28,24},{32,60},... | collective-permute-start | bytes 786440 | tf_op jit(solution)/shard_map/ppermute | solution.py:30
  43.0 2.0 %collective-permute-start.19 = (bf16[256,256]{1,0:T(8,128)(2,1)S(1)}, bf16[256,256]{1,0:T(8,128)(2,1)S(1)}, u32[]{:S(2)}, u32[]{:S(2)}) collective-permute-start(bf16[256,256]{1,0:T(8,128)(2,1)S(1)} %copy-done.1), channel_id=1, source_target_pairs={{0,2},{1,3},{2,0},{3,1},{4,6},{5,7},{6,4},{7,5},{8,10},{9,11},{10,... | collective-permute-start | bytes 393224 | tf_op jit(solution)/shard_map/ppermute | solution.py:34
  45.0 3.3 %collective-permute-start.10 = (bf16[8,128,128]{2,1,0:T(8,128)(2,1)S(1)}, bf16[8,128,128]{2,1,0:T(8,128)(2,1)S(1)}, u32[]{:S(2)}, u32[]{:S(2)}) collective-permute-start(bf16[8,128,128]{2,1,0:T(8,128)(2,1)S(1)} %collective-permute-done.9.refs_8_), channel_id=1, source_target_pairs={{0,28},{4,0},{8,4},{12,8},{16,12},{20,16},{24,20},{28,24},{32,60},... | collective-permute-start | bytes 786440 | tf_op jit(solution)/shard_map/ppermute | solution.py:30
  48.4 2.9 %collective-permute-done.14.refs_8_ = bf16[8,128,128]{2,1,0:T(8,128)(2,1)S(1)} collective-permute-done((bf16[8,128,128]{2,1,0:T(8,128)(2,1)S(1)}, bf16[8,128,128]{2,1,0:T(8,128)(2,1)S(1)}, u32[]{:S(2)}, u32[]{:S(2)}) %collective-permute-start.14) | collective-permute-done | bytes 262176 | tf_op jit(solution)/shard_map/ppermute | solution.py:30
  51.3 2.7 %collective-permute-start.11 = (bf16[8,128,128]{2,1,0:T(8,128)(2,1)S(1)}, bf16[8,128,128]{2,1,0:T(8,128)(2,1)}, u32[]{:S(2)}, u32[]{:S(2)}) collective-permute-start(bf16[8,128,128]{2,1,0:T(8,128)(2,1)S(1)} %collective-permute-done.5.refs_3_), channel_id=1, source_target_pairs={{0,28},{4,0},{8,4},{12,8},{16,12},{20,16},{24,20},{28,24},{32,60},... | collective-permute-start | bytes 786440 | tf_op jit(solution)/shard_map/ppermute | solution.py:30
  54.6 2.3 %collective-permute-start.20 = (bf16[256,256]{1,0:T(8,128)(2,1)}, bf16[256,256]{1,0:T(8,128)(2,1)}, u32[]{:S(2)}, u32[]{:S(2)}) collective-permute-start(bf16[256,256]{1,0:T(8,128)(2,1)} %copy-done.2), channel_id=1, source_target_pairs={{0,2},{1,3},{2,0},{3,1},{4,6},{5,7},{6,4},{7,5},{8,10},{9,11},{10,... | collective-permute-start | bytes 393224 | tf_op jit(solution)/shard_map/ppermute | solution.py:34
  56.9 3.4 %copy-done = bf16[1,1,256,128,128]{4,3,2,1,0:T(8,128)(2,1)S(1)} copy-done((bf16[1,1,256,128,128]{4,3,2,1,0:T(8,128)(2,1)S(1)}, bf16[1,1,256,128,128]{4,3,2,1,0:T(8,128)(2,1)}, u32[]{:S(2)}) %copy-start) | copy-done | bytes 8388632
  60.9 1.4 forward_near.1.refs_9_
  62.6 1.8 %forward_far.1 = (bf16[4,128,128]{2,1,0:T(8,128)(2,1)S(1)}, bf16[4,128,128]{2,1,0:T(8,128)(2,1)S(1)}) custom-call(s32[562]{0:T(1024)S(1)} %copy-done.7, s32[1]{0:T(128)} %bitcast.4.refs_1_, bf16[256,128,128]{2,1,0:T(8,128)(2,1)S(1)} %bitcast.15, bf16[8,128,128]{2,1,0:T(8,128)(2,1)S(1)} %collective-permute-done.5.refs_3_, ...), custom_call_target="tpu_custom_call" | custom-call | flops 402653184 | bytes 3145728 | tf_op jit(solution)/shard_map/forward_far/pallas_call | solution.py:174
  64.4 8.5 %collective-permute-start.21 = (bf16[4,128,128]{2,1,0:T(8,128)(2,1)S(1)}, bf16[4,128,128]{2,1,0:T(8,128)(2,1)S(1)}, u32[]{:S(2)}, u32[]{:S(2)}) collective-permute-start(bf16[4,128,128]{2,1,0:T(8,128)(2,1)S(1)} %get-tuple-element.39), channel_id=1, source_target_pairs={{0,1},{1,0},{2,3},{3,2},{4,5},{5,4},{6,7},{7,6},{8,9},{9,8},{10,11... | collective-permute-start | bytes 393224 | tf_op jit(solution)/shard_map/ppermute | solution.py:34
  72.8 1.0 collective-permute-done.21
  73.9 1.4 collective-permute-start.22
  75.3 4.9 %collective-permute-done.22 = bf16[4,128,128]{2,1,0:T(8,128)(2,1)S(1)} collective-permute-done((bf16[4,128,128]{2,1,0:T(8,128)(2,1)S(1)}, bf16[4,128,128]{2,1,0:T(8,128)(2,1)S(1)}, u32[]{:S(2)}, u32[]{:S(2)}) %collective-permute-start.22) | collective-permute-done | bytes 131104 | tf_op jit(solution)/shard_map/ppermute | solution.py:34
  80.2 1.3 collective-permute-start.23
  82.5 3.0 %dense_and_backward_far.1 = (bf16[256,256]{1,0:T(8,128)(2,1)}, bf16[1,128,128]{2,1,0:T(8,128)(2,1)S(1)}, bf16[9,128,128]{2,1,0:T(8,128)(2,1)S(1)}, bf16[9,128,12...) custom-call(s32[562]{0:T(1024)S(1)} %copy-done.7, ...), custom_call_target="tpu_custom_call" | custom-call | flops 402653184 | bytes 4718592 | tf_op jit(solution)/shard_map/dense_and_backward_far/pallas_call | solution.py:270
  85.5 1.5 collective-permute-start.24
  87.0 5.0 %collective-permute-done.35.b_ref = bf16[8,128,128]{2,1,0:T(8,128)(2,1)S(1)} collective-permute-done((bf16[8,128,128]{2,1,0:T(8,128)(2,1)S(1)}, bf16[8,128,128]{2,1,0:T(8,128)(2,1)S(1)}, u32[]{:S(2)}, u32[]{:S(2)}) %collective-permute-start.35) | collective-permute-done | bytes 262176 | tf_op jit(solution)/shard_map/ppermute | solution.py:30
  92.0 1.6 %collective-permute-start.36 = (bf16[8,128,128]{2,1,0:T(8,128)(2,1)S(1)}, bf16[8,128,128]{2,1,0:T(8,128)(2,1)S(1)}, u32[]{:S(2)}, u32[]{:S(2)}) collective-permute-start(bf16[8,128,128]{2,1,0:T(8,128)(2,1)S(1)} %add_rounded.17), channel_id=1, source_target_pairs={{0,28},{4,0},{8,4},{12,8},{16,12},{20,16},{24,20},{28,24},{32,60},... | collective-permute-start | bytes 786440 | tf_op jit(solution)/shard_map/ppermute | solution.py:30
  94.0 1.3 collective-permute-start.25
  95.2 2.0 %backward_near.1 = (bf16[8,128,128]{2,1,0:T(8,128)(2,1)S(1)}, bf16[8,128,128]{2,1,0:T(8,128)(2,1)S(1)}, bf16[9,128,128]{2,1,0:T(8,128)(2,1)S(1)}, bf16[8,128,128...) custom-call(s32[562]{0:T(1024)S(1)} %copy-done.7, ...), custom_call_target="tpu_custom_call" | custom-call | flops 671088640 | bytes 7864320 | tf_op jit(solution)/shard_map/backward_near/pallas_call | solution.py:314
  97.2 2.3 %collective-permute-done.32.b_ref = bf16[8,128,128]{2,1,0:T(8,128)(2,1)S(1)} collective-permute-done((bf16[8,128,128]{2,1,0:T(8,128)(2,1)S(1)}, bf16[8,128,128]{2,1,0:T(8,128)(2,1)S(1)}, u32[]{:S(2)}, u32[]{:S(2)}) %collective-permute-start.32) | collective-permute-done | bytes 262176 | tf_op jit(solution)/shard_map/ppermute | solution.py:30
  99.7 2.7 %collective-permute-start.37 = (bf16[8,128,128]{2,1,0:T(8,128)(2,1)S(1)}, bf16[8,128,128]{2,1,0:T(8,128)(2,1)S(1)}, u32[]{:S(2)}, u32[]{:S(2)}) collective-permute-start(bf16[8,128,128]{2,1,0:T(8,128)(2,1)S(1)} %add_rounded.18), channel_id=1, source_target_pairs={{0,28},{4,0},{8,4},{12,8},{16,12},{20,16},{24,20},{28,24},{32,60},... | collective-permute-start | bytes 786440 | tf_op jit(solution)/shard_map/ppermute | solution.py:30
  102.5 1.5 %collective-permute-done.28.b_ref = bf16[9,128,128]{2,1,0:T(8,128)(2,1)S(1)} collective-permute-done((bf16[9,128,128]{2,1,0:T(8,128)(2,1)S(1)}, bf16[9,128,128]{2,1,0:T(8,128)(2,1)S(1)}, u32[]{:S(2)}, u32[]{:S(2)}) %collective-permute-start.28) | collective-permute-done | bytes 294944 | tf_op jit(solution)/shard_map/ppermute | solution.py:30
  104.1 3.1 %collective-permute-start.29 = (bf16[9,128,128]{2,1,0:T(8,128)(2,1)S(1)}, bf16[9,128,128]{2,1,0:T(8,128)(2,1)S(1)}, u32[]{:S(2)}, u32[]{:S(2)}) collective-permute-start(bf16[9,128,128]{2,1,0:T(8,128)(2,1)S(1)} %add_rounded.13), channel_id=1, source_target_pairs={{0,28},{4,0},{8,4},{12,8},{16,12},{20,16},{24,20},{28,24},{32,60},... | collective-permute-start | bytes 884744 | tf_op jit(solution)/shard_map/ppermute | solution.py:30
  107.3 4.1 %collective-permute-done.33.b_ref = bf16[8,128,128]{2,1,0:T(8,128)(2,1)S(1)} collective-permute-done((bf16[8,128,128]{2,1,0:T(8,128)(2,1)S(1)}, bf16[8,128,128]{2,1,0:T(8,128)(2,1)S(1)}, u32[]{:S(2)}, u32[]{:S(2)}) %collective-permute-start.33) | collective-permute-done | bytes 262176 | tf_op jit(solution)/shard_map/ppermute | solution.py:30
  111.7 2.7 %collective-permute-start.38 = (bf16[8,128,128]{2,1,0:T(8,128)(2,1)S(1)}, bf16[8,128,128]{2,1,0:T(8,128)(2,1)S(1)}, u32[]{:S(2)}, u32[]{:S(2)}) collective-permute-start(bf16[8,128,128]{2,1,0:T(8,128)(2,1)S(1)} %add_rounded.19), channel_id=1, source_target_pairs={{0,28},{4,0},{8,4},{12,8},{16,12},{20,16},{24,20},{28,24},{32,60},... | collective-permute-start | bytes 786440 | tf_op jit(solution)/shard_map/ppermute | solution.py:30
  114.4 1.5 %collective-permute-done.29.b_ref = bf16[9,128,128]{2,1,0:T(8,128)(2,1)S(1)} collective-permute-done((bf16[9,128,128]{2,1,0:T(8,128)(2,1)S(1)}, bf16[9,128,128]{2,1,0:T(8,128)(2,1)S(1)}, u32[]{:S(2)}, u32[]{:S(2)}) %collective-permute-start.29) | collective-permute-done | bytes 294944 | tf_op jit(solution)/shard_map/ppermute | solution.py:30
  116.0 3.1 %collective-permute-start.30 = (bf16[9,128,128]{2,1,0:T(8,128)(2,1)S(1)}, bf16[9,128,128]{2,1,0:T(8,128)(2,1)S(1)}, u32[]{:S(2)}, u32[]{:S(2)}) collective-permute-start(bf16[9,128,128]{2,1,0:T(8,128)(2,1)S(1)} %add_rounded.14), channel_id=1, source_target_pairs={{0,28},{4,0},{8,4},{12,8},{16,12},{20,16},{24,20},{28,24},{32,60},... | collective-permute-start | bytes 884744 | tf_op jit(solution)/shard_map/ppermute | solution.py:30
  119.3 1.9 %collective-permute-done.34 = bf16[8,128,128]{2,1,0:T(8,128)(2,1)S(1)} collective-permute-done((bf16[8,128,128]{2,1,0:T(8,128)(2,1)S(1)}, bf16[8,128,128]{2,1,0:T(8,128)(2,1)S(1)}, u32[]{:S(2)}, u32[]{:S(2)}) %collective-permute-start.34) | collective-permute-done | bytes 262176 | tf_op jit(solution)/shard_map/ppermute | solution.py:30
  121.7 6.2 %collective-permute-done.30 = bf16[9,128,128]{2,1,0:T(8,128)(2,1)S(1)} collective-permute-done((bf16[9,128,128]{2,1,0:T(8,128)(2,1)S(1)}, bf16[9,128,128]{2,1,0:T(8,128)(2,1)S(1)}, u32[]{:S(2)}, u32[]{:S(2)}) %collective-permute-start.30) | collective-permute-done | bytes 294944 | tf_op jit(solution)/shard_map/ppermute | solution.py:30
  128.8 3.8 %collective-permute-start.39 = (bf16[5,128,128]{2,1,0:T(8,128)(2,1)S(1)}, bf16[5,128,128]{2,1,0:T(8,128)(2,1)S(1)}, u32[]{:S(2)}, u32[]{:S(2)}) collective-permute-start(bf16[5,128,128]{2,1,0:T(8,128)(2,1)S(1)} %get-tuple-element.66), channel_id=1, source_target_pairs={{0,64},{4,68},{8,72},{12,76},{16,80},{20,84},{24,88},{28,92},{32,9... | collective-permute-start | bytes 491528 | tf_op jit(solution)/shard_map/ppermute | solution.py:30
  132.5 2.0 %collective-permute-start.40 = (bf16[5,128,128]{2,1,0:T(8,128)(2,1)S(1)}, bf16[5,128,128]{2,1,0:T(8,128)(2,1)S(1)}, u32[]{:S(2)}, u32[]{:S(2)}) collective-permute-start(bf16[5,128,128]{2,1,0:T(8,128)(2,1)S(1)} %get-tuple-element.67), channel_id=1, source_target_pairs={{0,96},{4,100},{8,104},{12,108},{16,112},{20,116},{24,120},{28,124... | collective-permute-start | bytes 491528 | tf_op jit(solution)/shard_map/ppermute | solution.py:30
  134.5 2.4 %collective-permute-done.39 = bf16[5,128,128]{2,1,0:T(8,128)(2,1)S(1)} collective-permute-done((bf16[5,128,128]{2,1,0:T(8,128)(2,1)S(1)}, bf16[5,128,128]{2,1,0:T(8,128)(2,1)S(1)}, u32[]{:S(2)}, u32[]{:S(2)}) %collective-permute-start.39) | collective-permute-done | bytes 163872 | tf_op jit(solution)/shard_map/ppermute | solution.py:30
  137.1 3.7 %collective-permute-done.41 = bf16[3,128,128]{2,1,0:T(8,128)(2,1)S(1)} collective-permute-done((bf16[3,128,128]{2,1,0:T(8,128)(2,1)S(1)}, bf16[3,128,128]{2,1,0:T(8,128)(2,1)S(1)}, u32[]{:S(2)}, u32[]{:S(2)}) %collective-permute-start.41) | collective-permute-done | bytes 98336 | tf_op jit(solution)/shard_map/ppermute | solution.py:30
  140.9 6.7 %collective-permute-start.42 = (f32[64,256]{1,0:T(8,128)S(1)}, f32[64,256]{1,0:T(8,128)S(1)}, u32[]{:S(2)}, u32[]{:S(2)}) collective-permute-start(f32[64,256]{1,0:T(8,128)S(1)} %pad_maximum_fusion.6), channel_id=1, source_target_pairs={{0,1},{1,0},{2,3},{3,2},{4,5},{5,4},{6,7},{7,6},{8,9},{9,8},{10,11... | collective-permute-start | bytes 196616 | tf_op jit(solution)/shard_map/ppermute | solution.py:34
  (100 shorter events, 11.6 us)
Async XLA Ops:
  0.6 42.3 %copy-start.1 = (bf16[256,256]{1,0:T(8,128)(2,1)S(1)}, bf16[256,256]{1,0:T(8,128)(2,1)}, u32[]{:S(2)}) copy-start(bf16[256,256]{1,0:T(8,128)(2,1)} %refs_5_.1) | copy-start | bytes 393220
  0.6 6.1 %collective-permute-start = (bf16[2,128,128]{2,1,0:T(8,128)(2,1)}, bf16[2,128,128]{2,1,0:T(8,128)(2,1)S(1)}, u32[]{:S(2)}, u32[]{:S(2)}) collective-permute-start(bf16[2,128,128]{2,1,0:T(8,128)(2,1)} %bitcast.20), channel_id=1, source_target_pairs={{0,128},{4,132},{8,136},{12,140},{16,144},{20,148},{24,152},{28,15... | collective-permute-start | bytes 196616 | tf_op jit(solution)/shard_map/ppermute | solution.py:30
  2.8 3.9 %collective-permute-start.1 = (bf16[256,256]{1,0:T(8,128)(2,1)}, bf16[256,256]{1,0:T(8,128)(2,1)S(1)}, u32[]{:S(2)}, u32[]{:S(2)}) collective-permute-start(bf16[256,256]{1,0:T(8,128)(2,1)} %refs_5_.1), channel_id=1, source_target_pairs={{0,1},{1,0},{2,3},{3,2},{4,5},{5,4},{6,7},{7,6},{8,9},{9,8},{10,11... | collective-permute-start | bytes 393224 | tf_op jit(solution)/shard_map/ppermute | solution.py:34
  7.6 5.4 %collective-permute-start.6 = (bf16[4,128,128]{2,1,0:T(8,128)(2,1)S(1)}, bf16[4,128,128]{2,1,0:T(8,128)(2,1)S(1)}, u32[]{:S(2)}, u32[]{:S(2)}) collective-permute-start(bf16[4,128,128]{2,1,0:T(8,128)(2,1)S(1)} %pad_maximum_fusion.4), channel_id=1, source_target_pairs={{0,64},{4,68},{8,72},{12,76},{16,80},{20,84},{24,88},{28,92},{32,9... | collective-permute-start | bytes 393224 | tf_op jit(solution)/shard_map/ppermute | solution.py:30
  10.3 7.5 %collective-permute-start.7 = (bf16[4,128,128]{2,1,0:T(8,128)(2,1)S(1)}, bf16[4,128,128]{2,1,0:T(8,128)(2,1)S(1)}, u32[]{:S(2)}, u32[]{:S(2)}) collective-permute-start(bf16[4,128,128]{2,1,0:T(8,128)(2,1)S(1)} %pad_maximum_fusion.4), channel_id=1, source_target_pairs={{0,32},{4,36},{8,40},{12,44},{16,48},{20,52},{24,56},{28,60},{32,6... | collective-permute-start | bytes 393224 | tf_op jit(solution)/shard_map/ppermute | solution.py:30
  10.7 7.9 %collective-permute-start.2 = (bf16[4,128,128]{2,1,0:T(8,128)(2,1)S(1)}, bf16[4,128,128]{2,1,0:T(8,128)(2,1)S(1)}, u32[]{:S(2)}, u32[]{:S(2)}) collective-permute-start(bf16[4,128,128]{2,1,0:T(8,128)(2,1)S(1)} %pad_maximum_fusion.4), channel_id=1, source_target_pairs={{0,96},{4,100},{8,104},{12,108},{16,112},{20,116},{24,120},{28,124... | collective-permute-start | bytes 393224 | tf_op jit(solution)/shard_map/ppermute | solution.py:30
  17.8 10.4 %collective-permute-start.12 = (bf16[8,128,128]{2,1,0:T(8,128)(2,1)S(1)}, bf16[8,128,128]{2,1,0:T(8,128)(2,1)S(1)}, u32[]{:S(2)}, u32[]{:S(2)}) collective-permute-start(bf16[8,128,128]{2,1,0:T(8,128)(2,1)S(1)} %constant_dynamic-update-slice_fusion.refs_4_), channel_id=1, source_target_pairs={{0,4},{4,8},{8,12},{12,16},{16,20},{20,24},{24,28},{28,0},{32,36},... | collective-permute-start | bytes 786440 | tf_op jit(solution)/shard_map/ppermute | solution.py:30
  19.5 8.6 %collective-permute-start.3 = (bf16[8,128,128]{2,1,0:T(8,128)(2,1)S(1)}, bf16[8,128,128]{2,1,0:T(8,128)(2,1)S(1)}, u32[]{:S(2)}, u32[]{:S(2)}) collective-permute-start(bf16[8,128,128]{2,1,0:T(8,128)(2,1)S(1)} %pad_maximum_fusion.refs_3_), channel_id=1, source_target_pairs={{0,28},{4,0},{8,4},{12,8},{16,12},{20,16},{24,20},{28,24},{32,60},... | collective-permute-start | bytes 786440 | tf_op jit(solution)/shard_map/ppermute | solution.py:30
  26.0 36.6 %copy-start.7 = (s32[562]{0:T(1024)S(1)}, s32[562]{0:T(1024)}, u32[]{:S(2)}) copy-start(s32[562]{0:T(1024)} %sort_slots.1.refs_0_) | copy-start | bytes 6748
  26.0 7.7 %collective-permute-start.8 = (bf16[8,128,128]{2,1,0:T(8,128)(2,1)S(1)}, bf16[8,128,128]{2,1,0:T(8,128)(2,1)S(1)}, u32[]{:S(2)}, u32[]{:S(2)}) collective-permute-start(bf16[8,128,128]{2,1,0:T(8,128)(2,1)S(1)} %constant_dynamic-update-slice_fusion.refs_4_), channel_id=1, source_target_pairs={{0,28},{4,0},{8,4},{12,8},{16,12},{20,16},{24,20},{28,24},{32,60},... | collective-permute-start | bytes 786440 | tf_op jit(solution)/shard_map/ppermute | solution.py:30
  27.5 9.6 %collective-permute-start.16 = (bf16[8,128,128]{2,1,0:T(8,128)(2,1)S(1)}, bf16[8,128,128]{2,1,0:T(8,128)(2,1)S(1)}, u32[]{:S(2)}, u32[]{:S(2)}) collective-permute-start(bf16[8,128,128]{2,1,0:T(8,128)(2,1)S(1)} %pad_maximum_fusion.refs_3_), channel_id=1, source_target_pairs={{0,4},{4,8},{8,12},{12,16},{16,20},{20,24},{24,28},{28,0},{32,36},... | collective-permute-start | bytes 786440 | tf_op jit(solution)/shard_map/ppermute | solution.py:30
  28.2 12.1 %collective-permute-start.13 = (bf16[8,128,128]{2,1,0:T(8,128)(2,1)S(1)}, bf16[8,128,128]{2,1,0:T(8,128)(2,1)S(1)}, u32[]{:S(2)}, u32[]{:S(2)}) collective-permute-start(bf16[8,128,128]{2,1,0:T(8,128)(2,1)S(1)} %collective-permute-done.12.refs_12_), channel_id=1, source_target_pairs={{0,4},{4,8},{8,12},{12,16},{16,20},{20,24},{24,28},{28,0},{32,36},... | collective-permute-start | bytes 786440 | tf_op jit(solution)/shard_map/ppermute | solution.py:30
  28.2 12.1 %collective-permute-start.4 = (bf16[8,128,128]{2,1,0:T(8,128)(2,1)S(1)}, bf16[8,128,128]{2,1,0:T(8,128)(2,1)S(1)}, u32[]{:S(2)}, u32[]{:S(2)}) collective-permute-start(bf16[8,128,128]{2,1,0:T(8,128)(2,1)S(1)} %collective-permute-done.3.refs_5_), channel_id=1, source_target_pairs={{0,28},{4,0},{8,4},{12,8},{16,12},{20,16},{24,20},{28,24},{32,60},... | collective-permute-start | bytes 786440 | tf_op jit(solution)/shard_map/ppermute | solution.py:30
  33.7 11.3 %collective-permute-start.9 = (bf16[8,128,128]{2,1,0:T(8,128)(2,1)S(1)}, bf16[8,128,128]{2,1,0:T(8,128)(2,1)S(1)}, u32[]{:S(2)}, u32[]{:S(2)}) collective-permute-start(bf16[8,128,128]{2,1,0:T(8,128)(2,1)S(1)} %collective-permute-done.8.refs_6_), channel_id=1, source_target_pairs={{0,28},{4,0},{8,4},{12,8},{16,12},{20,16},{24,20},{28,24},{32,60},... | collective-permute-start | bytes 786440 | tf_op jit(solution)/shard_map/ppermute | solution.py:30
  37.1 11.2 %collective-permute-start.17 = (bf16[8,128,128]{2,1,0:T(8,128)(2,1)S(1)}, bf16[8,128,128]{2,1,0:T(8,128)(2,1)S(1)}, u32[]{:S(2)}, u32[]{:S(2)}) collective-permute-start(bf16[8,128,128]{2,1,0:T(8,128)(2,1)S(1)} %collective-permute-done.16.refs_11_), channel_id=1, source_target_pairs={{0,4},{4,8},{8,12},{12,16},{16,20},{20,24},{24,28},{28,0},{32,36},... | collective-permute-start | bytes 786440 | tf_op jit(solution)/shard_map/ppermute | solution.py:30
  40.3 11.0 %collective-permute-start.14 = (bf16[8,128,128]{2,1,0:T(8,128)(2,1)S(1)}, bf16[8,128,128]{2,1,0:T(8,128)(2,1)S(1)}, u32[]{:S(2)}, u32[]{:S(2)}) collective-permute-start(bf16[8,128,128]{2,1,0:T(8,128)(2,1)S(1)} %collective-permute-done.13.refs_10_), channel_id=1, source_target_pairs={{0,4},{4,8},{8,12},{12,16},{16,20},{20,24},{24,28},{28,0},{32,36},... | collective-permute-start | bytes 786440 | tf_op jit(solution)/shard_map/ppermute | solution.py:30
  40.3 11.0 %collective-permute-start.5 = (bf16[8,128,128]{2,1,0:T(8,128)(2,1)S(1)}, bf16[8,128,128]{2,1,0:T(8,128)(2,1)S(1)}, u32[]{:S(2)}, u32[]{:S(2)}) collective-permute-start(bf16[8,128,128]{2,1,0:T(8,128)(2,1)S(1)} %collective-permute-done.4.refs_7_), channel_id=1, source_target_pairs={{0,28},{4,0},{8,4},{12,8},{16,12},{20,16},{24,20},{28,24},{32,60},... | collective-permute-start | bytes 786440 | tf_op jit(solution)/shard_map/ppermute | solution.py:30
  43.0 11.0 %collective-permute-start.19 = (bf16[256,256]{1,0:T(8,128)(2,1)S(1)}, bf16[256,256]{1,0:T(8,128)(2,1)S(1)}, u32[]{:S(2)}, u32[]{:S(2)}) collective-permute-start(bf16[256,256]{1,0:T(8,128)(2,1)S(1)} %copy-done.1), channel_id=1, source_target_pairs={{0,2},{1,3},{2,0},{3,1},{4,6},{5,7},{6,4},{7,5},{8,10},{9,11},{10,... | collective-permute-start | bytes 393224 | tf_op jit(solution)/shard_map/ppermute | solution.py:34
  45.0 17.4 %collective-permute-start.10 = (bf16[8,128,128]{2,1,0:T(8,128)(2,1)S(1)}, bf16[8,128,128]{2,1,0:T(8,128)(2,1)S(1)}, u32[]{:S(2)}, u32[]{:S(2)}) collective-permute-start(bf16[8,128,128]{2,1,0:T(8,128)(2,1)S(1)} %collective-permute-done.9.refs_8_), channel_id=1, source_target_pairs={{0,28},{4,0},{8,4},{12,8},{16,12},{20,16},{24,20},{28,24},{32,60},... | collective-permute-start | bytes 786440 | tf_op jit(solution)/shard_map/ppermute | solution.py:30
  48.4 14.1 %collective-permute-start.18 = (bf16[8,128,128]{2,1,0:T(8,128)(2,1)S(1)}, bf16[8,128,128]{2,1,0:T(8,128)(2,1)}, u32[]{:S(2)}, u32[]{:S(2)}) collective-permute-start(bf16[8,128,128]{2,1,0:T(8,128)(2,1)S(1)} %collective-permute-done.17.refs_9_), channel_id=1, source_target_pairs={{0,4},{4,8},{8,12},{12,16},{16,20},{20,24},{24,28},{28,0},{32,36},... | collective-permute-start | bytes 786440 | tf_op jit(solution)/shard_map/ppermute | solution.py:30
  51.3 11.3 %collective-permute-start.15 = (bf16[8,128,128]{2,1,0:T(8,128)(2,1)S(1)}, bf16[8,128,128]{2,1,0:T(8,128)(2,1)}, u32[]{:S(2)}, u32[]{:S(2)}) collective-permute-start(bf16[8,128,128]{2,1,0:T(8,128)(2,1)S(1)} %collective-permute-done.14.refs_8_), channel_id=1, source_target_pairs={{0,4},{4,8},{8,12},{12,16},{16,20},{20,24},{24,28},{28,0},{32,36},... | collective-permute-start | bytes 786440 | tf_op jit(solution)/shard_map/ppermute | solution.py:30
  51.3 11.3 %collective-permute-start.11 = (bf16[8,128,128]{2,1,0:T(8,128)(2,1)S(1)}, bf16[8,128,128]{2,1,0:T(8,128)(2,1)}, u32[]{:S(2)}, u32[]{:S(2)}) collective-permute-start(bf16[8,128,128]{2,1,0:T(8,128)(2,1)S(1)} %collective-permute-done.5.refs_3_), channel_id=1, source_target_pairs={{0,28},{4,0},{8,4},{12,8},{16,12},{20,16},{24,20},{28,24},{32,60},... | collective-permute-start | bytes 786440 | tf_op jit(solution)/shard_map/ppermute | solution.py:30
  54.6 7.8 %collective-permute-start.20 = (bf16[256,256]{1,0:T(8,128)(2,1)}, bf16[256,256]{1,0:T(8,128)(2,1)}, u32[]{:S(2)}, u32[]{:S(2)}) collective-permute-start(bf16[256,256]{1,0:T(8,128)(2,1)} %copy-done.2), channel_id=1, source_target_pairs={{0,2},{1,3},{2,0},{3,1},{4,6},{5,7},{6,4},{7,5},{8,10},{9,11},{10,... | collective-permute-start | bytes 393224 | tf_op jit(solution)/shard_map/ppermute | solution.py:34
  62.4 20.1 %copy-start.3 = (bf16[256,256]{1,0:T(8,128)(2,1)S(1)}, bf16[256,256]{1,0:T(8,128)(2,1)}, u32[]{:S(2)}) copy-start(bf16[256,256]{1,0:T(8,128)(2,1)} %copy-done.2) | copy-start | bytes 393220
  62.6 32.6 %slice-start = ((s8[8388608]{0:T(1024)(128)(4,1)}), s8[4194304]{0:T(1024)(128)(4,1)S(1)}, s32[]{:S(2)}) async-start(s8[8388608]{0:T(1024)(128)(4,1)} %bitcast.17), calls=%async_computation | async-start | bytes 8388608
  64.4 9.4 %collective-permute-start.21 = (bf16[4,128,128]{2,1,0:T(8,128)(2,1)S(1)}, bf16[4,128,128]{2,1,0:T(8,128)(2,1)S(1)}, u32[]{:S(2)}, u32[]{:S(2)}) collective-permute-start(bf16[4,128,128]{2,1,0:T(8,128)(2,1)S(1)} %get-tuple-element.39), channel_id=1, source_target_pairs={{0,1},{1,0},{2,3},{3,2},{4,5},{5,4},{6,7},{7,6},{8,9},{9,8},{10,11... | collective-permute-start | bytes 393224 | tf_op jit(solution)/shard_map/ppermute | solution.py:34
  73.9 21.4 %slice-start.1 = ((s8[8388608]{0:T(1024)(128)(4,1)}), s8[4194304]{0:T(1024)(128)(4,1)S(1)}, s32[]{:S(2)}) async-start(s8[8388608]{0:T(1024)(128)(4,1)} %bitcast.17), calls=%async_computation.1 | async-start | bytes 8388608
  73.9 6.3 %collective-permute-start.22 = (bf16[4,128,128]{2,1,0:T(8,128)(2,1)S(1)}, bf16[4,128,128]{2,1,0:T(8,128)(2,1)S(1)}, u32[]{:S(2)}, u32[]{:S(2)}) collective-permute-start(bf16[4,128,128]{2,1,0:T(8,128)(2,1)S(1)} %add_convert_fusion.2), channel_id=1, source_target_pairs={{0,2},{1,3},{2,0},{3,1},{4,6},{5,7},{6,4},{7,5},{8,10},{9,11},{10,... | collective-permute-start | bytes 393224 | tf_op jit(solution)/shard_map/ppermute | solution.py:34
  80.2 2.3 %collective-permute-start.23 = (bf16[4,128,128]{2,1,0:T(8,128)(2,1)S(1)}, bf16[4,128,128]{2,1,0:T(8,128)(2,1)S(1)}, u32[]{:S(2)}, u32[]{:S(2)}) collective-permute-start(bf16[4,128,128]{2,1,0:T(8,128)(2,1)S(1)} %add_convert_fusion.1.refs_3_), channel_id=1, source_target_pairs={{0,1},{1,0},{2,3},{3,2},{4,5},{5,4},{6,7},{7,6},{8,9},{9,8},{10,11... | collective-permute-start | bytes 393224 | tf_op jit(solution)/shard_map/ppermute | solution.py:34
  85.5 6.5 %collective-permute-start.35 = (bf16[8,128,128]{2,1,0:T(8,128)(2,1)S(1)}, bf16[8,128,128]{2,1,0:T(8,128)(2,1)S(1)}, u32[]{:S(2)}, u32[]{:S(2)}) collective-permute-start(bf16[8,128,128]{2,1,0:T(8,128)(2,1)S(1)} %get-tuple-element.60), channel_id=1, source_target_pairs={{0,28},{4,0},{8,4},{12,8},{16,12},{20,16},{24,20},{28,24},{32,60},... | collective-permute-start | bytes 786440 | tf_op jit(solution)/shard_map/ppermute | solution.py:30
  85.5 8.4 %collective-permute-start.24 = (bf16[9,128,128]{2,1,0:T(8,128)(2,1)S(1)}, bf16[9,128,128]{2,1,0:T(8,128)(2,1)S(1)}, u32[]{:S(2)}, u32[]{:S(2)}) collective-permute-start(bf16[9,128,128]{2,1,0:T(8,128)(2,1)S(1)} %get-tuple-element.48), channel_id=1, source_target_pairs={{0,4},{4,8},{8,12},{12,16},{16,20},{20,24},{24,28},{28,0},{32,36},... | collective-permute-start | bytes 884744 | tf_op jit(solution)/shard_map/ppermute | solution.py:30
  86.9 12.6 %collective-permute-start.32 = (bf16[8,128,128]{2,1,0:T(8,128)(2,1)S(1)}, bf16[8,128,128]{2,1,0:T(8,128)(2,1)S(1)}, u32[]{:S(2)}, u32[]{:S(2)}) collective-permute-start(bf16[8,128,128]{2,1,0:T(8,128)(2,1)S(1)} %get-tuple-element.56), channel_id=1, source_target_pairs={{0,4},{4,8},{8,12},{12,16},{16,20},{20,24},{24,28},{28,0},{32,36},... | collective-permute-start | bytes 786440 | tf_op jit(solution)/shard_map/ppermute | solution.py:30
  92.0 7.6 %collective-permute-start.36 = (bf16[8,128,128]{2,1,0:T(8,128)(2,1)S(1)}, bf16[8,128,128]{2,1,0:T(8,128)(2,1)S(1)}, u32[]{:S(2)}, u32[]{:S(2)}) collective-permute-start(bf16[8,128,128]{2,1,0:T(8,128)(2,1)S(1)} %add_rounded.17), channel_id=1, source_target_pairs={{0,28},{4,0},{8,4},{12,8},{16,12},{20,16},{24,20},{28,24},{32,60},... | collective-permute-start | bytes 786440 | tf_op jit(solution)/shard_map/ppermute | solution.py:30
  93.6 10.4 %collective-permute-start.28 = (bf16[9,128,128]{2,1,0:T(8,128)(2,1)S(1)}, bf16[9,128,128]{2,1,0:T(8,128)(2,1)S(1)}, u32[]{:S(2)}, u32[]{:S(2)}) collective-permute-start(bf16[9,128,128]{2,1,0:T(8,128)(2,1)S(1)} %get-tuple-element.51), channel_id=1, source_target_pairs={{0,28},{4,0},{8,4},{12,8},{16,12},{20,16},{24,20},{28,24},{32,60},... | collective-permute-start | bytes 884744 | tf_op jit(solution)/shard_map/ppermute | solution.py:30
  94.0 13.2 %collective-permute-start.25 = (bf16[9,128,128]{2,1,0:T(8,128)(2,1)S(1)}, bf16[9,128,128]{2,1,0:T(8,128)(2,1)S(1)}, u32[]{:S(2)}, u32[]{:S(2)}) collective-permute-start(bf16[9,128,128]{2,1,0:T(8,128)(2,1)S(1)} %add_rounded.10), channel_id=1, source_target_pairs={{0,4},{4,8},{8,12},{12,16},{16,20},{20,24},{24,28},{28,0},{32,36},... | collective-permute-start | bytes 884744 | tf_op jit(solution)/shard_map/ppermute | solution.py:30
  99.6 11.9 %collective-permute-start.33 = (bf16[8,128,128]{2,1,0:T(8,128)(2,1)S(1)}, bf16[8,128,128]{2,1,0:T(8,128)(2,1)S(1)}, u32[]{:S(2)}, u32[]{:S(2)}) collective-permute-start(bf16[8,128,128]{2,1,0:T(8,128)(2,1)S(1)} %add_rounded.15), channel_id=1, source_target_pairs={{0,4},{4,8},{8,12},{12,16},{16,20},{20,24},{24,28},{28,0},{32,36},... | collective-permute-start | bytes 786440 | tf_op jit(solution)/shard_map/ppermute | solution.py:30
  99.7 11.9 %collective-permute-start.37 = (bf16[8,128,128]{2,1,0:T(8,128)(2,1)S(1)}, bf16[8,128,128]{2,1,0:T(8,128)(2,1)S(1)}, u32[]{:S(2)}, u32[]{:S(2)}) collective-permute-start(bf16[8,128,128]{2,1,0:T(8,128)(2,1)S(1)} %add_rounded.18), channel_id=1, source_target_pairs={{0,28},{4,0},{8,4},{12,8},{16,12},{20,16},{24,20},{28,24},{32,60},... | collective-permute-start | bytes 786440 | tf_op jit(solution)/shard_map/ppermute | solution.py:30
  104.1 11.9 %collective-permute-start.29 = (bf16[9,128,128]{2,1,0:T(8,128)(2,1)S(1)}, bf16[9,128,128]{2,1,0:T(8,128)(2,1)S(1)}, u32[]{:S(2)}, u32[]{:S(2)}) collective-permute-start(bf16[9,128,128]{2,1,0:T(8,128)(2,1)S(1)} %add_rounded.13), channel_id=1, source_target_pairs={{0,28},{4,0},{8,4},{12,8},{16,12},{20,16},{24,20},{28,24},{32,60},... | collective-permute-start | bytes 884744 | tf_op jit(solution)/shard_map/ppermute | solution.py:30
  107.2 11.9 %collective-permute-start.26 = (bf16[9,128,128]{2,1,0:T(8,128)(2,1)S(1)}, bf16[9,128,128]{2,1,0:T(8,128)(2,1)S(1)}, u32[]{:S(2)}, u32[]{:S(2)}) collective-permute-start(bf16[9,128,128]{2,1,0:T(8,128)(2,1)S(1)} %add_rounded.11), channel_id=1, source_target_pairs={{0,4},{4,8},{8,12},{12,16},{16,20},{20,24},{24,28},{28,0},{32,36},... | collective-permute-start | bytes 884744 | tf_op jit(solution)/shard_map/ppermute | solution.py:30
  111.5 9.6 %collective-permute-start.34 = (bf16[8,128,128]{2,1,0:T(8,128)(2,1)S(1)}, bf16[8,128,128]{2,1,0:T(8,128)(2,1)S(1)}, u32[]{:S(2)}, u32[]{:S(2)}) collective-permute-start(bf16[8,128,128]{2,1,0:T(8,128)(2,1)S(1)} %add_rounded.16), channel_id=1, source_target_pairs={{0,4},{4,8},{8,12},{12,16},{16,20},{20,24},{24,28},{28,0},{32,36},... | collective-permute-start | bytes 786440 | tf_op jit(solution)/shard_map/ppermute | solution.py:30
  111.7 9.9 %collective-permute-start.38 = (bf16[8,128,128]{2,1,0:T(8,128)(2,1)S(1)}, bf16[8,128,128]{2,1,0:T(8,128)(2,1)S(1)}, u32[]{:S(2)}, u32[]{:S(2)}) collective-permute-start(bf16[8,128,128]{2,1,0:T(8,128)(2,1)S(1)} %add_rounded.19), channel_id=1, source_target_pairs={{0,28},{4,0},{8,4},{12,8},{16,12},{20,16},{24,20},{28,24},{32,60},... | collective-permute-start | bytes 786440 | tf_op jit(solution)/shard_map/ppermute | solution.py:30
  116.0 11.9 %collective-permute-start.30 = (bf16[9,128,128]{2,1,0:T(8,128)(2,1)S(1)}, bf16[9,128,128]{2,1,0:T(8,128)(2,1)S(1)}, u32[]{:S(2)}, u32[]{:S(2)}) collective-permute-start(bf16[9,128,128]{2,1,0:T(8,128)(2,1)S(1)} %add_rounded.14), channel_id=1, source_target_pairs={{0,28},{4,0},{8,4},{12,8},{16,12},{20,16},{24,20},{28,24},{32,60},... | collective-permute-start | bytes 884744 | tf_op jit(solution)/shard_map/ppermute | solution.py:30
  119.2 8.9 %collective-permute-start.27 = (bf16[9,128,128]{2,1,0:T(8,128)(2,1)S(1)}, bf16[9,128,128]{2,1,0:T(8,128)(2,1)S(1)}, u32[]{:S(2)}, u32[]{:S(2)}) collective-permute-start(bf16[9,128,128]{2,1,0:T(8,128)(2,1)S(1)} %add_rounded.12), channel_id=1, source_target_pairs={{0,4},{4,8},{8,12},{12,16},{16,20},{20,24},{24,28},{28,0},{32,36},... | collective-permute-start | bytes 884744 | tf_op jit(solution)/shard_map/ppermute | solution.py:30
  128.3 6.2 %collective-permute-start.31 = (bf16[5,128,128]{2,1,0:T(8,128)(2,1)S(1)}, bf16[5,128,128]{2,1,0:T(8,128)(2,1)S(1)}, u32[]{:S(2)}, u32[]{:S(2)}) collective-permute-start(bf16[5,128,128]{2,1,0:T(8,128)(2,1)S(1)} %get-tuple-element.65), channel_id=1, source_target_pairs={{0,32},{4,36},{8,40},{12,44},{16,48},{20,52},{24,56},{28,60},{32,6... | collective-permute-start | bytes 491528 | tf_op jit(solution)/shard_map/ppermute | solution.py:30
  128.8 8.1 %collective-permute-start.39 = (bf16[5,128,128]{2,1,0:T(8,128)(2,1)S(1)}, bf16[5,128,128]{2,1,0:T(8,128)(2,1)S(1)}, u32[]{:S(2)}, u32[]{:S(2)}) collective-permute-start(bf16[5,128,128]{2,1,0:T(8,128)(2,1)S(1)} %get-tuple-element.66), channel_id=1, source_target_pairs={{0,64},{4,68},{8,72},{12,76},{16,80},{20,84},{24,88},{28,92},{32,9... | collective-permute-start | bytes 491528 | tf_op jit(solution)/shard_map/ppermute | solution.py:30
  132.5 4.4 %collective-permute-start.40 = (bf16[5,128,128]{2,1,0:T(8,128)(2,1)S(1)}, bf16[5,128,128]{2,1,0:T(8,128)(2,1)S(1)}, u32[]{:S(2)}, u32[]{:S(2)}) collective-permute-start(bf16[5,128,128]{2,1,0:T(8,128)(2,1)S(1)} %get-tuple-element.67), channel_id=1, source_target_pairs={{0,96},{4,100},{8,104},{12,108},{16,112},{20,116},{24,120},{28,124... | collective-permute-start | bytes 491528 | tf_op jit(solution)/shard_map/ppermute | solution.py:30
  137.0 3.8 %collective-permute-start.41 = (bf16[3,128,128]{2,1,0:T(8,128)(2,1)S(1)}, bf16[3,128,128]{2,1,0:T(8,128)(2,1)S(1)}, u32[]{:S(2)}, u32[]{:S(2)}) collective-permute-start(bf16[3,128,128]{2,1,0:T(8,128)(2,1)S(1)} %pad_maximum_fusion.5), channel_id=1, source_target_pairs={{0,128},{4,132},{8,136},{12,140},{16,144},{20,148},{24,152},{28,15... | collective-permute-start | bytes 294920 | tf_op jit(solution)/shard_map/ppermute | solution.py:30
  140.9 7.6 %collective-permute-start.42 = (f32[64,256]{1,0:T(8,128)S(1)}, f32[64,256]{1,0:T(8,128)S(1)}, u32[]{:S(2)}, u32[]{:S(2)}) collective-permute-start(f32[64,256]{1,0:T(8,128)S(1)} %pad_maximum_fusion.6), channel_id=1, source_target_pairs={{0,1},{1,0},{2,3},{3,2},{4,5},{5,4},{6,7},{7,6},{8,9},{9,8},{10,11... | collective-permute-start | bytes 196616 | tf_op jit(solution)/shard_map/ppermute | solution.py:34
  (6 other events, 51.2 us)
